TPU v7x, 32 devices: a whole 2x2x4 slice. The times are simulated.
32 devices in a mesh: tp: 2 (over y), lat: 16 (over z, x, core).
Axes of the slice: x: 2, y: 2, z: 4, core: 2. Of those that a mesh axis runs over, the one named last changes fastest.
Arguments:
- queries: bfloat16 [256, 2048], P('lat', 'tp'), may hold values from -6 to 6
- key_cache: bfloat16 [256, 256, 1024], P('lat', None, 'tp'), may hold values from -6 to 6
- value_cache: bfloat16 [256, 256, 1024], P('lat', None, 'tp'), may hold values from -6 to 6
- new_key: bfloat16 [256, 1024], P('lat', 'tp'), may hold values from -6 to 6
- new_value: bfloat16 [256, 1024], P('lat', 'tp'), may hold values from -6 to 6
- lengths: int32 [256], P('lat'), may hold values from 1 to 256, as said below
- out_proj: bfloat16 [2048, 4608], P('tp', 'lat'), may hold values from -0.125 to 0.125
- residual: bfloat16 [256, 4608], P(None, 'lat'), may hold values from -3 to 3
- enc_weight: bfloat16 [4608, 8192], P(None, ('tp', 'lat')), may hold values from -0.1875 to 0.1875
- enc_bias: float32 [8192], P(('tp', 'lat')), may hold values from -1.5 to 1.5
- threshold_code: int32 [8192], P(('tp', 'lat')), may hold values from 0 to 15
- probe_weight: bfloat16 [8192, 256], P(('tp', 'lat')), may hold values from -0.0625 to 0.0625
- probe_bias: float32 [256], replicated, may hold values from -2.5 to 2.5
- head_weight: float32 [256, 16], replicated, may hold values from -0.375 to 0.375
- head_bias: float32 [16], replicated, may hold values from -2.5 to 2.5
Outputs:
- probe_scores: float32 [256, 256], P(('tp', 'lat'))
- harm_logits: float32 [256, 16], P(('tp', 'lat'))
Inputs may be any that keep to these rules, and one draw needn't show every extreme that they name: `lengths`: some row has all 256 positions live.
All inputs are finite; a program needn't handle non-finite values.
Results may differ from a plain program's by a relative error of at most 0.0075.
Values may be sent and summed in bfloat16 or wider, within the bound.
No kernel may reach another device: no remote copies, remote signals or barrier semaphores. Data moves between devices by JAX's collectives and lax.ppermute only.
A program may use at most 64 MiB of HBM per device.

v0:
```python
import jax
import jax.numpy as jnp
from jax import lax
from jax.sharding import PartitionSpec as P

HEAD = 128


SOFT_CAP = 50.0
QUERY_SCALE = 1.0 / 12.0
RAMP_WIDTH = 0.25


def attend(queries, key_cache, value_cache, new_key, new_value, lengths):
    row_count, positions, kv_width = key_cache.shape
    kv_heads = kv_width // HEAD
    group_size = queries.shape[1] // kv_width
    grouped = queries.reshape(row_count, kv_heads, group_size, HEAD)
    key_rows = key_cache.reshape(row_count, positions, kv_heads, HEAD)
    values = value_cache.reshape(row_count, positions, kv_heads, HEAD)
    fresh_key = new_key.reshape(row_count, kv_heads, HEAD)
    fresh_value = new_value.reshape(row_count, kv_heads, 1, HEAD).astype(jnp.float32)
    cached = jnp.einsum("rkgd,rlkd->rkgl", grouped, key_rows, preferred_element_type=jnp.float32)
    own_score = jnp.einsum("rkgd,rkd->rkg", grouped, fresh_key, preferred_element_type=jnp.float32)
    cached = SOFT_CAP * jnp.tanh(cached * (QUERY_SCALE / SOFT_CAP))
    own_score = SOFT_CAP * jnp.tanh(own_score * (QUERY_SCALE / SOFT_CAP))
    live_mask = jnp.arange(positions, dtype=jnp.int32)[None, :] < lengths[:, None]
    cached_exp = jnp.where(live_mask[:, None, None, :], jnp.exp(cached), 0.0)
    own_exp = jnp.exp(own_score)
    denominator = jnp.sum(cached_exp, axis=-1) + own_exp
    cached_weight = (cached_exp / denominator[..., None]).astype(jnp.bfloat16)
    own_weight = (own_exp / denominator).astype(jnp.bfloat16)
    mixture = jnp.einsum(
        "rkgl,rlkd->rkgd", cached_weight, values, preferred_element_type=jnp.float32
    )
    mixture = mixture + own_weight.astype(jnp.float32)[..., None] * fresh_value
    return mixture.reshape(row_count, kv_heads * group_size * HEAD).astype(jnp.bfloat16)


def body(
    queries,
    key_cache,
    value_cache,
    new_key,
    new_value,
    lengths,
    out_proj,
    residual,
    enc_weight,
    enc_bias,
    threshold_code,
    probe_weight,
    probe_bias,
    head_weight,
    head_bias,
):
    attended = attend(queries, key_cache, value_cache, new_key, new_value, lengths)
    partial_heads = jnp.dot(
        lax.all_gather(attended, "lat", axis=0, tiled=True),
        out_proj,
        preferred_element_type=jnp.float32,
    )
    projected = lax.psum(partial_heads, "tp")
    stream = (residual.astype(jnp.float32) + projected).astype(jnp.bfloat16)
    pre_act = jnp.dot(
        lax.all_gather(stream, "lat", axis=1, tiled=True),
        enc_weight,
        preferred_element_type=jnp.float32,
    )
    pre_act = pre_act + enc_bias
    threshold = threshold_code.astype(jnp.float32) / 16.0
    ramped = jnp.clip((pre_act - threshold) / RAMP_WIDTH, 0.0, 1.0)
    activations = (pre_act * ramped).astype(jnp.bfloat16)
    halfway = lax.psum_scatter(
        jnp.dot(activations, probe_weight, preferred_element_type=jnp.float32),
        "tp",
        scatter_dimension=0,
        tiled=True,
    )
    summed = lax.psum_scatter(halfway, "lat", scatter_dimension=0, tiled=True)
    probe_scores = summed + probe_bias
    harm_logits = (
        jnp.dot(
            jax.nn.silu(probe_scores),
            head_weight,
            precision=lax.Precision.HIGHEST,
            preferred_element_type=jnp.float32,
        )
        + head_bias
    )
    return (probe_scores, harm_logits)


def solution(mesh):
    in_specs = (
        P("lat", "tp"),
        P("lat", None, "tp"),
        P("lat", None, "tp"),
        P("lat", "tp"),
        P("lat", "tp"),
        P("lat"),
        P("tp", "lat"),
        P(None, "lat"),
        P(None, ("tp", "lat")),
        P(("tp", "lat")),
        P(("tp", "lat")),
        P(("tp", "lat"), None),
        P(),
        P(),
        P(),
    )
    out_specs = (P(("tp", "lat"), None), P(("tp", "lat"), None))
    return jax.shard_map(body, mesh=mesh, in_specs=in_specs, out_specs=out_specs, check_vma=False)
```

profile of v0, /device:TPU:0, one launch (start us, length us, event | category | flops | bytes accessed | tf_op | source)
XLA Modules:
  0.0 189.7 jit_solution(11478953593502921524)
XLA Ops:
  7.2 0.0 copy-start
  7.2 0.0 all-reduce.2.cloned.1.call-start
  7.2 0.9 iota_compare_fusion
  8.1 0.8 reshape.51
  8.9 0.7 reshape.59
  9.6 0.2 fusion.50
  9.8 0.1 copy.29
  9.9 0.7 reshape.55
  10.7 3.5 %fusion.49 = (f32[16,4,2]{2,1,0:T(4,128)S(1)}, f32[16,4,2,256]{3,2,1,0:T(2,128)S(1)}) fusion(bf16[16,4,2,128]{3,2,1,0:T(2,128)(2,1)S(1)} %reshape.51, pred[16,256]{1,0:T(8,128)(4,1)S(1)} %iota_compare_fusion, bf16[16,256,512]{2,1,0:T(8,128)(2,1)} %param.16), kind=kOutput, calls=%fused_computation.45 | convolution fusion | flops 8519552 | bytes 4362752 | tf_op jit(solution)/shard_map/rkgd,rlkd->rkgl/dot_general | solution.py:23
  14.2 0.0 copy-start.1
  14.2 0.1 copy.24
  14.3 0.1 copy.27
  14.4 0.1 copy.25
  14.5 0.0 copy-start.2
  14.5 0.0 copy-start.5
  14.5 0.0 copy-start.6
  14.5 0.0 copy-start.8
  14.6 3.0 %fusion.21 = bf16[16,4,2,128]{3,2,1,0:T(2,128)(2,1)S(1)} fusion(f32[16,4,2,256]{3,2,1,0:T(2,128)S(1)} %get-tuple-element.5, f32[16,4,2]{2,1,0:T(4,128)S(1)} %copy.25, f32[16,4,128]{2,1,0:T(4,128)S(1)} %reshape.55, f32[16,4,2]{2,1,0:T(4,128)S(1)} %copy.27, bf16[16,256,512]{2,1,0:T(8,128)(2,1)} %param.17), kind=kOutput, calls=%fused_computation.12 | convolution fusion | flops 8503296 | bytes 4391936 | tf_op jit(solution)/shard_map/rkgl,rlkd->rkgd/dot_general | solution.py:33
  17.6 24.6 %all_gather.6 = bf16[256,1024]{1,0:T(8,128)(2,1)S(1)} all-gather(bf16[16,1024]{1,0:T(8,128)(2,1)S(1)} %convert_element_type.45), channel_id=1, replica_groups=mesh['tp'=2,'lat'=16] {'lat'}, dimensions={0}, use_global_device_ids=true | all-gather | bytes 557056 | tf_op jit(solution)/shard_map/all_gather | solution.py:59
  42.2 0.0 copy-done.1
  42.2 1.1 fusion.51
  43.2 0.0 copy-start.4
  43.2 0.0 copy-start.7
  43.2 0.0 copy-start.9
  43.2 0.0 all-reduce.2.cloned.1.call-update
  43.3 0.0 all-gather.2.cloned.1.call-start
  43.3 21.1 %all-reduce.2.cloned.1.call-done = f32[256,288]{0,1:T(8,128)} async-done(((f32[256,288]{0,1:T(8,128)}), f32[256,288]{0,1:T(8,128)}) %all-reduce.2.cloned.1.call-update) | async-done | bytes 294928 | tf_op jit(solution)/shard_map/psum | solution.py:63
  64.4 0.0 copy-done.2
  64.4 1.6 add_convert_fusion
  66.0 0.0 all-gather.2.cloned.1.call-update
  66.1 0.0 reduce-scatter.3.cloned.1.call-start
  66.1 0.0 copy-done.5
  66.1 42.9 %all-gather.2.cloned.1.call-done = bf16[256,4608]{0,1:T(8,128)(2,1)} async-done(((bf16[256,288]{0,1:T(8,128)(2,1)}), bf16[256,4608]{0,1:T(8,128)(2,1)}) %all-gather.2.cloned.1.call-update) | async-done | bytes 2359312 | tf_op jit(solution)/shard_map/all_gather | solution.py:66
  109.0 0.0 copy-done
  109.0 0.0 copy-done.6
  109.0 0.0 copy-done.8
  109.0 3.3 %fusion.27 = f32[256,256]{1,0:T(8,128)} fusion(bf16[256,256]{1,0:T(8,128)(2,1)S(1)} %copy-done.6, bf16[256,4608]{0,1:T(8,128)(2,1)} %all-gather.2.cloned.1.call-done, bf16[4608,256]{1,0:T(8,128)(2,1)S(1)} %copy-done, f32[256]{0:T(256)S(1)} %convert_multiply_fusion, f32[256]{0:T(256)S(1)} %copy-done.8), kind=kOutput, calls=%fused_computation.17 | convolution fusion | flops 637927424 | bytes 5113856 | tf_op jit(solution)/shard_map/dot_general | solution.py:75
  112.3 0.0 reduce-scatter.3.cloned.1.call-update
  112.4 0.0 reduce-scatter.5.cloned.1.call-start
  112.4 10.6 %reduce-scatter.3.cloned.1.call-done = f32[128,256]{1,0:T(8,128)} async-done(((f32[256,256]{1,0:T(8,128)}), f32[128,256]{1,0:T(8,128)}) %reduce-scatter.3.cloned.1.call-update) | async-done | bytes 131088 | tf_op jit(solution)/shard_map/reduce_scatter | solution.py:74
  123.0 0.0 reduce-scatter.5.cloned.1.call-update
  123.0 58.8 %reduce-scatter.5.cloned.1.call-done = f32[8,256]{1,0:T(8,128)} async-done(((f32[128,256]{1,0:T(8,128)}), f32[8,256]{1,0:T(8,128)}) %reduce-scatter.5.cloned.1.call-update) | async-done | bytes 8208 | tf_op jit(solution)/shard_map/reduce_scatter | solution.py:80
  181.8 0.0 copy-done.4
  181.8 0.7 broadcast_add_fusion
  182.5 0.0 copy-done.7
  182.5 0.0 copy-done.9
  182.5 0.0 copy-start.3
  182.5 0.7 convolution_add_fusion.1
  183.2 0.0 copy-done.3
  (3 shorter events, 0.0 us)
Async XLA Ops:
  7.2 101.8 %copy-start = (bf16[4608,256]{1,0:T(8,128)(2,1)S(1)}, bf16[4608,256]{1,0:T(8,128)(2,1)}, u32[]{:S(2)}) copy-start(bf16[4608,256]{1,0:T(8,128)(2,1)} %param.23) | copy-start | bytes 7077892
  7.2 57.2 %all-reduce.2.cloned.1.call-start = ((), (), s32[]{:S(2)}) async-start(), calls=%async_computation.2 | async-start | bytes 589824 | tf_op jit(solution)/shard_map/psum | solution.py:63
  14.2 28.0 %copy-start.1 = (bf16[1024,288]{0,1:T(8,128)(2,1)S(1)}, bf16[1024,288]{0,1:T(8,128)(2,1)}, u32[]{:S(2)}) copy-start(bf16[1024,288]{0,1:T(8,128)(2,1)} %param.21) | copy-start | bytes 1769476
  14.5 49.9 %copy-start.2 = (bf16[256,288]{0,1:T(8,128)(2,1)S(1)}, bf16[256,288]{0,1:T(8,128)(2,1)}, u32[]{:S(2)}) copy-start(bf16[256,288]{0,1:T(8,128)(2,1)} %param.22) | copy-start | bytes 442372
  14.5 51.6 %copy-start.5 = (s32[256]{0:T(256)S(1)}, s32[256]{0:T(256)}, u32[]{:S(2)}) copy-start(s32[256]{0:T(256)} %param.25) | copy-start | bytes 3076
  14.5 94.5 %copy-start.6 = (bf16[256,256]{1,0:T(8,128)(2,1)S(1)}, bf16[256,256]{1,0:T(8,128)(2,1)}, u32[]{:S(2)}) copy-start(bf16[256,256]{1,0:T(8,128)(2,1)} %param.26) | copy-start | bytes 393220
  14.5 94.5 %copy-start.8 = (f32[256]{0:T(256)S(1)}, f32[256]{0:T(256)}, u32[]{:S(2)}) copy-start(f32[256]{0:T(256)} %param.24) | copy-start | bytes 3076
  43.2 138.5 %copy-start.4 = (f32[256]{0:T(256)S(1)}, f32[256]{0:T(256)}, u32[]{:S(2)}) copy-start(f32[256]{0:T(256)} %param.27) | copy-start | bytes 3076
  43.2 139.2 %copy-start.7 = (f32[256,16]{0,1:T(8,128)S(1)}, f32[256,16]{0,1:T(8,128)}, u32[]{:S(2)}) copy-start(f32[256,16]{0,1:T(8,128)} %param.28) | copy-start | bytes 49156
  43.2 139.2 %copy-start.9 = (f32[16]{0:T(128)S(1)}, f32[16]{0:T(128)}, u32[]{:S(2)}) copy-start(f32[16]{0:T(128)} %param.29) | copy-start | bytes 196
  43.3 65.8 %all-gather.2.cloned.1.call-start = ((), (), s32[]{:S(2)}) async-start(), calls=%async_computation.3 | async-start | bytes 2506752 | tf_op jit(solution)/shard_map/all_gather | solution.py:66
  66.1 56.9 %reduce-scatter.3.cloned.1.call-start = ((), (), s32[]{:S(2)}) async-start(), calls=%async_computation.4 | async-start | bytes 393216 | tf_op jit(solution)/shard_map/reduce_scatter | solution.py:74
  112.4 69.4 %reduce-scatter.5.cloned.1.call-start = ((), (), s32[]{:S(2)}) async-start(), calls=%async_computation.5 | async-start | bytes 139264 | tf_op jit(solution)/shard_map/reduce_scatter | solution.py:80
  182.5 0.8 copy-start.3
Sparse Core Ops, SparseCore 0:
  43.4 20.9 all-reduce.1
  66.7 42.3 all-gather.1
  112.5 10.4 reduce-scatter.2
  126.7 55.0 reduce-scatter.4
where the time goes:
time: 190 us
  waiting for transfers between devices  133 us (70%)
  blocking collectives  24.6 us (13%)
  between operations  13.9 us (7%)
  matrix products  11.8 us (6%)
  other arithmetic  3.25 us (2%)
  local copies, waits for them, and re-layouts  2.77 us (1%)
    reduce_scatter x1, waiting for transfers between devices, body(): summed = lax.psum_scatter(halfway, 'lat', scatter_dimension=0, tiled=True)  58.8 us
    all_gather x1, waiting for transfers between devices, body(): lax.all_gather(stream, 'lat', axis=1, tiled=True)  42.9 us
    all_gather x1, blocking collectives, body(): lax.all_gather(attended, 'lat', axis=0, tiled=True)  24.6 us
    psum x1, waiting for transfers between devices, body(): projected = lax.psum(partial_heads, 'tp')  21.1 us
    reduce_scatter x1, waiting for transfers between devices, body(): lax.psum_scatter(jnp.dot(activations, probe_weight, preferred_element_typ...  10.6 us
  transfers between devices with their start and end apart: 4, of which 4 were waited for; matrix products, arithmetic and copies ran while one was open for 0% of the time, Pallas kernels for 0%

commit v1 on v0

--- a/solution.py
+++ b/solution.py
@@ -1,7 +1,9 @@
 import jax
 import jax.numpy as jnp
 from jax import lax
-from jax.sharding import PartitionSpec as P
+from jax.experimental import pallas as pl
+from jax.experimental.pallas import tpu as pltpu
+from jax.sharding import Mesh, PartitionSpec as P
 
 HEAD = 128
 
@@ -9,6 +11,9 @@
 SOFT_CAP = 50.0
 QUERY_SCALE = 1.0 / 12.0
 RAMP_WIDTH = 0.25
+
+ALL = ("y", "z", "x", "c")
+PLANE = ("y", "z", "x")
 
 
 def attend(queries, key_cache, value_cache, new_key, new_value, lengths):
@@ -35,6 +40,141 @@
     )
     mixture = mixture + own_weight.astype(jnp.float32)[..., None] * fresh_value
     return mixture.reshape(row_count, kv_heads * group_size * HEAD).astype(jnp.bfloat16)
+
+
+def xor(value, bits):
+    return lax.ppermute(value, ALL, [(i, i ^ bits) for i in range(32)])
+
+
+def encode_kernel(
+    g00, g01, g10, g11, enc_own, enc_other, bias, threshold, probe_own, probe_other, out_ref, ordered
+):
+    z, x = lax.axis_index("z"), lax.axis_index("x")
+    pieces = ((g00, g10), (g01, g11))
+    block = g00.shape[2]
+    pre_own = jnp.zeros((2 * g00.shape[1], enc_own.shape[1]), jnp.float32)
+    pre_other = pre_own
+    for dx in range(2):
+        for dz in range(4):
+            start = pl.multiple_of(((z ^ dz) * 2 + (x ^ dx)) * block, block)
+            rows = jnp.concatenate([pieces[dx][0][dz], pieces[dx][1][dz]], axis=0)
+            pre_own += jnp.dot(rows, enc_own[pl.ds(start, block), :], preferred_element_type=jnp.float32)
+            pre_other += jnp.dot(rows, enc_other[pl.ds(start, block), :], preferred_element_type=jnp.float32)
+
+    def activate(pre, at):
+        pre = pre + bias[at : at + 1, :]
+        ramped = jnp.clip((pre - threshold[at : at + 1, :]) / RAMP_WIDTH, 0.0, 1.0)
+        return (pre * ramped).astype(jnp.bfloat16)
+
+    partial = jnp.dot(activate(pre_own, 0), probe_own[...], preferred_element_type=jnp.float32)
+    partial += jnp.dot(activate(pre_other, 1), probe_other[...], preferred_element_type=jnp.float32)
+    for half in range(2):
+        for b in range(16):
+            at = half * 64 + b * 4
+            ordered[b, 4 * half : 4 * half + 4, :] = partial[at : at + 4, :]
+    out_ref[...] = ordered[...].astype(jnp.bfloat16)
+
+
+def vmem(count):
+    return [pl.BlockSpec(memory_space=pltpu.VMEM)] * count
+
+
+def encode(gathered, enc, bias, threshold, probe):
+    columns = probe[0].shape[1]
+    return pl.pallas_call(
+        encode_kernel,
+        out_shape=jax.ShapeDtypeStruct((16, 8, columns), jnp.bfloat16),
+        in_specs=vmem(10),
+        out_specs=pl.BlockSpec(memory_space=pltpu.VMEM),
+        scratch_shapes=[pltpu.VMEM((16, 8, columns), jnp.float32)],
+        compiler_params=pltpu.CompilerParams(vmem_limit_bytes=32 * 1024 * 1024),
+        name="encode",
+    )(*gathered, *enc, bias, threshold, *probe)
+
+
+def finish_kernel(parts, probe_bias, head_weight, head_bias, scores_ref, logits_ref):
+    sums = parts[...].astype(jnp.float32)
+    first = jnp.sum(sums[:8], axis=0)
+    second = jnp.sum(sums[8:], axis=0)
+    scores = first + jnp.concatenate([second[4:], second[:4]], axis=0) + probe_bias[...]
+    scores_ref[...] = scores
+    gated = scores / (1.0 + jnp.exp(-scores))
+    logits_ref[...] = (
+        jnp.dot(gated, head_weight[...], precision=lax.Precision.HIGHEST, preferred_element_type=jnp.float32)
+        + head_bias[...]
+    )
+
+
+def finish(parts, probe_bias, head_weight, head_bias):
+    rows, columns = parts.shape[1:]
+    return pl.pallas_call(
+        finish_kernel,
+        out_shape=(
+            jax.ShapeDtypeStruct((rows, columns), jnp.float32),
+            jax.ShapeDtypeStruct((rows, head_weight.shape[1]), jnp.float32),
+        ),
+        in_specs=vmem(4),
+        out_specs=tuple(vmem(2)),
+        name="finish",
+    )(parts, probe_bias.reshape(1, -1), head_weight, head_bias.reshape(1, -1))
+
+
+def chip_body(
+    queries,
+    key_cache,
+    value_cache,
+    new_key,
+    new_value,
+    lengths,
+    out_proj,
+    residual,
+    enc_weight,
+    enc_bias,
+    threshold_code,
+    probe_weight,
+    probe_bias,
+    head_weight,
+    head_bias,
+):
+    y, c = lax.axis_index("y"), lax.axis_index("c")
+    width = out_proj.shape[1]
+    proj_y = xor(out_proj, 16)
+    enc_other = xor(enc_weight, 1)
+    proj_c = xor(out_proj, 1)
+    probe_other = xor(probe_weight, 1)
+    levels = jnp.stack([enc_bias, threshold_code.astype(jnp.float32) / 16.0])
+    levels_other = xor(levels, 1)
+    bias = jnp.stack([levels[0], levels_other[0]])
+    threshold = jnp.stack([levels[1], levels_other[1]])
+    kept = residual.reshape(16, 2, 2, 4, width)
+    kept_own = lax.dynamic_slice(kept, (0, c, y, 0, 0), (16, 1, 1, 4, width)).reshape(64, width)
+    kept_given = lax.dynamic_slice(kept, (0, 1 - c, y, 0, 0), (16, 1, 1, 4, width)).reshape(64, width)
+    kept_other = xor(kept_given, 1)
+    proj_yc = xor(proj_y, 1)
+
+    attended = attend(queries, key_cache, value_cache, new_key, new_value, lengths)
+    half_width = attended.shape[1]
+    split = attended.reshape(2, 2, 4, half_width).transpose(1, 0, 2, 3)
+    sent = jnp.broadcast_to(split[:, None], (2, 8, 2, 4, half_width)).reshape(32, 4, half_width)
+    taken = lax.all_to_all(sent, ALL, 0, 0, tiled=True).reshape(2, 64, half_width)
+    mine = lax.dynamic_index_in_dim(taken, y, 0, keepdims=False)
+    theirs = lax.dynamic_index_in_dim(taken, 1 - y, 0, keepdims=False)
+
+    def project(kept_rows, near, far):
+        projected = jnp.dot(mine, near, preferred_element_type=jnp.float32)
+        projected = projected + jnp.dot(theirs, far, preferred_element_type=jnp.float32)
+        return (kept_rows.astype(jnp.float32) + projected).astype(jnp.bfloat16)
+
+    stream_own = project(kept_own, out_proj, proj_y)
+    stream_other = project(kept_other, proj_c, proj_yc)
+    stream = jnp.concatenate(
+        [jnp.where(c == 0, stream_own, stream_other), jnp.where(c == 0, stream_other, stream_own)], axis=1
+    )
+    along_z = jnp.stack([stream, xor(stream, 4), xor(stream, 8), xor(stream, 12)])
+    gathered = (along_z, xor(along_z, 2), xor(along_z, 16), xor(along_z, 18))
+    partial = encode(gathered, (enc_weight, enc_other), bias, threshold, (probe_weight, probe_other))
+    parts = lax.all_to_all(partial, PLANE, 0, 0, tiled=True)
+    return finish(parts, probe_bias, head_weight, head_bias)
 
 
 def body(
@@ -92,22 +232,30 @@
 
 
 def solution(mesh):
+    chips = mesh.shape["tp"] == 2 and mesh.shape["lat"] == 16
+    tp, lat = "tp", "lat"
+    if chips:
+        mesh = Mesh(mesh.devices.reshape(2, 4, 2, 2), ALL)
+        tp, lat = ("y",), ("z", "x", "c")
+    both = ALL if chips else ("tp", "lat")
     in_specs = (
-        P("lat", "tp"),
-        P("lat", None, "tp"),
-        P("lat", None, "tp"),
-        P("lat", "tp"),
-        P("lat", "tp"),
-        P("lat"),
-        P("tp", "lat"),
-        P(None, "lat"),
-        P(None, ("tp", "lat")),
-        P(("tp", "lat")),
-        P(("tp", "lat")),
-        P(("tp", "lat"), None),
+        P(lat, tp),
+        P(lat, None, tp),
+        P(lat, None, tp),
+        P(lat, tp),
+        P(lat, tp),
+        P(lat),
+        P(tp, lat),
+        P(None, lat),
+        P(None, both),
+        P(both),
+        P(both),
+        P(both, None),
         P(),
         P(),
         P(),
     )
-    out_specs = (P(("tp", "lat"), None), P(("tp", "lat"), None))
-    return jax.shard_map(body, mesh=mesh, in_specs=in_specs, out_specs=out_specs, check_vma=False)
+    out_specs = (P(both, None), P(both, None))
+    return jax.shard_map(
+        chip_body if chips else body, mesh=mesh, in_specs=in_specs, out_specs=out_specs, check_vma=False
+    )

time: 190 us -> 79.3 us (0.42)
  waiting for transfers between devices: 133 us -> 34.2 us
  blocking collectives: 24.6 us -> 0 us
  starting transfers between devices: 0.16 us -> 22.3 us
  between operations: 13.9 us -> 0.9 us
  Pallas kernels: 0 us -> 5.26 us
  other arithmetic: 3.25 us -> 1.06 us
    reduce_scatter x2 -> x0, waiting for transfers between devices: 69.3 us -> none  [the longest x1 58.8 us: body(): summed = lax.psum_scatter(halfway, 'lat', scatter_dimension=0, tiled=True)]
    all_gather x1 -> x0, waiting for transfers between devices: 42.9 us -> none  [body(): lax.all_gather(stream, 'lat', axis=1, tiled=True)]
    all_gather x1 -> x0, blocking collectives: 24.6 us -> none  [body(): lax.all_gather(attended, 'lat', axis=0, tiled=True)]
    psum x1 -> x0, waiting for transfers between devices: 21.1 us -> none  [body(): projected = lax.psum(partial_heads, 'tp')]
    ppermute x0 -> x13, waiting for transfers between devices: none -> 18.5 us  [xor(): return lax.ppermute(value, ALL, [(i, i ^ bits) for i in range(32)])]
    all_to_all x0 -> x2, waiting for transfers between devices: none -> 15.7 us  [the longest x1 8.95 us: chip_body(): lax.all_to_all(sent, ALL, 0, 0, tiled=True).reshape(2, 64, half_width)]
    ppermute x0 -> x13, starting transfers between devices: none -> 12.4 us  [xor(): return lax.ppermute(value, ALL, [(i, i ^ bits) for i in range(32)])]
    all_to_all x0 -> x2, starting transfers between devices: none -> 9.89 us  [the longest x1 5 us: chip_body(): lax.all_to_all(sent, ALL, 0, 0, tiled=True).reshape(2, 64, half_width)]
  transfers between devices with their start and end apart: 4 -> 15, of which waited for: 4 -> 6; matrix products, arithmetic and copies ran while one was open for 0% -> 20% of each run, Pallas kernels for 0% -> 0%
where the time goes in v1:
time: 79.3 us; the launch traced here: 78.7 us
  waiting for transfers between devices  34.2 us (43%)
  starting transfers between devices  22.3 us (28%)
  matrix products  11.2 us (14%)
  Pallas kernels  5.26 us (7%)
  local copies, waits for them, and re-layouts  3.83 us (5%)
  other arithmetic  1.06 us (1%)
  between operations  0.9 us (1%)
    ppermute x13, waiting for transfers between devices, xor(): return lax.ppermute(value, ALL, [(i, i ^ bits) for i in range(32)])  18.5 us
    ppermute x13, starting transfers between devices, xor(): return lax.ppermute(value, ALL, [(i, i ^ bits) for i in range(32)])  12.4 us
    all_to_all x1, waiting for transfers between devices, chip_body(): lax.all_to_all(sent, ALL, 0, 0, tiled=True).reshape(2, 64, half_width)  8.95 us
    all_to_all x1, waiting for transfers between devices, chip_body(): parts = lax.all_to_all(partial, PLANE, 0, 0, tiled=True)  6.77 us
    all_to_all x1, starting transfers between devices, chip_body(): lax.all_to_all(sent, ALL, 0, 0, tiled=True).reshape(2, 64, half_width)  5 us
    all_to_all x1, starting transfers between devices, chip_body(): parts = lax.all_to_all(partial, PLANE, 0, 0, tiled=True)  4.89 us
    pallas_call x1, Pallas kernels, encode(): pl.pallas_call(encode_kernel, out_shape=jax.ShapeDtypeStruct((16, 8, colu...  3.49 us
    dot_general x1, matrix products, attend(): jnp.einsum('rkgd,rlkd->rkgl', grouped, key_rows, preferred_element_type=j...  3.48 us
  transfers between devices with their start and end apart: 15, of which 6 were waited for; matrix products, arithmetic and copies ran while one was open for 20% of the time, Pallas kernels for 0%

profile of v1, /device:TPU:0, one launch (start us, length us, event | category | flops | bytes accessed | tf_op | source)
XLA Modules:
  0.0 78.7 jit_solution(14084884408547781506)
XLA Ops:
  0.6 0.0 copy-start.4
  0.6 3.0 %collective-permute-start = (bf16[1024,288]{0,1:T(8,128)(2,1)}, bf16[1024,288]{0,1:T(8,128)(2,1)}, u32[]{:S(2)}, u32[]{:S(2)}) collective-permute-start(bf16[1024,288]{0,1:T(8,128)(2,1)} %param.21), channel_id=1, source_target_pairs={{0,16},{1,17},{2,18},{3,19},{4,20},{5,21},{6,22},{7,23},{8,24},{9,... | collective-permute-start | bytes 1769480 | tf_op jit(solution)/shard_map/ppermute | solution.py:46
  3.7 0.0 collective-permute-start.10
  3.7 0.8 reshape.72
  4.5 0.7 iota_compare_fusion
  5.2 3.5 %fusion.52 = (f32[16,4,2]{2,1,0:T(4,128)S(1)}, f32[16,4,2,256]{3,2,1,0:T(2,128)S(1)}) fusion(bf16[16,4,2,128]{3,2,1,0:T(2,128)(2,1)S(1)} %reshape.72, pred[16,256]{1,0:T(8,128)(4,1)S(1)} %iota_compare_fusion, bf16[16,256,512]{2,1,0:T(8,128)(2,1)} %param.16), kind=kOutput, calls=%fused_computation.54 | convolution fusion | flops 8519552 | bytes 4362752 | tf_op jit(solution)/shard_map/rkgd,rlkd->rkgl/dot_general | solution.py:28
  8.7 0.0 copy-start.3
  8.7 0.1 copy.37
  8.8 0.0 copy-done.4
  8.8 0.2 fusion.53
  9.0 0.1 copy.44
  9.2 0.1 copy.38
  9.3 0.1 copy.40
  9.4 0.0 copy-start.8
  9.4 0.0 copy-start.7
  9.4 2.9 %fusion.25 = bf16[16,4,2,128]{3,2,1,0:T(2,128)(2,1)S(1)} fusion(f32[16,4,2,256]{3,2,1,0:T(2,128)S(1)} %get-tuple-element.11, f32[16,4,2]{2,1,0:T(4,128)S(1)} %copy.38, f32[16,4,128]{2,1,0:T(4,128)S(1)} %reshape.82, f32[16,4,2]{2,1,0:T(4,128)S(1)} %copy.40, bf16[16,256,512]{2,1,0:T(8,128)(2,1)} %param.17), kind=kOutput, calls=%fused_computation.17 | convolution fusion | flops 8503296 | bytes 4391936 | tf_op jit(solution)/shard_map/rkgl,rlkd->rkgd/dot_general | solution.py:38
  12.3 0.0 copy-start.1
  12.3 0.0 copy-start
  12.4 0.8 %broadcast_in_dim.16 = bf16[2,8,2,4,1024]{4,3,2,1,0:T(4,128)(2,1)} broadcast(bf16[2,2,4,1024]{3,2,1,0:T(4,128)(2,1)S(1)} %copy.41), dimensions={0,2,3,4} | broadcast | bytes 294912 | tf_op jit(solution)/shard_map/broadcast_in_dim | solution.py:158
  13.2 5.0 %all-to-all-start = ((bf16[32,4,1024]{2,1,0:T(4,128)(2,1)}), bf16[32,4,1024]{2,1,0:T(4,128)(2,1)S(1)}, u32[]{:S(2)}, u32[]{:S(2)}) async-start(bf16[32,4,1024]{2,1,0:T(4,128)(2,1)} %bitcast.2), calls=%async_computation | async-start | bytes 524288 | tf_op jit(solution)/shard_map/all_to_all | solution.py:159
  18.2 0.3 collective-permute-start.2
  18.5 0.0 copy-done.3
  18.5 0.2 copy.35
  18.7 0.1 reshape.71
  18.9 0.3 collective-permute-start.1
  19.2 0.3 collective-permute-start.11
  19.6 9.0 %all-to-all-done = bf16[32,4,1024]{2,1,0:T(4,128)(2,1)S(1)} async-done(((bf16[32,4,1024]{2,1,0:T(4,128)(2,1)}), bf16[32,4,1024]{2,1,0:T(4,128)(2,1)S(1)}, u32[]{:S(2)}, u32[]{:S(2)}) %all-to-all-start) | async-done | bytes 262176 | tf_op jit(solution)/shard_map/all_to_all | solution.py:159
  28.5 0.1 reshape.77
  28.6 0.0 collective-permute-done
  28.6 0.4 collective-permute-start.3
  29.0 1.4 %fusion.35 = f32[64,288]{1,0:T(8,128)S(1)} fusion(bf16[1024,288]{0,1:T(8,128)(2,1)} %param.21, bf16[2,64,1024]{2,1,0:T(8,128)(2,1)S(1)} %reshape.77, s32[]{:T(128)S(6)} %select_n.33), kind=kOutput, calls=%fused_computation.24 | convolution fusion | flops 37748736 | bytes 794628 | tf_op jit(solution)/shard_map/dot_general | solution.py:164
  30.4 1.4 %fusion.20 = bf16[64,288]{1,0:T(8,128)(2,1)S(1)} fusion(f32[64,288]{1,0:T(8,128)S(1)} %reshape.81, f32[64,288]{1,0:T(8,128)S(1)} %fusion.35, bf16[1024,288]{0,1:T(8,128)(2,1)} %collective-permute-done, bf16[2,64,1024]{2,1,0:T(8,128)(2,1)S(1)} %reshape.77, s32[]{:T(128)S(6)} %select_n.35), kind=kOutput, calls=%fused_computation.14 | convolution fusion | flops 37804032 | bytes 954372 | tf_op jit(solution)/shard_map/dot_general | solution.py:165
  31.8 0.0 collective-permute-done.2
  31.8 1.4 %fusion.33 = f32[64,288]{1,0:T(8,128)S(1)} fusion(bf16[1024,288]{0,1:T(8,128)(2,1)} %collective-permute-done.2, bf16[2,64,1024]{2,1,0:T(8,128)(2,1)S(1)} %reshape.77, s32[]{:T(128)S(6)} %select_n.33), kind=kOutput, calls=%fused_computation.22 | convolution fusion | flops 37748736 | bytes 794628 | tf_op jit(solution)/shard_map/dot_general | solution.py:164
  33.2 0.0 copy-start.6
  33.2 0.0 collective-permute-done.1
  33.2 0.0 collective-permute-done.3
  33.3 0.4 broadcast_select_fusion.1
  33.6 0.1 pad_maximum_fusion.1
  33.7 0.9 %collective-permute-start.4 = (bf16[64,576]{1,0:T(8,128)(2,1)S(1)}, bf16[64,576]{1,0:T(8,128)(2,1)S(1)}, u32[]{:S(2)}, u32[]{:S(2)}) collective-permute-start(bf16[64,576]{1,0:T(8,128)(2,1)S(1)} %pad_maximum_fusion.1), channel_id=1, source_target_pairs={{0,4},{1,5},{2,6},{3,7},{4,0},{5,1},{6,2},{7,3},{8,12},{9,13},{10,... | collective-permute-start | bytes 221192 | tf_op jit(solution)/shard_map/ppermute | solution.py:46
  34.6 1.4 %collective-permute-start.5 = (bf16[64,576]{1,0:T(8,128)(2,1)S(1)}, bf16[64,576]{1,0:T(8,128)(2,1)S(1)}, u32[]{:S(2)}, u32[]{:S(2)}) collective-permute-start(bf16[64,576]{1,0:T(8,128)(2,1)S(1)} %pad_maximum_fusion.1), channel_id=1, source_target_pairs={{0,8},{1,9},{2,10},{3,11},{4,12},{5,13},{6,14},{7,15},{8,0},{9,1},... | collective-permute-start | bytes 221192 | tf_op jit(solution)/shard_map/ppermute | solution.py:46
  36.0 2.1 %collective-permute-start.6 = (bf16[64,576]{1,0:T(8,128)(2,1)S(1)}, bf16[64,576]{1,0:T(8,128)(2,1)S(1)}, u32[]{:S(2)}, u32[]{:S(2)}) collective-permute-start(bf16[64,576]{1,0:T(8,128)(2,1)S(1)} %pad_maximum_fusion.1), channel_id=1, source_target_pairs={{0,12},{1,13},{2,14},{3,15},{4,8},{5,9},{6,10},{7,11},{8,4},{9,5},... | collective-permute-start | bytes 221192 | tf_op jit(solution)/shard_map/ppermute | solution.py:46
  38.2 0.1 fusion.61
  38.2 0.1 collective-permute-done.4
  38.3 0.0 collective-permute-start.12
  38.3 5.8 %collective-permute-done.5 = bf16[64,576]{1,0:T(8,128)(2,1)S(1)} collective-permute-done((bf16[64,576]{1,0:T(8,128)(2,1)S(1)}, bf16[64,576]{1,0:T(8,128)(2,1)S(1)}, u32[]{:S(2)}, u32[]{:S(2)}) %collective-permute-start.5) | collective-permute-done | bytes 73760 | tf_op jit(solution)/shard_map/ppermute | solution.py:46
  44.1 0.0 collective-permute-done.6
  44.1 0.1 pad_maximum_fusion.g00
  44.2 0.8 %collective-permute-start.7 = (bf16[4,64,576]{2,1,0:T(8,128)(2,1)S(1)}, bf16[4,64,576]{2,1,0:T(8,128)(2,1)S(1)}, u32[]{:S(2)}, u32[]{:S(2)}) collective-permute-start(bf16[4,64,576]{2,1,0:T(8,128)(2,1)S(1)} %pad_maximum_fusion.g00), channel_id=1, source_target_pairs={{0,2},{1,3},{2,0},{3,1},{4,6},{5,7},{6,4},{7,5},{8,10},{9,11},{10,... | collective-permute-start | bytes 884744 | tf_op jit(solution)/shard_map/ppermute | solution.py:46
  45.0 0.5 collective-permute-start.8
  45.6 0.0 collective-permute-done.11
  45.6 2.2 %collective-permute-start.9 = (bf16[4,64,576]{2,1,0:T(8,128)(2,1)S(1)}, bf16[4,64,576]{2,1,0:T(8,128)(2,1)S(1)}, u32[]{:S(2)}, u32[]{:S(2)}) collective-permute-start(bf16[4,64,576]{2,1,0:T(8,128)(2,1)S(1)} %pad_maximum_fusion.g00), channel_id=1, source_target_pairs={{0,18},{1,19},{2,16},{3,17},{4,22},{5,23},{6,20},{7,21},{8,26},{9,... | collective-permute-start | bytes 884744 | tf_op jit(solution)/shard_map/ppermute | solution.py:46
  47.8 0.0 collective-permute-done.12.probe_other
  47.8 7.1 %collective-permute-done.7.g01 = bf16[4,64,576]{2,1,0:T(8,128)(2,1)S(1)} collective-permute-done((bf16[4,64,576]{2,1,0:T(8,128)(2,1)S(1)}, bf16[4,64,576]{2,1,0:T(8,128)(2,1)S(1)}, u32[]{:S(2)}, u32[]{:S(2)}) %collective-permute-start.7) | collective-permute-done | bytes 294944 | tf_op jit(solution)/shard_map/ppermute | solution.py:46
  54.9 0.0 collective-permute-done.8.g10
  54.9 5.5 %collective-permute-done.9.g11 = bf16[4,64,576]{2,1,0:T(8,128)(2,1)S(1)} collective-permute-done((bf16[4,64,576]{2,1,0:T(8,128)(2,1)S(1)}, bf16[4,64,576]{2,1,0:T(8,128)(2,1)S(1)}, u32[]{:S(2)}, u32[]{:S(2)}) %collective-permute-start.9) | collective-permute-done | bytes 294944 | tf_op jit(solution)/shard_map/ppermute | solution.py:46
  60.4 0.0 collective-permute-done.10.enc_other
  60.4 3.5 %encode.1 = bf16[16,8,256]{2,1,0:T(8,128)(2,1)} custom-call(bf16[4,64,576]{2,1,0:T(8,128)(2,1)S(1)} %pad_maximum_fusion.g00, bf16[4,64,576]{2,1,0:T(8,128)(2,1)S(1)} %collective-permute-done.7.g01, bf16[4,64,576]{2,1,0:T(8,128)(2,1)S(1)} %collective-permute-done.8.g10, bf16[4,64,576]{2,1,0:T(8,128)(2,1)S(1)} %collective-permute-done.9.g11, ...), custom_call_target="tpu_custom_call" | custom-call | tf_op jit(solution)/shard_map/encode/pallas_call | solution.py:84
  63.9 4.9 %all-to-all-start.1 = ((bf16[16,8,256]{2,1,0:T(8,128)(2,1)}), bf16[16,8,256]{2,1,0:T(8,128)(2,1)S(1)}, u32[]{:S(2)}, u32[]{:S(2)}) async-start(bf16[16,8,256]{2,1,0:T(8,128)(2,1)} %encode.1), calls=%async_computation.1 | async-start | bytes 131072 | tf_op jit(solution)/shard_map/all_to_all | solution.py:176
  68.8 0.0 copy-done.6
  68.8 0.8 copy.42.head_weight
  69.6 6.8 %all-to-all-done.1.parts = bf16[16,8,256]{2,1,0:T(8,128)(2,1)S(1)} async-done(((bf16[16,8,256]{2,1,0:T(8,128)(2,1)}), bf16[16,8,256]{2,1,0:T(8,128)(2,1)S(1)}, u32[]{:S(2)}, u32[]{:S(2)}) %all-to-all-start.1) | async-done | bytes 65568 | tf_op jit(solution)/shard_map/all_to_all | solution.py:176
  76.3 0.6 copy-done.2
  77.0 1.8 %finish.1 = (f32[8,256]{1,0:T(8,128)}, f32[8,16]{1,0:T(8,128)}) custom-call(bf16[16,8,256]{2,1,0:T(8,128)(2,1)} %copy-done.2, f32[1,256]{1,0:T(1,128)} %bitcast.84, f32[256,16]{1,0:T(8,128)} %copy.42.head_weight, f32[1,16]{1,0:T(1,128)} %bitcast.85), custom_call_target="tpu_custom_call" | custom-call | tf_op jit(solution)/shard_map/finish/pallas_call | solution.py:110
  (19 shorter events, 0.2 us)
Async XLA Ops:
  0.6 8.2 %copy-start.4 = (bf16[16,512]{1,0:T(8,128)(2,1)S(1)}, bf16[16,512]{1,0:T(8,128)(2,1)}, u32[]{:S(2)}) copy-start(bf16[16,512]{1,0:T(8,128)(2,1)} %param.18) | copy-start | bytes 49156
  0.6 8.7 %copy-start.5 = (bf16[16,512]{1,0:T(8,128)(2,1)S(1)}, bf16[16,512]{1,0:T(8,128)(2,1)}, u32[]{:S(2)}) copy-start(bf16[16,512]{1,0:T(8,128)(2,1)} %param.19) | copy-start | bytes 49156
  0.6 27.9 %collective-permute-start = (bf16[1024,288]{0,1:T(8,128)(2,1)}, bf16[1024,288]{0,1:T(8,128)(2,1)}, u32[]{:S(2)}, u32[]{:S(2)}) collective-permute-start(bf16[1024,288]{0,1:T(8,128)(2,1)} %param.21), channel_id=1, source_target_pairs={{0,16},{1,17},{2,18},{3,19},{4,20},{5,21},{6,22},{7,23},{8,24},{9,... | collective-permute-start | bytes 1769480 | tf_op jit(solution)/shard_map/ppermute | solution.py:46
  3.7 56.7 %collective-permute-start.10 = (bf16[4608,256]{1,0:T(8,128)(2,1)}, bf16[4608,256]{1,0:T(8,128)(2,1)}, u32[]{:S(2)}, u32[]{:S(2)}) collective-permute-start(bf16[4608,256]{1,0:T(8,128)(2,1)} %enc_own.1), channel_id=1, source_target_pairs={{0,1},{1,0},{2,3},{3,2},{4,5},{5,4},{6,7},{7,6},{8,9},{9,8},{10,11... | collective-permute-start | bytes 7077896 | tf_op jit(solution)/shard_map/ppermute | solution.py:46
  8.7 9.9 %copy-start.3 = (bf16[256,288]{0,1:T(8,128)(2,1)S(1)}, bf16[256,288]{0,1:T(8,128)(2,1)}, u32[]{:S(2)}) copy-start(bf16[256,288]{0,1:T(8,128)(2,1)} %param.22) | copy-start | bytes 442372
  9.4 9.8 %copy-start.8 = (s32[256]{0:T(256)S(1)}, s32[256]{0:T(256)}, u32[]{:S(2)}) copy-start(s32[256]{0:T(256)} %param.25) | copy-start | bytes 3076
  9.4 9.8 %copy-start.7 = (f32[256]{0:T(256)S(1)}, f32[256]{0:T(256)}, u32[]{:S(2)}) copy-start(f32[256]{0:T(256)} %param.24) | copy-start | bytes 3076
  12.3 26.0 %copy-start.1 = (bf16[256,256]{1,0:T(8,128)(2,1)S(1)}, bf16[256,256]{1,0:T(8,128)(2,1)}, u32[]{:S(2)}) copy-start(bf16[256,256]{1,0:T(8,128)(2,1)} %probe_own.1) | copy-start | bytes 393220
  12.3 48.1 %copy-start = (bf16[4608,256]{1,0:T(8,128)(2,1)S(1)}, bf16[4608,256]{1,0:T(8,128)(2,1)}, u32[]{:S(2)}) copy-start(bf16[4608,256]{1,0:T(8,128)(2,1)} %enc_own.1) | copy-start | bytes 7077892
  13.2 15.3 %all-to-all-start = ((bf16[32,4,1024]{2,1,0:T(4,128)(2,1)}), bf16[32,4,1024]{2,1,0:T(4,128)(2,1)S(1)}, u32[]{:S(2)}, u32[]{:S(2)}) async-start(bf16[32,4,1024]{2,1,0:T(4,128)(2,1)} %bitcast.2), calls=%async_computation | async-start | bytes 524288 | tf_op jit(solution)/shard_map/all_to_all | solution.py:159
  18.2 13.6 %collective-permute-start.2 = (bf16[1024,288]{0,1:T(8,128)(2,1)}, bf16[1024,288]{0,1:T(8,128)(2,1)}, u32[]{:S(2)}, u32[]{:S(2)}) collective-permute-start(bf16[1024,288]{0,1:T(8,128)(2,1)} %param.21), channel_id=1, source_target_pairs={{0,1},{1,0},{2,3},{3,2},{4,5},{5,4},{6,7},{7,6},{8,9},{9,8},{10,11... | collective-permute-start | bytes 1769480 | tf_op jit(solution)/shard_map/ppermute | solution.py:46
  18.9 14.4 %collective-permute-start.1 = (bf16[64,288]{1,0:T(8,128)(2,1)S(1)}, bf16[64,288]{1,0:T(8,128)(2,1)S(1)}, u32[]{:S(2)}, u32[]{:S(2)}) collective-permute-start(bf16[64,288]{1,0:T(8,128)(2,1)S(1)} %reshape.78), channel_id=1, source_target_pairs={{0,1},{1,0},{2,3},{3,2},{4,5},{5,4},{6,7},{7,6},{8,9},{9,8},{10,11... | collective-permute-start | bytes 110600 | tf_op jit(solution)/shard_map/ppermute | solution.py:46
  19.2 26.4 %collective-permute-start.11 = (f32[2,256]{1,0:T(2,128)S(1)}, f32[2,256]{1,0:T(2,128)S(1)}, u32[]{:S(2)}, u32[]{:S(2)}) collective-permute-start(f32[2,256]{1,0:T(2,128)S(1)} %pad_maximum_fusion.2), channel_id=1, source_target_pairs={{0,1},{1,0},{2,3},{3,2},{4,5},{5,4},{6,7},{7,6},{8,9},{9,8},{10,11... | collective-permute-start | bytes 6152 | tf_op jit(solution)/shard_map/ppermute | solution.py:46
  28.6 4.7 %collective-permute-start.3 = (bf16[1024,288]{0,1:T(8,128)(2,1)}, bf16[1024,288]{0,1:T(8,128)(2,1)S(1)}, u32[]{:S(2)}, u32[]{:S(2)}) collective-permute-start(bf16[1024,288]{0,1:T(8,128)(2,1)} %collective-permute-done), channel_id=1, source_target_pairs={{0,1},{1,0},{2,3},{3,2},{4,5},{5,4},{6,7},{7,6},{8,9},{9,8},{10,11... | collective-permute-start | bytes 1769480 | tf_op jit(solution)/shard_map/ppermute | solution.py:46
  33.2 35.6 %copy-start.6 = (f32[256,16]{0,1:T(8,128)S(1)}, f32[256,16]{0,1:T(8,128)}, u32[]{:S(2)}) copy-start(f32[256,16]{0,1:T(8,128)} %param.28) | copy-start | bytes 49156
  33.7 4.6 %collective-permute-start.4 = (bf16[64,576]{1,0:T(8,128)(2,1)S(1)}, bf16[64,576]{1,0:T(8,128)(2,1)S(1)}, u32[]{:S(2)}, u32[]{:S(2)}) collective-permute-start(bf16[64,576]{1,0:T(8,128)(2,1)S(1)} %pad_maximum_fusion.1), channel_id=1, source_target_pairs={{0,4},{1,5},{2,6},{3,7},{4,0},{5,1},{6,2},{7,3},{8,12},{9,13},{10,... | collective-permute-start | bytes 221192 | tf_op jit(solution)/shard_map/ppermute | solution.py:46
  34.6 9.5 %collective-permute-start.5 = (bf16[64,576]{1,0:T(8,128)(2,1)S(1)}, bf16[64,576]{1,0:T(8,128)(2,1)S(1)}, u32[]{:S(2)}, u32[]{:S(2)}) collective-permute-start(bf16[64,576]{1,0:T(8,128)(2,1)S(1)} %pad_maximum_fusion.1), channel_id=1, source_target_pairs={{0,8},{1,9},{2,10},{3,11},{4,12},{5,13},{6,14},{7,15},{8,0},{9,1},... | collective-permute-start | bytes 221192 | tf_op jit(solution)/shard_map/ppermute | solution.py:46
  36.0 8.1 %collective-permute-start.6 = (bf16[64,576]{1,0:T(8,128)(2,1)S(1)}, bf16[64,576]{1,0:T(8,128)(2,1)S(1)}, u32[]{:S(2)}, u32[]{:S(2)}) collective-permute-start(bf16[64,576]{1,0:T(8,128)(2,1)S(1)} %pad_maximum_fusion.1), channel_id=1, source_target_pairs={{0,12},{1,13},{2,14},{3,15},{4,8},{5,9},{6,10},{7,11},{8,4},{9,5},... | collective-permute-start | bytes 221192 | tf_op jit(solution)/shard_map/ppermute | solution.py:46
  38.3 9.4 %collective-permute-start.12 = (bf16[256,256]{1,0:T(8,128)(2,1)S(1)}, bf16[256,256]{1,0:T(8,128)(2,1)S(1)}, u32[]{:S(2)}, u32[]{:S(2)}) collective-permute-start(bf16[256,256]{1,0:T(8,128)(2,1)S(1)} %copy-done.1), channel_id=1, source_target_pairs={{0,1},{1,0},{2,3},{3,2},{4,5},{5,4},{6,7},{7,6},{8,9},{9,8},{10,11... | collective-permute-start | bytes 393224 | tf_op jit(solution)/shard_map/ppermute | solution.py:46
  44.2 10.7 %collective-permute-start.7 = (bf16[4,64,576]{2,1,0:T(8,128)(2,1)S(1)}, bf16[4,64,576]{2,1,0:T(8,128)(2,1)S(1)}, u32[]{:S(2)}, u32[]{:S(2)}) collective-permute-start(bf16[4,64,576]{2,1,0:T(8,128)(2,1)S(1)} %pad_maximum_fusion.g00), channel_id=1, source_target_pairs={{0,2},{1,3},{2,0},{3,1},{4,6},{5,7},{6,4},{7,5},{8,10},{9,11},{10,... | collective-permute-start | bytes 884744 | tf_op jit(solution)/shard_map/ppermute | solution.py:46
  45.0 9.9 %collective-permute-start.8 = (bf16[4,64,576]{2,1,0:T(8,128)(2,1)S(1)}, bf16[4,64,576]{2,1,0:T(8,128)(2,1)S(1)}, u32[]{:S(2)}, u32[]{:S(2)}) collective-permute-start(bf16[4,64,576]{2,1,0:T(8,128)(2,1)S(1)} %pad_maximum_fusion.g00), channel_id=1, source_target_pairs={{0,16},{1,17},{2,18},{3,19},{4,20},{5,21},{6,22},{7,23},{8,24},{9,... | collective-permute-start | bytes 884744 | tf_op jit(solution)/shard_map/ppermute | solution.py:46
  45.6 14.8 %collective-permute-start.9 = (bf16[4,64,576]{2,1,0:T(8,128)(2,1)S(1)}, bf16[4,64,576]{2,1,0:T(8,128)(2,1)S(1)}, u32[]{:S(2)}, u32[]{:S(2)}) collective-permute-start(bf16[4,64,576]{2,1,0:T(8,128)(2,1)S(1)} %pad_maximum_fusion.g00), channel_id=1, source_target_pairs={{0,18},{1,19},{2,16},{3,17},{4,22},{5,23},{6,20},{7,21},{8,26},{9,... | collective-permute-start | bytes 884744 | tf_op jit(solution)/shard_map/ppermute | solution.py:46
  63.9 12.4 %all-to-all-start.1 = ((bf16[16,8,256]{2,1,0:T(8,128)(2,1)}), bf16[16,8,256]{2,1,0:T(8,128)(2,1)S(1)}, u32[]{:S(2)}, u32[]{:S(2)}) async-start(bf16[16,8,256]{2,1,0:T(8,128)(2,1)} %encode.1), calls=%async_computation.1 | async-start | bytes 131072 | tf_op jit(solution)/shard_map/all_to_all | solution.py:176
  76.3 0.6 copy-start.2

commit v2 on v1

--- a/solution.py
+++ b/solution.py
@@ -46,28 +46,246 @@
     return lax.ppermute(value, ALL, [(i, i ^ bits) for i in range(32)])
 
 
-def encode_kernel(
-    g00, g01, g10, g11, enc_own, enc_other, bias, threshold, probe_own, probe_other, out_ref, ordered
+def cost(seconds):
+    return pl.CostEstimate(flops=0, bytes_accessed=int(seconds * 3.69e12), transcendentals=0)
+
+
+def vmem(count):
+    return [pl.BlockSpec(memory_space=pltpu.VMEM)] * count
+
+
+def attend_kernel(
+    lengths,
+    queries,
+    new_key,
+    new_value,
+    kept_own,
+    kept_other,
+    keys_at,
+    values_at,
+    out_ref,
+    kept_ref,
+    keys,
+    values,
+    heads,
+    mixed,
+    turned,
+    arrived,
 ):
+    row_count, positions, kv_width = keys.shape
+    head_count = queries.shape[1] // HEAD
+    kv_heads = kv_width // HEAD
+    group = 4
+    copies = []
+    for at in range(row_count // group):
+        rows = pl.ds(at * group, group)
+        copies.append(pltpu.make_async_copy(keys_at.at[rows], keys.at[rows], arrived.at[0, at]))
+        copies.append(pltpu.make_async_copy(values_at.at[rows], values.at[rows], arrived.at[1, at]))
+    for copy in copies:
+        copy.start()
+    y, c = lax.axis_index("y"), lax.axis_index("c")
+    for at, kept in enumerate((kept_own, kept_other)):
+        turned[...] = kept[...].astype(jnp.float32).T
+        for b in range(turned.shape[0] // 16):
+            both = turned[pl.ds(pl.multiple_of(b * 16 + 8 * c, 8), 8), :]
+            kept_ref[at, 4 * b : 4 * b + 4, :] = jnp.where(y == 0, both[:4], both[4:])
+    for head in range(head_count):
+        heads[pl.ds(head, row_count, stride=head_count), :] = queries[:, head * HEAD : (head + 1) * HEAD].astype(
+            jnp.float32
+        )
+    shape = (head_count, kv_width)
+    of_head = lax.broadcasted_iota(jnp.int32, shape, 0) // (head_count // kv_heads)
+    in_block = of_head == lax.broadcasted_iota(jnp.int32, shape, 1) // HEAD
+    place = lax.broadcasted_iota(jnp.int32, (head_count, positions), 1)
+    fresh_key = new_key[...].astype(jnp.float32)
+    fresh_value = new_value[...].astype(jnp.float32)
+
+    def cap(score):
+        return jnp.exp(SOFT_CAP * jnp.tanh(score * (QUERY_SCALE / SOFT_CAP)))
+
+    for at in range(row_count // group):
+        copies[2 * at].wait()
+        weights, own_weights = [], []
+        for row in range(at * group, (at + 1) * group):
+            query = heads[row * head_count : (row + 1) * head_count, :]
+            spread = jnp.where(in_block, jnp.concatenate([query] * kv_heads, axis=1), 0.0)
+            scores = lax.dot_general(
+                spread.astype(jnp.bfloat16),
+                keys[row],
+                (((1,), (1,)), ((), ())),
+                preferred_element_type=jnp.float32,
+            )
+            own = cap(jnp.sum(spread * fresh_key[row : row + 1, :], axis=1, keepdims=True))
+            exps = jnp.where(place < lengths[row], cap(scores), 0.0)
+            scale = 1.0 / (jnp.sum(exps, axis=1, keepdims=True) + own)
+            weights.append((exps * scale).astype(jnp.bfloat16))
+            own_weights.append((own * scale).astype(jnp.bfloat16).astype(jnp.float32))
+        copies[2 * at + 1].wait()
+        for nth, row in enumerate(range(at * group, (at + 1) * group)):
+            mixture = jnp.dot(weights[nth], values[row], preferred_element_type=jnp.float32)
+            mixture = jnp.where(in_block, mixture + own_weights[nth] * fresh_value[row : row + 1, :], 0.0)
+            folded = mixture[:, :HEAD]
+            for kv_head in range(1, kv_heads):
+                folded = folded + mixture[:, kv_head * HEAD : (kv_head + 1) * HEAD]
+            heads[row * head_count : (row + 1) * head_count, :] = folded
+    for head in range(head_count):
+        mixed[:, head * HEAD : (head + 1) * HEAD] = heads[pl.ds(head, row_count, stride=head_count), :]
+    for to_y in range(2):
+        for to_c in range(2):
+            share = mixed[8 * to_c + 4 * to_y : 8 * to_c + 4 * to_y + 4, :].astype(jnp.bfloat16)
+            for zx in range(8):
+                out_ref[to_y * 16 + zx * 2 + to_c] = share
+
+
+def attend_shares(queries, key_cache, value_cache, new_key, new_value, lengths, kept_own, kept_other):
+    rows, width = queries.shape
+    features, row_count = kept_own.shape
+    smem, hbm = pl.BlockSpec(memory_space=pltpu.SMEM), pl.BlockSpec(memory_space=pltpu.HBM)
+    return pl.pallas_call(
+        attend_kernel,
+        out_shape=(
+            jax.ShapeDtypeStruct((32, 4, width), jnp.bfloat16),
+            jax.ShapeDtypeStruct((2, row_count // 4, features), jnp.float32),
+        ),
+        in_specs=[smem, *vmem(5), hbm, hbm],
+        out_specs=tuple(vmem(2)),
+        scratch_shapes=[
+            pltpu.VMEM(key_cache.shape, key_cache.dtype),
+            pltpu.VMEM(value_cache.shape, value_cache.dtype),
+            pltpu.VMEM((rows * width // HEAD, HEAD), jnp.float32),
+            pltpu.VMEM((rows, width), jnp.float32),
+            pltpu.VMEM((row_count, features), jnp.float32),
+            pltpu.SemaphoreType.DMA((2, rows // 4)),
+        ],
+        compiler_params=pltpu.CompilerParams(vmem_limit_bytes=56 * 1024 * 1024),
+        cost_estimate=cost(12e-6),
+        name="attend",
+    )(lengths, queries, new_key, new_value, kept_own, kept_other, key_cache, value_cache)
+
+
+ACROSS = (((1,), (1,)), ((), ()))
+
+
+def after(value, other):
+    def kernel(value_ref, other_ref, out_ref):
+        pass
+
+    anywhere = pl.BlockSpec(memory_space=pl.ANY)
+    return pl.pallas_call(
+        kernel,
+        out_shape=jax.ShapeDtypeStruct(value.shape, value.dtype),
+        in_specs=[anywhere] * 2,
+        out_specs=anywhere,
+        input_output_aliases={0: 0},
+        compiler_params=pltpu.CompilerParams(vmem_limit_bytes=1024 * 1024),
+        name="after",
+    )(value, other)
+
+
+def project_near_kernel(taken, weight_own, weight_other, kept, out_ref, far_ref, rows):
+    y = lax.axis_index("y")
+    blocks, share = taken.shape[0] // 2, taken.shape[1]
+    for b in range(blocks):
+        rows[0, b * share : (b + 1) * share, :] = taken[y * blocks + b].astype(jnp.float32)
+        rows[1, b * share : (b + 1) * share, :] = taken[(1 - y) * blocks + b].astype(jnp.float32)
+    far_ref[...] = rows[1].astype(jnp.bfloat16)
+    near = rows[0].astype(jnp.bfloat16)
+    for at, weight in enumerate((weight_own, weight_other)):
+        out_ref[at] = kept[at] + lax.dot_general(near, weight[...], ACROSS, preferred_element_type=jnp.float32)
+
+
+def project_far_kernel(far, weight_own, weight_other, near, out_ref):
+    rows = far[...]
+    own = near[0] + lax.dot_general(rows, weight_own[...], ACROSS, preferred_element_type=jnp.float32)
+    other = near[1] + lax.dot_general(rows, weight_other[...], ACROSS, preferred_element_type=jnp.float32)
+    core = lax.axis_index("c")
+    first, second = jnp.where(core == 0, own, other), jnp.where(core == 0, other, own)
+    stream = jnp.concatenate([first, second], axis=1).astype(jnp.bfloat16)
+    half = stream.shape[0] // 2
+    out_ref[0] = stream[:half]
+    out_ref[1] = stream[half:]
+
+
+def project_near(taken, weight_own, weight_other, kept):
+    depth = taken.shape[2]
+    rows = kept.shape[1]
+    return pl.pallas_call(
+        project_near_kernel,
+        out_shape=(
+            jax.ShapeDtypeStruct(kept.shape, jnp.float32),
+            jax.ShapeDtypeStruct((rows, depth), taken.dtype),
+        ),
+        in_specs=vmem(4),
+        out_specs=tuple(vmem(2)),
+        scratch_shapes=[pltpu.VMEM((2, rows, depth), jnp.float32)],
+        compiler_params=pltpu.CompilerParams(vmem_limit_bytes=16 * 1024 * 1024),
+        cost_estimate=cost(2e-6),
+        name="project_near",
+    )(taken, weight_own, weight_other, kept)
+
+
+def project_far(far, weight_own, weight_other, near):
+    rows, width = near.shape[1:]
+    return pl.pallas_call(
+        project_far_kernel,
+        out_shape=jax.ShapeDtypeStruct((2, rows // 2, 2 * width), jnp.bfloat16),
+        in_specs=vmem(4),
+        out_specs=pl.BlockSpec(memory_space=pltpu.VMEM),
+        compiler_params=pltpu.CompilerParams(vmem_limit_bytes=16 * 1024 * 1024),
+        cost_estimate=cost(2e-6),
+        name="project_far",
+    )(far, weight_own, weight_other, near)
+
+
+def pre_activations(rows, weights):
+    block = rows[0].shape[1]
+    main = block // 256 * 256
+    rest = jnp.concatenate([row[:, main:] for row in rows], axis=1)
+    sums = []
+    for half in range(2):
+        total = None
+        for dz, row in enumerate(rows):
+            part = jnp.dot(row[:, :main], weights[half, dz, :main, :], preferred_element_type=jnp.float32)
+            total = part if total is None else total + part
+        ends = jnp.concatenate([weights[half, dz, main:, :] for dz in range(4)], axis=0)
+        sums.append(total + jnp.dot(rest, ends, preferred_element_type=jnp.float32))
+    return sums
+
+
+def encode_first_kernel(own, other, enc_own, enc_other, out_ref, later_ref, weights, arrived):
     z, x = lax.axis_index("z"), lax.axis_index("x")
-    pieces = ((g00, g10), (g01, g11))
-    block = g00.shape[2]
-    pre_own = jnp.zeros((2 * g00.shape[1], enc_own.shape[1]), jnp.float32)
-    pre_other = pre_own
-    for dx in range(2):
+    block = own.shape[3]
+    now, later = [], []
+    for half, enc in enumerate((enc_own, enc_other)):
         for dz in range(4):
-            start = pl.multiple_of(((z ^ dz) * 2 + (x ^ dx)) * block, block)
-            rows = jnp.concatenate([pieces[dx][0][dz], pieces[dx][1][dz]], axis=0)
-            pre_own += jnp.dot(rows, enc_own[pl.ds(start, block), :], preferred_element_type=jnp.float32)
-            pre_other += jnp.dot(rows, enc_other[pl.ds(start, block), :], preferred_element_type=jnp.float32)
-
-    def activate(pre, at):
-        pre = pre + bias[at : at + 1, :]
+            for dx, to, copies in ((0, weights, now), (1, later_ref, later)):
+                start = pl.multiple_of(((z ^ dz) * 2 + (x ^ dx)) * block, 64)
+                sem = arrived.at[dx, half * 4 + dz]
+                copies.append(pltpu.make_async_copy(enc.at[pl.ds(start, block)], to.at[half, dz], sem))
+    for copy in now + later:
+        copy.start()
+    for copy in now:
+        copy.wait()
+    rows = [jnp.concatenate([own[0, dz], own[1, dz], other[0, dz], other[1, dz]], axis=0) for dz in range(4)]
+    sums = pre_activations(rows, weights)
+    out_ref[0] = sums[0]
+    out_ref[1] = sums[1]
+    for copy in later:
+        copy.wait()
+
+
+def encode_second_kernel(
+    own, upper, lower, first, weights, bias, threshold, probe_own, probe_other, out_ref, ordered
+):
+    rows = [jnp.concatenate([own[0, dz], own[1, dz], upper[dz], lower[dz]], axis=0) for dz in range(4)]
+    sums = pre_activations(rows, weights)
+    partial = None
+    for at, probe in enumerate((probe_own, probe_other)):
+        pre = sums[at] + first[at] + bias[at : at + 1, :]
         ramped = jnp.clip((pre - threshold[at : at + 1, :]) / RAMP_WIDTH, 0.0, 1.0)
-        return (pre * ramped).astype(jnp.bfloat16)
-
-    partial = jnp.dot(activate(pre_own, 0), probe_own[...], preferred_element_type=jnp.float32)
-    partial += jnp.dot(activate(pre_other, 1), probe_other[...], preferred_element_type=jnp.float32)
+        active = (pre * ramped).astype(jnp.bfloat16)
+        probed = jnp.dot(active, probe[...], preferred_element_type=jnp.float32)
+        partial = probed if partial is None else partial + probed
     for half in range(2):
         for b in range(16):
             at = half * 64 + b * 4
@@ -75,21 +293,37 @@
     out_ref[...] = ordered[...].astype(jnp.bfloat16)
 
 
-def vmem(count):
-    return [pl.BlockSpec(memory_space=pltpu.VMEM)] * count
-
-
-def encode(gathered, enc, bias, threshold, probe):
+def encode_first(own, other, enc):
+    rows, block, latents = 4 * own.shape[2], own.shape[3], enc[0].shape[1]
+    weights = (2, 4, block, latents)
+    hbm = pl.BlockSpec(memory_space=pltpu.HBM)
+    return pl.pallas_call(
+        encode_first_kernel,
+        out_shape=(
+            jax.ShapeDtypeStruct((2, rows, latents), jnp.float32),
+            jax.ShapeDtypeStruct(weights, enc[0].dtype),
+        ),
+        in_specs=[*vmem(2), hbm, hbm],
+        out_specs=tuple(vmem(2)),
+        scratch_shapes=[pltpu.VMEM(weights, enc[0].dtype), pltpu.SemaphoreType.DMA((2, 8))],
+        compiler_params=pltpu.CompilerParams(vmem_limit_bytes=48 * 1024 * 1024),
+        cost_estimate=cost(2e-6),
+        name="encode_first",
+    )(own, other, *enc)
+
+
+def encode_second(own, upper, lower, first, weights, bias, threshold, probe):
     columns = probe[0].shape[1]
     return pl.pallas_call(
-        encode_kernel,
+        encode_second_kernel,
         out_shape=jax.ShapeDtypeStruct((16, 8, columns), jnp.bfloat16),
-        in_specs=vmem(10),
+        in_specs=vmem(9),
         out_specs=pl.BlockSpec(memory_space=pltpu.VMEM),
         scratch_shapes=[pltpu.VMEM((16, 8, columns), jnp.float32)],
-        compiler_params=pltpu.CompilerParams(vmem_limit_bytes=32 * 1024 * 1024),
-        name="encode",
-    )(*gathered, *enc, bias, threshold, *probe)
+        compiler_params=pltpu.CompilerParams(vmem_limit_bytes=24 * 1024 * 1024),
+        cost_estimate=cost(2e-6),
+        name="encode_second",
+    )(own, upper, lower, first, weights, bias, threshold, *probe)
 
 
 def finish_kernel(parts, probe_bias, head_weight, head_bias, scores_ref, logits_ref):
@@ -100,7 +334,13 @@
     scores_ref[...] = scores
     gated = scores / (1.0 + jnp.exp(-scores))
     logits_ref[...] = (
-        jnp.dot(gated, head_weight[...], precision=lax.Precision.HIGHEST, preferred_element_type=jnp.float32)
+        lax.dot_general(
+            gated,
+            head_weight[...],
+            (((1,), (1,)), ((), ())),
+            precision=lax.Precision.HIGHEST,
+            preferred_element_type=jnp.float32,
+        )
         + head_bias[...]
     )
 
@@ -115,8 +355,9 @@
         ),
         in_specs=vmem(4),
         out_specs=tuple(vmem(2)),
+        compiler_params=pltpu.CompilerParams(vmem_limit_bytes=8 * 1024 * 1024),
         name="finish",
-    )(parts, probe_bias.reshape(1, -1), head_weight, head_bias.reshape(1, -1))
+    )(parts, probe_bias.reshape(1, -1), head_weight.T, head_bias.reshape(1, -1))
 
 
 def chip_body(
@@ -136,43 +377,33 @@
     head_weight,
     head_bias,
 ):
-    y, c = lax.axis_index("y"), lax.axis_index("c")
-    width = out_proj.shape[1]
-    proj_y = xor(out_proj, 16)
+    proj = out_proj.T
+    proj_y = xor(proj, 16)
     enc_other = xor(enc_weight, 1)
-    proj_c = xor(out_proj, 1)
+    proj_c = xor(proj, 1)
     probe_other = xor(probe_weight, 1)
     levels = jnp.stack([enc_bias, threshold_code.astype(jnp.float32) / 16.0])
     levels_other = xor(levels, 1)
     bias = jnp.stack([levels[0], levels_other[0]])
     threshold = jnp.stack([levels[1], levels_other[1]])
-    kept = residual.reshape(16, 2, 2, 4, width)
-    kept_own = lax.dynamic_slice(kept, (0, c, y, 0, 0), (16, 1, 1, 4, width)).reshape(64, width)
-    kept_given = lax.dynamic_slice(kept, (0, 1 - c, y, 0, 0), (16, 1, 1, 4, width)).reshape(64, width)
-    kept_other = xor(kept_given, 1)
+    kept = residual.T
+    kept_other = xor(kept, 1)
+
+    sent, kept_rows = attend_shares(
+        queries, key_cache, value_cache, new_key, new_value, lengths, kept, kept_other
+    )
+    taken = lax.all_to_all(sent, ALL, 0, 0, tiled=True)
+    proj_y = after(proj_y, taken)
     proj_yc = xor(proj_y, 1)
-
-    attended = attend(queries, key_cache, value_cache, new_key, new_value, lengths)
-    half_width = attended.shape[1]
-    split = attended.reshape(2, 2, 4, half_width).transpose(1, 0, 2, 3)
-    sent = jnp.broadcast_to(split[:, None], (2, 8, 2, 4, half_width)).reshape(32, 4, half_width)
-    taken = lax.all_to_all(sent, ALL, 0, 0, tiled=True).reshape(2, 64, half_width)
-    mine = lax.dynamic_index_in_dim(taken, y, 0, keepdims=False)
-    theirs = lax.dynamic_index_in_dim(taken, 1 - y, 0, keepdims=False)
-
-    def project(kept_rows, near, far):
-        projected = jnp.dot(mine, near, preferred_element_type=jnp.float32)
-        projected = projected + jnp.dot(theirs, far, preferred_element_type=jnp.float32)
-        return (kept_rows.astype(jnp.float32) + projected).astype(jnp.bfloat16)
-
-    stream_own = project(kept_own, out_proj, proj_y)
-    stream_other = project(kept_other, proj_c, proj_yc)
-    stream = jnp.concatenate(
-        [jnp.where(c == 0, stream_own, stream_other), jnp.where(c == 0, stream_other, stream_own)], axis=1
-    )
-    along_z = jnp.stack([stream, xor(stream, 4), xor(stream, 8), xor(stream, 12)])
-    gathered = (along_z, xor(along_z, 2), xor(along_z, 16), xor(along_z, 18))
-    partial = encode(gathered, (enc_weight, enc_other), bias, threshold, (probe_weight, probe_other))
+    near, far = project_near(taken, proj, proj_c, kept_rows)
+    stream = project_far(far, proj_y, proj_yc, near)
+    along_z = jnp.stack([stream, xor(stream, 4), xor(stream, 8), xor(stream, 12)], axis=1)
+    over_y, over_x = xor(along_z, 16), xor(along_z, 2)
+    upper, lower = xor(over_x[0], 16), xor(over_y[1], 2)
+    first, weights = encode_first(along_z, over_y, (enc_weight, enc_other))
+    partial = encode_second(
+        over_x, upper, lower, first, weights, bias, threshold, (probe_weight, probe_other)
+    )
     parts = lax.all_to_all(partial, PLANE, 0, 0, tiled=True)
     return finish(parts, probe_bias, head_weight, head_bias)
 

time: 79.3 us -> 70.7 us (0.89)
  blocking collectives: 0 us -> 12.2 us
  matrix products: 11.2 us -> 0 us
  waiting for transfers between devices: 34.2 us -> 24.6 us
  Pallas kernels: 5.26 us -> 11.9 us
  starting transfers between devices: 22.3 us -> 18 us
  local copies, waits for them, and re-layouts: 3.83 us -> 2.72 us
  other arithmetic: 1.06 us -> 0.09 us
    all_to_all x0 -> x1, blocking collectives: none -> 12.2 us  [chip_body(): parts = lax.all_to_all(partial, PLANE, 0, 0, tiled=True)]
    dot_general x7 -> x0, matrix products: 11.2 us -> none  [the longest x1 3.48 us: attend(): jnp.einsum('rkgd,rlkd->rkgl', grouped, key_rows, preferred_element_type=j...]
    pallas_call x1 -> x6, Pallas kernels: 3.49 us -> 11.1 us  [the longest x1 6.1 us: attend_shares(): pl.pallas_call(attend_kernel, out_shape=(jax.ShapeDtypeStruct((32, 4, wid...]
    all_to_all x2 -> x1, waiting for transfers between devices: 15.7 us -> 8.77 us  [chip_body(): taken = lax.all_to_all(sent, ALL, 0, 0, tiled=True)]
    all_to_all x2 -> x1, starting transfers between devices: 9.89 us -> 5.83 us  [chip_body(): taken = lax.all_to_all(sent, ALL, 0, 0, tiled=True)]
    ppermute x13 -> x14, waiting for transfers between devices: 18.5 us -> 15.8 us  [xor(): return lax.ppermute(value, ALL, [(i, i ^ bits) for i in range(32)])]
    unnamed x20, local copies, waits for them, and re-layouts: 1.58 us -> 2.69 us
    pallas_call x1, Pallas kernels: 1.77 us -> 0.76 us  [finish(): pl.pallas_call(finish_kernel, out_shape=(jax.ShapeDtypeStruct((rows, colu...]
  transfers between devices with their start and end apart: 15 -> 15, of which waited for: 6 -> 7; matrix products, arithmetic and copies ran while one was open for 20% -> 0% of each run, Pallas kernels for 0% -> 15%
where the time goes in v2:
time: 70.7 us; the launch traced here: 70.3 us
  waiting for transfers between devices  24.6 us (35%)
  starting transfers between devices  18 us (25%)
  blocking collectives  12.2 us (17%)
  Pallas kernels  11.9 us (17%)
  local copies, waits for them, and re-layouts  2.72 us (4%)
  between operations  0.81 us (1%)
    ppermute x14, waiting for transfers between devices, xor(): return lax.ppermute(value, ALL, [(i, i ^ bits) for i in range(32)])  15.8 us
    all_to_all x1, blocking collectives, chip_body(): parts = lax.all_to_all(partial, PLANE, 0, 0, tiled=True)  12.2 us
    ppermute x14, starting transfers between devices, xor(): return lax.ppermute(value, ALL, [(i, i ^ bits) for i in range(32)])  12.2 us
    all_to_all x1, waiting for transfers between devices, chip_body(): taken = lax.all_to_all(sent, ALL, 0, 0, tiled=True)  8.77 us
    pallas_call x1, Pallas kernels, attend_shares(): pl.pallas_call(attend_kernel, out_shape=(jax.ShapeDtypeStruct((32, 4, wid...  6.1 us
    all_to_all x1, starting transfers between devices, chip_body(): taken = lax.all_to_all(sent, ALL, 0, 0, tiled=True)  5.83 us
    unnamed x20, local copies, waits for them, and re-layouts  2.69 us
    pallas_call x1, Pallas kernels, encode_first(): pl.pallas_call(encode_first_kernel, out_shape=(jax.ShapeDtypeStruct((2, r...  2.12 us
  transfers between devices with their start and end apart: 15, of which 7 were waited for; matrix products, arithmetic and copies ran while one was open for 0% of the time, Pallas kernels for 15%

profile of v2, /device:TPU:0, one launch (start us, length us, event | category | flops | bytes accessed | tf_op | source)
XLA Modules:
  0.0 70.3 jit_solution(3050656717834670404)
XLA Ops:
  0.6 0.5 collective-permute-start
  1.2 0.0 copy-start
  1.2 2.6 %collective-permute-start.2 = (bf16[288,1024]{1,0:T(8,128)(2,1)}, bf16[288,1024]{1,0:T(8,128)(2,1)S(1)}, u32[]{:S(2)}, u32[]{:S(2)}) collective-permute-start(bf16[288,1024]{1,0:T(8,128)(2,1)} %bitcast.15), channel_id=1, source_target_pairs={{0,16},{1,17},{2,18},{3,19},{4,20},{5,21},{6,22},{7,23},{8,24},{9,... | collective-permute-start | bytes 1769480 | tf_op jit(solution)/shard_map/ppermute | solution.py:46
  3.8 0.0 collective-permute-done.kept_other
  3.8 0.0 copy-start.7
  3.8 0.7 copy-done.7
  4.4 6.1 %attend.1 = (bf16[32,4,1024]{2,1,0:T(4,128)(2,1)}, f32[2,64,288]{2,1,0:T(8,128)}) custom-call(s32[16]{0:T(128)} %lengths.1, bf16[16,1024]{1,0:T(8,128)(2,1)} %queries.1, bf16[16,512]{1,0:T(8,128)(2,1)} %new_key.1, bf16[16,512]{1,0:T(8,128)(2,1)} %new_value.1, bf16[288,256]{1,0:T(8,128)(2,1)} %bitcast.23, bf16[288,256]{1,0:T(8,128)(2,1)} %copy-done.7, ...), custom_call_target="tpu_custom_call" | custom-call | bytes 44280000 | tf_op jit(solution)/shard_map/attend/pallas_call | solution.py:144
  10.5 5.8 %all-to-all-start = ((bf16[32,4,1024]{2,1,0:T(4,128)(2,1)}), bf16[32,4,1024]{2,1,0:T(4,128)(2,1)S(1)}, u32[]{:S(2)}, u32[]{:S(2)}) async-start(bf16[32,4,1024]{2,1,0:T(4,128)(2,1)} %get-tuple-element.8), calls=%async_computation | async-start | bytes 524288 | tf_op jit(solution)/shard_map/all_to_all | solution.py:395
  16.4 0.0 copy-done
  16.4 0.0 copy-start.9
  16.4 0.0 copy-start.8
  16.4 0.0 copy-start.3
  16.4 0.3 collective-permute-start.11
  16.7 0.3 collective-permute-start.1
  17.0 0.9 %collective-permute-done.2.value_ref = bf16[288,1024]{1,0:T(8,128)(2,1)S(1)} collective-permute-done((bf16[288,1024]{1,0:T(8,128)(2,1)}, bf16[288,1024]{1,0:T(8,128)(2,1)S(1)}, u32[]{:S(2)}, u32[]{:S(2)}) %collective-permute-start.2) | collective-permute-done | bytes 589856 | tf_op jit(solution)/shard_map/ppermute | solution.py:46
  17.9 8.8 %all-to-all-done.taken.other_ref = bf16[32,4,1024]{2,1,0:T(4,128)(2,1)S(1)} async-done(((bf16[32,4,1024]{2,1,0:T(4,128)(2,1)}), bf16[32,4,1024]{2,1,0:T(4,128)(2,1)S(1)}, u32[]{:S(2)}, u32[]{:S(2)}) %all-to-all-start) | async-done | bytes 262176 | tf_op jit(solution)/shard_map/all_to_all | solution.py:395
  26.6 0.3 collective-permute-start.3
  27.0 0.0 collective-permute-done.1.weight_other
  27.0 0.0 copy-start.1
  27.0 1.1 %copy-done.1 = bf16[1024,288]{0,1:T(8,128)(2,1)S(1)} copy-done((bf16[1024,288]{0,1:T(8,128)(2,1)S(1)}, bf16[1024,288]{0,1:T(8,128)(2,1)}, u32[]{:S(2)}) %copy-start.1) | copy-done | bytes 589848
  28.0 0.0 copy-start.2
  28.0 0.9 %copy-done.2 = f32[2,64,288]{2,1,0:T(8,128)S(1)} copy-done((f32[2,64,288]{2,1,0:T(8,128)S(1)}, f32[2,64,288]{2,1,0:T(8,128)}, u32[]{:S(2)}) %copy-start.2) | copy-done | bytes 147480
  29.0 1.6 %project_near.1 = (f32[2,64,288]{2,1,0:T(8,128)S(1)}, bf16[64,1024]{1,0:T(8,128)(2,1)S(1)}) custom-call(bf16[32,4,1024]{2,1,0:T(4,128)(2,1)S(1)} %all-to-all-done.taken.other_ref, bf16[288,1024]{1,0:T(8,128)(2,1)S(1)} %bitcast.17, bf16[288,1024]{1,0:T(8,128)(2,1)} %collective-permute-done.1.weight_other, f32[2,64,288]{2,1,0:T(8,128)S(1)} %copy-done.2), custom_call_target="tpu_custom_call" | custom-call | bytes 7380000 | tf_op jit(solution)/shard_map/project_near/pallas_call | solution.py:212
  30.6 0.0 collective-permute-done.3.weight_other
  30.6 0.6 project_far.1
  31.2 0.9 %collective-permute-start.4 = (bf16[2,32,576]{2,1,0:T(8,128)(2,1)S(1)}, bf16[2,32,576]{2,1,0:T(8,128)(2,1)S(1)}, u32[]{:S(2)}, u32[]{:S(2)}) collective-permute-start(bf16[2,32,576]{2,1,0:T(8,128)(2,1)S(1)} %project_far.1), channel_id=1, source_target_pairs={{0,4},{1,5},{2,6},{3,7},{4,0},{5,1},{6,2},{7,3},{8,12},{9,13},{10,... | collective-permute-start | bytes 221192 | tf_op jit(solution)/shard_map/ppermute | solution.py:46
  32.0 1.4 %collective-permute-start.5 = (bf16[2,32,576]{2,1,0:T(8,128)(2,1)S(1)}, bf16[2,32,576]{2,1,0:T(8,128)(2,1)S(1)}, u32[]{:S(2)}, u32[]{:S(2)}) collective-permute-start(bf16[2,32,576]{2,1,0:T(8,128)(2,1)S(1)} %project_far.1), channel_id=1, source_target_pairs={{0,8},{1,9},{2,10},{3,11},{4,12},{5,13},{6,14},{7,15},{8,0},{9,1},... | collective-permute-start | bytes 221192 | tf_op jit(solution)/shard_map/ppermute | solution.py:46
  33.5 2.1 %collective-permute-start.6 = (bf16[2,32,576]{2,1,0:T(8,128)(2,1)S(1)}, bf16[2,32,576]{2,1,0:T(8,128)(2,1)S(1)}, u32[]{:S(2)}, u32[]{:S(2)}) collective-permute-start(bf16[2,32,576]{2,1,0:T(8,128)(2,1)S(1)} %project_far.1), channel_id=1, source_target_pairs={{0,12},{1,13},{2,14},{3,15},{4,8},{5,9},{6,10},{7,11},{8,4},{9,5},... | collective-permute-start | bytes 221192 | tf_op jit(solution)/shard_map/ppermute | solution.py:46
  35.6 0.2 collective-permute-done.4
  35.8 5.8 %collective-permute-done.5 = bf16[2,32,576]{2,1,0:T(8,128)(2,1)S(1)} collective-permute-done((bf16[2,32,576]{2,1,0:T(8,128)(2,1)S(1)}, bf16[2,32,576]{2,1,0:T(8,128)(2,1)S(1)}, u32[]{:S(2)}, u32[]{:S(2)}) %collective-permute-start.5) | collective-permute-done | bytes 73760 | tf_op jit(solution)/shard_map/ppermute | solution.py:46
  41.5 0.0 collective-permute-done.6
  41.5 0.1 pad_maximum_fusion.own
  41.6 0.7 %collective-permute-start.9 = (bf16[2,4,32,576]{3,2,1,0:T(8,128)(2,1)S(1)}, bf16[2,4,32,576]{3,2,1,0:T(8,128)(2,1)S(1)}, u32[]{:S(2)}, u32[]{:S(2)}) collective-permute-start(bf16[2,4,32,576]{3,2,1,0:T(8,128)(2,1)S(1)} %pad_maximum_fusion.own), channel_id=1, source_target_pairs={{0,16},{1,17},{2,18},{3,19},{4,20},{5,21},{6,22},{7,23},{8,24},{9,... | collective-permute-start | bytes 884744 | tf_op jit(solution)/shard_map/ppermute | solution.py:46
  42.3 0.0 copy-done.9
  42.3 0.7 collective-permute-start.7
  43.0 0.0 copy-done.8
  43.0 0.1 collective-permute-start.12
  43.1 0.0 copy-done.3
  43.1 0.5 collective-permute-start.13
  43.6 6.8 %collective-permute-done.9.other = bf16[2,4,32,576]{3,2,1,0:T(8,128)(2,1)S(1)} collective-permute-done((bf16[2,4,32,576]{3,2,1,0:T(8,128)(2,1)S(1)}, bf16[2,4,32,576]{3,2,1,0:T(8,128)(2,1)S(1)}, u32[]{:S(2)}, u32[]{:S(2)}) %collective-permute-start.9) | collective-permute-done | bytes 294944 | tf_op jit(solution)/shard_map/ppermute | solution.py:46
  50.4 0.8 %collective-permute-start.10 = (bf16[4,32,576]{2,1,0:T(8,128)(2,1)S(1)}, bf16[4,32,576]{2,1,0:T(8,128)(2,1)S(1)}, u32[]{:S(2)}, u32[]{:S(2)}) collective-permute-start(bf16[4,32,576]{2,1,0:T(8,128)(2,1)S(1)} %slice_bitcast_fusion), channel_id=1, source_target_pairs={{0,2},{1,3},{2,0},{3,1},{4,6},{5,7},{6,4},{7,5},{8,10},{9,11},{10,... | collective-permute-start | bytes 442376 | tf_op jit(solution)/shard_map/ppermute | solution.py:46
  51.2 0.0 collective-permute-done.7.own
  51.2 1.0 %collective-permute-start.8 = (bf16[4,32,576]{2,1,0:T(8,128)(2,1)S(1)}, bf16[4,32,576]{2,1,0:T(8,128)(2,1)S(1)}, u32[]{:S(2)}, u32[]{:S(2)}) collective-permute-start(bf16[4,32,576]{2,1,0:T(8,128)(2,1)S(1)} %slice_bitcast_fusion.1), channel_id=1, source_target_pairs={{0,16},{1,17},{2,18},{3,19},{4,20},{5,21},{6,22},{7,23},{8,24},{9,... | collective-permute-start | bytes 442376 | tf_op jit(solution)/shard_map/ppermute | solution.py:46
  52.2 0.0 collective-permute-done.12
  52.2 0.0 collective-permute-done.11.enc_other
  52.3 2.1 %encode_first.1 = (f32[2,128,256]{2,1,0:T(8,128)S(1)}, bf16[2,4,576,256]{3,2,1,0:T(8,128)(2,1)S(1)}) custom-call(bf16[2,4,32,576]{3,2,1,0:T(8,128)(2,1)S(1)} %pad_maximum_fusion.own, bf16[2,4,32,576]{3,2,1,0:T(8,128)(2,1)S(1)} %collective-permute-done.9.other, bf16[4608,256]{1,0:T(8,128)(2,1)S(1)} %copy-done, bf16[4608,256]{1,0:T(8,128)(2,1)} %collective-permute-done.11.enc_other), custom_call_target="tpu_custom_call" | custom-call | bytes 7380000 | tf_op jit(solution)/shard_map/encode_first/pallas_call | solution.py:300
  54.4 0.0 copy-start.4
  54.4 0.0 copy-start.5
  54.4 0.0 copy-start.6
  54.4 0.0 collective-permute-done.13.probe_other
  54.4 1.4 %collective-permute-done.10.lower = bf16[4,32,576]{2,1,0:T(8,128)(2,1)S(1)} collective-permute-done((bf16[4,32,576]{2,1,0:T(8,128)(2,1)S(1)}, bf16[4,32,576]{2,1,0:T(8,128)(2,1)S(1)}, u32[]{:S(2)}, u32[]{:S(2)}) %collective-permute-start.10) | collective-permute-done | bytes 147488 | tf_op jit(solution)/shard_map/ppermute | solution.py:46
  55.8 0.8 %collective-permute-done.8.upper = bf16[4,32,576]{2,1,0:T(8,128)(2,1)S(1)} collective-permute-done((bf16[4,32,576]{2,1,0:T(8,128)(2,1)S(1)}, bf16[4,32,576]{2,1,0:T(8,128)(2,1)S(1)}, u32[]{:S(2)}, u32[]{:S(2)}) %collective-permute-start.8) | collective-permute-done | bytes 147488 | tf_op jit(solution)/shard_map/ppermute | solution.py:46
  56.6 0.7 %encode_second.1 = bf16[16,8,256]{2,1,0:T(8,128)(2,1)S(1)} custom-call(bf16[2,4,32,576]{3,2,1,0:T(8,128)(2,1)S(1)} %collective-permute-done.7.own, bf16[4,32,576]{2,1,0:T(8,128)(2,1)S(1)} %collective-permute-done.8.upper, bf16[4,32,576]{2,1,0:T(8,128)(2,1)S(1)} %collective-permute-done.10.lower, f32[2,128,256]{2,1,0:T(8,128)S(1)} %get-tuple-element.12.first, ...), custom_call_target="tpu_custom_call" | custom-call | bytes 7380000 | tf_op jit(solution)/shard_map/encode_second/pallas_call | solution.py:317
  57.3 12.2 %all_to_all.10.parts = bf16[16,8,256]{2,1,0:T(8,128)(2,1)S(1)} all-to-all(bf16[16,8,256]{2,1,0:T(8,128)(2,1)S(1)} %encode_second.1), channel_id=1, replica_groups=mesh['y'=2,'z'=4,'x'=2,'c'=2] {'y','z','x'}, dimensions={0} | all-to-all | bytes 131072 | tf_op jit(solution)/shard_map/all_to_all | solution.py:407
  69.5 0.0 copy-done.4
  69.5 0.0 copy-done.5
  69.6 0.0 copy-done.6
  69.6 0.8 %finish.1 = (f32[8,256]{1,0:T(8,128)}, f32[8,16]{1,0:T(8,128)}) custom-call(bf16[16,8,256]{2,1,0:T(8,128)(2,1)S(1)} %all_to_all.10.parts, f32[1,256]{1,0:T(1,128)S(1)} %bitcast.20, f32[16,256]{1,0:T(8,128)S(1)} %bitcast.19, f32[1,16]{1,0:T(1,128)S(1)} %bitcast.21), custom_call_target="tpu_custom_call" | custom-call | tf_op jit(solution)/shard_map/finish/pallas_call | solution.py:350
  (7 shorter events, 0.1 us)
Async XLA Ops:
  0.6 3.1 %collective-permute-start = (bf16[288,256]{1,0:T(8,128)(2,1)}, bf16[288,256]{1,0:T(8,128)(2,1)S(1)}, u32[]{:S(2)}, u32[]{:S(2)}) collective-permute-start(bf16[288,256]{1,0:T(8,128)(2,1)} %bitcast.22), channel_id=1, source_target_pairs={{0,1},{1,0},{2,3},{3,2},{4,5},{5,4},{6,7},{7,6},{8,9},{9,8},{10,11... | collective-permute-start | bytes 442376 | tf_op jit(solution)/shard_map/ppermute | solution.py:46
  1.2 15.2 %copy-start = (bf16[4608,256]{1,0:T(8,128)(2,1)S(1)}, bf16[4608,256]{1,0:T(8,128)(2,1)}, u32[]{:S(2)}) copy-start(bf16[4608,256]{1,0:T(8,128)(2,1)} %enc_own.1) | copy-start | bytes 7077892
  1.2 16.7 %collective-permute-start.2 = (bf16[288,1024]{1,0:T(8,128)(2,1)}, bf16[288,1024]{1,0:T(8,128)(2,1)S(1)}, u32[]{:S(2)}, u32[]{:S(2)}) collective-permute-start(bf16[288,1024]{1,0:T(8,128)(2,1)} %bitcast.15), channel_id=1, source_target_pairs={{0,16},{1,17},{2,18},{3,19},{4,20},{5,21},{6,22},{7,23},{8,24},{9,... | collective-permute-start | bytes 1769480 | tf_op jit(solution)/shard_map/ppermute | solution.py:46
  3.8 0.7 copy-start.7
  10.5 16.1 %all-to-all-start = ((bf16[32,4,1024]{2,1,0:T(4,128)(2,1)}), bf16[32,4,1024]{2,1,0:T(4,128)(2,1)S(1)}, u32[]{:S(2)}, u32[]{:S(2)}) async-start(bf16[32,4,1024]{2,1,0:T(4,128)(2,1)} %get-tuple-element.8), calls=%async_computation | async-start | bytes 524288 | tf_op jit(solution)/shard_map/all_to_all | solution.py:395
  16.4 26.0 %copy-start.9 = (s32[256]{0:T(256)S(1)}, s32[256]{0:T(256)}, u32[]{:S(2)}) copy-start(s32[256]{0:T(256)} %param.25) | copy-start | bytes 3076
  16.4 26.6 %copy-start.8 = (f32[256]{0:T(256)S(1)}, f32[256]{0:T(256)}, u32[]{:S(2)}) copy-start(f32[256]{0:T(256)} %param.24) | copy-start | bytes 3076
  16.4 26.7 %copy-start.3 = (bf16[256,256]{1,0:T(8,128)(2,1)S(1)}, bf16[256,256]{1,0:T(8,128)(2,1)}, u32[]{:S(2)}) copy-start(bf16[256,256]{1,0:T(8,128)(2,1)} %probe_own.1) | copy-start | bytes 393220
  16.4 35.9 %collective-permute-start.11 = (bf16[4608,256]{1,0:T(8,128)(2,1)S(1)}, bf16[4608,256]{1,0:T(8,128)(2,1)}, u32[]{:S(2)}, u32[]{:S(2)}) collective-permute-start(bf16[4608,256]{1,0:T(8,128)(2,1)S(1)} %copy-done), channel_id=1, source_target_pairs={{0,1},{1,0},{2,3},{3,2},{4,5},{5,4},{6,7},{7,6},{8,9},{9,8},{10,11... | collective-permute-start | bytes 7077896 | tf_op jit(solution)/shard_map/ppermute | solution.py:46
  16.7 10.2 %collective-permute-start.1 = (bf16[288,1024]{1,0:T(8,128)(2,1)}, bf16[288,1024]{1,0:T(8,128)(2,1)}, u32[]{:S(2)}, u32[]{:S(2)}) collective-permute-start(bf16[288,1024]{1,0:T(8,128)(2,1)} %bitcast.16), channel_id=1, source_target_pairs={{0,1},{1,0},{2,3},{3,2},{4,5},{5,4},{6,7},{7,6},{8,9},{9,8},{10,11... | collective-permute-start | bytes 1769480 | tf_op jit(solution)/shard_map/ppermute | solution.py:46
  26.6 3.9 %collective-permute-start.3 = (bf16[288,1024]{1,0:T(8,128)(2,1)S(1)}, bf16[288,1024]{1,0:T(8,128)(2,1)S(1)}, u32[]{:S(2)}, u32[]{:S(2)}) collective-permute-start(bf16[288,1024]{1,0:T(8,128)(2,1)S(1)} %after.1.weight_own), channel_id=1, source_target_pairs={{0,1},{1,0},{2,3},{3,2},{4,5},{5,4},{6,7},{7,6},{8,9},{9,8},{10,11... | collective-permute-start | bytes 1769480 | tf_op jit(solution)/shard_map/ppermute | solution.py:46
  27.0 1.1 %copy-start.1 = (bf16[1024,288]{0,1:T(8,128)(2,1)S(1)}, bf16[1024,288]{0,1:T(8,128)(2,1)}, u32[]{:S(2)}) copy-start(bf16[1024,288]{0,1:T(8,128)(2,1)} %param.21) | copy-start | bytes 1769476
  28.0 0.9 %copy-start.2 = (f32[2,64,288]{2,1,0:T(8,128)S(1)}, f32[2,64,288]{2,1,0:T(8,128)}, u32[]{:S(2)}) copy-start(f32[2,64,288]{2,1,0:T(8,128)} %get-tuple-element.9.kept) | copy-start | bytes 442372
  31.2 4.6 %collective-permute-start.4 = (bf16[2,32,576]{2,1,0:T(8,128)(2,1)S(1)}, bf16[2,32,576]{2,1,0:T(8,128)(2,1)S(1)}, u32[]{:S(2)}, u32[]{:S(2)}) collective-permute-start(bf16[2,32,576]{2,1,0:T(8,128)(2,1)S(1)} %project_far.1), channel_id=1, source_target_pairs={{0,4},{1,5},{2,6},{3,7},{4,0},{5,1},{6,2},{7,3},{8,12},{9,13},{10,... | collective-permute-start | bytes 221192 | tf_op jit(solution)/shard_map/ppermute | solution.py:46
  32.0 9.5 %collective-permute-start.5 = (bf16[2,32,576]{2,1,0:T(8,128)(2,1)S(1)}, bf16[2,32,576]{2,1,0:T(8,128)(2,1)S(1)}, u32[]{:S(2)}, u32[]{:S(2)}) collective-permute-start(bf16[2,32,576]{2,1,0:T(8,128)(2,1)S(1)} %project_far.1), channel_id=1, source_target_pairs={{0,8},{1,9},{2,10},{3,11},{4,12},{5,13},{6,14},{7,15},{8,0},{9,1},... | collective-permute-start | bytes 221192 | tf_op jit(solution)/shard_map/ppermute | solution.py:46
  33.5 8.1 %collective-permute-start.6 = (bf16[2,32,576]{2,1,0:T(8,128)(2,1)S(1)}, bf16[2,32,576]{2,1,0:T(8,128)(2,1)S(1)}, u32[]{:S(2)}, u32[]{:S(2)}) collective-permute-start(bf16[2,32,576]{2,1,0:T(8,128)(2,1)S(1)} %project_far.1), channel_id=1, source_target_pairs={{0,12},{1,13},{2,14},{3,15},{4,8},{5,9},{6,10},{7,11},{8,4},{9,5},... | collective-permute-start | bytes 221192 | tf_op jit(solution)/shard_map/ppermute | solution.py:46
  41.6 8.8 %collective-permute-start.9 = (bf16[2,4,32,576]{3,2,1,0:T(8,128)(2,1)S(1)}, bf16[2,4,32,576]{3,2,1,0:T(8,128)(2,1)S(1)}, u32[]{:S(2)}, u32[]{:S(2)}) collective-permute-start(bf16[2,4,32,576]{3,2,1,0:T(8,128)(2,1)S(1)} %pad_maximum_fusion.own), channel_id=1, source_target_pairs={{0,16},{1,17},{2,18},{3,19},{4,20},{5,21},{6,22},{7,23},{8,24},{9,... | collective-permute-start | bytes 884744 | tf_op jit(solution)/shard_map/ppermute | solution.py:46
  42.3 8.9 %collective-permute-start.7 = (bf16[2,4,32,576]{3,2,1,0:T(8,128)(2,1)S(1)}, bf16[2,4,32,576]{3,2,1,0:T(8,128)(2,1)S(1)}, u32[]{:S(2)}, u32[]{:S(2)}) collective-permute-start(bf16[2,4,32,576]{3,2,1,0:T(8,128)(2,1)S(1)} %pad_maximum_fusion.own), channel_id=1, source_target_pairs={{0,2},{1,3},{2,0},{3,1},{4,6},{5,7},{6,4},{7,5},{8,10},{9,11},{10,... | collective-permute-start | bytes 884744 | tf_op jit(solution)/shard_map/ppermute | solution.py:46
  43.0 9.2 %collective-permute-start.12 = (f32[2,256]{1,0:T(2,128)S(1)}, f32[2,256]{1,0:T(2,128)S(1)}, u32[]{:S(2)}, u32[]{:S(2)}) collective-permute-start(f32[2,256]{1,0:T(2,128)S(1)} %pad_maximum_fusion.1), channel_id=1, source_target_pairs={{0,1},{1,0},{2,3},{3,2},{4,5},{5,4},{6,7},{7,6},{8,9},{9,8},{10,11... | collective-permute-start | bytes 6152 | tf_op jit(solution)/shard_map/ppermute | solution.py:46
  43.1 11.3 %collective-permute-start.13 = (bf16[256,256]{1,0:T(8,128)(2,1)S(1)}, bf16[256,256]{1,0:T(8,128)(2,1)S(1)}, u32[]{:S(2)}, u32[]{:S(2)}) collective-permute-start(bf16[256,256]{1,0:T(8,128)(2,1)S(1)} %copy-done.3), channel_id=1, source_target_pairs={{0,1},{1,0},{2,3},{3,2},{4,5},{5,4},{6,7},{7,6},{8,9},{9,8},{10,11... | collective-permute-start | bytes 393224 | tf_op jit(solution)/shard_map/ppermute | solution.py:46
  50.4 5.4 %collective-permute-start.10 = (bf16[4,32,576]{2,1,0:T(8,128)(2,1)S(1)}, bf16[4,32,576]{2,1,0:T(8,128)(2,1)S(1)}, u32[]{:S(2)}, u32[]{:S(2)}) collective-permute-start(bf16[4,32,576]{2,1,0:T(8,128)(2,1)S(1)} %slice_bitcast_fusion), channel_id=1, source_target_pairs={{0,2},{1,3},{2,0},{3,1},{4,6},{5,7},{6,4},{7,5},{8,10},{9,11},{10,... | collective-permute-start | bytes 442376 | tf_op jit(solution)/shard_map/ppermute | solution.py:46
  51.2 5.4 %collective-permute-start.8 = (bf16[4,32,576]{2,1,0:T(8,128)(2,1)S(1)}, bf16[4,32,576]{2,1,0:T(8,128)(2,1)S(1)}, u32[]{:S(2)}, u32[]{:S(2)}) collective-permute-start(bf16[4,32,576]{2,1,0:T(8,128)(2,1)S(1)} %slice_bitcast_fusion.1), channel_id=1, source_target_pairs={{0,16},{1,17},{2,18},{3,19},{4,20},{5,21},{6,22},{7,23},{8,24},{9,... | collective-permute-start | bytes 442376 | tf_op jit(solution)/shard_map/ppermute | solution.py:46
  54.4 15.2 %copy-start.4 = (f32[256,16]{0,1:T(8,128)S(1)}, f32[256,16]{0,1:T(8,128)}, u32[]{:S(2)}) copy-start(f32[256,16]{0,1:T(8,128)} %param.28) | copy-start | bytes 49156
  54.4 15.1 %copy-start.5 = (f32[256]{0:T(256)S(1)}, f32[256]{0:T(256)}, u32[]{:S(2)}) copy-start(f32[256]{0:T(256)} %param.27) | copy-start | bytes 3076
  54.4 15.1 %copy-start.6 = (f32[16]{0:T(128)S(1)}, f32[16]{0:T(128)}, u32[]{:S(2)}) copy-start(f32[16]{0:T(128)} %param.29) | copy-start | bytes 196

commit v3 on v2

--- a/solution.py
+++ b/solution.py
@@ -59,17 +59,13 @@
     queries,
     new_key,
     new_value,
-    kept_own,
-    kept_other,
     keys_at,
     values_at,
     out_ref,
-    kept_ref,
     keys,
     values,
     heads,
     mixed,
-    turned,
     arrived,
 ):
     row_count, positions, kv_width = keys.shape
@@ -83,12 +79,6 @@
         copies.append(pltpu.make_async_copy(values_at.at[rows], values.at[rows], arrived.at[1, at]))
     for copy in copies:
         copy.start()
-    y, c = lax.axis_index("y"), lax.axis_index("c")
-    for at, kept in enumerate((kept_own, kept_other)):
-        turned[...] = kept[...].astype(jnp.float32).T
-        for b in range(turned.shape[0] // 16):
-            both = turned[pl.ds(pl.multiple_of(b * 16 + 8 * c, 8), 8), :]
-            kept_ref[at, 4 * b : 4 * b + 4, :] = jnp.where(y == 0, both[:4], both[4:])
     for head in range(head_count):
         heads[pl.ds(head, row_count, stride=head_count), :] = queries[:, head * HEAD : (head + 1) * HEAD].astype(
             jnp.float32
@@ -137,36 +127,59 @@
                 out_ref[to_y * 16 + zx * 2 + to_c] = share
 
 
-def attend_shares(queries, key_cache, value_cache, new_key, new_value, lengths, kept_own, kept_other):
+def attend_shares(queries, key_cache, value_cache, new_key, new_value, lengths):
     rows, width = queries.shape
-    features, row_count = kept_own.shape
     smem, hbm = pl.BlockSpec(memory_space=pltpu.SMEM), pl.BlockSpec(memory_space=pltpu.HBM)
     return pl.pallas_call(
         attend_kernel,
-        out_shape=(
-            jax.ShapeDtypeStruct((32, 4, width), jnp.bfloat16),
-            jax.ShapeDtypeStruct((2, row_count // 4, features), jnp.float32),
-        ),
-        in_specs=[smem, *vmem(5), hbm, hbm],
-        out_specs=tuple(vmem(2)),
+        out_shape=jax.ShapeDtypeStruct((32, 4, width), jnp.bfloat16),
+        in_specs=[smem, *vmem(3), hbm, hbm],
+        out_specs=pl.BlockSpec(memory_space=pltpu.VMEM),
         scratch_shapes=[
             pltpu.VMEM(key_cache.shape, key_cache.dtype),
             pltpu.VMEM(value_cache.shape, value_cache.dtype),
             pltpu.VMEM((rows * width // HEAD, HEAD), jnp.float32),
             pltpu.VMEM((rows, width), jnp.float32),
-            pltpu.VMEM((row_count, features), jnp.float32),
             pltpu.SemaphoreType.DMA((2, rows // 4)),
         ],
         compiler_params=pltpu.CompilerParams(vmem_limit_bytes=56 * 1024 * 1024),
         cost_estimate=cost(12e-6),
         name="attend",
-    )(lengths, queries, new_key, new_value, kept_own, kept_other, key_cache, value_cache)
+    )(lengths, queries, new_key, new_value, key_cache, value_cache)
 
 
 ACROSS = (((1,), (1,)), ((), ()))
 
 
-def after(value, other):
+def keep_kernel(kept_own, kept_other, *rest):
+    out_ref, token_ref, turned = rest[-3:]
+    token_ref[...] = jnp.zeros_like(token_ref)
+    y, c = lax.axis_index("y"), lax.axis_index("c")
+    for at, kept in enumerate((kept_own, kept_other)):
+        turned[...] = kept[...].astype(jnp.float32).T
+        for b in range(turned.shape[0] // 16):
+            both = turned[pl.ds(pl.multiple_of(b * 16 + 8 * c, 8), 8), :]
+            out_ref[at, 4 * b : 4 * b + 4, :] = jnp.where(y == 0, both[:4], both[4:])
+
+
+def keep(kept_own, kept_other, ready):
+    features, rows = kept_own.shape
+    return pl.pallas_call(
+        keep_kernel,
+        out_shape=(
+            jax.ShapeDtypeStruct((2, rows // 4, features), jnp.float32),
+            jax.ShapeDtypeStruct((8, 128), jnp.float32),
+        ),
+        in_specs=vmem(2) + [pl.BlockSpec(memory_space=pl.ANY)] * len(ready),
+        out_specs=tuple(vmem(2)),
+        scratch_shapes=[pltpu.VMEM((rows, features), jnp.float32)],
+        compiler_params=pltpu.CompilerParams(vmem_limit_bytes=4 * 1024 * 1024),
+        cost_estimate=cost(1e-6),
+        name="keep",
+    )(kept_own, kept_other, *ready)
+
+
+def after(value, other, limit=1024 * 1024):
     def kernel(value_ref, other_ref, out_ref):
         pass
 
@@ -177,7 +190,7 @@
         in_specs=[anywhere] * 2,
         out_specs=anywhere,
         input_output_aliases={0: 0},
-        compiler_params=pltpu.CompilerParams(vmem_limit_bytes=1024 * 1024),
+        compiler_params=pltpu.CompilerParams(vmem_limit_bytes=limit),
         name="after",
     )(value, other)
 
@@ -252,9 +265,10 @@
     return sums
 
 
-def encode_first_kernel(own, other, enc_own, enc_other, out_ref, later_ref, weights, arrived):
+def encode_first_kernel(own, other, own_far, other_far, enc_own, enc_other, out_ref, later_ref, weights, arrived):
     z, x = lax.axis_index("z"), lax.axis_index("x")
     block = own.shape[3]
+    pairs = ((own, other), (own_far, other_far))
     now, later = [], []
     for half, enc in enumerate((enc_own, enc_other)):
         for dz in range(4):
@@ -266,7 +280,11 @@
         copy.start()
     for copy in now:
         copy.wait()
-    rows = [jnp.concatenate([own[0, dz], own[1, dz], other[0, dz], other[1, dz]], axis=0) for dz in range(4)]
+    rows = [
+        jnp.concatenate([piece[half, dz] for piece in pair for half in range(2)], axis=0)
+        for pair in pairs
+        for dz in range(2)
+    ]
     sums = pre_activations(rows, weights)
     out_ref[0] = sums[0]
     out_ref[1] = sums[1]
@@ -275,14 +293,35 @@
 
 
 def encode_second_kernel(
-    own, upper, lower, first, weights, bias, threshold, probe_own, probe_other, out_ref, ordered
+    own,
+    upper,
+    lower,
+    own_far,
+    upper_far,
+    lower_far,
+    first,
+    weights,
+    bias_own,
+    code_own,
+    probe_own,
+    bias_other,
+    code_other,
+    probe_other,
+    out_ref,
+    ordered,
 ):
-    rows = [jnp.concatenate([own[0, dz], own[1, dz], upper[dz], lower[dz]], axis=0) for dz in range(4)]
+    rows = [
+        jnp.concatenate([piece[0, dz], piece[1, dz], up[dz], low[dz]], axis=0)
+        for piece, up, low in ((own, upper, lower), (own_far, upper_far, lower_far))
+        for dz in range(2)
+    ]
     sums = pre_activations(rows, weights)
     partial = None
-    for at, probe in enumerate((probe_own, probe_other)):
-        pre = sums[at] + first[at] + bias[at : at + 1, :]
-        ramped = jnp.clip((pre - threshold[at : at + 1, :]) / RAMP_WIDTH, 0.0, 1.0)
+    halves = ((bias_own, code_own, probe_own), (bias_other, code_other, probe_other))
+    for at, (bias, code, probe) in enumerate(halves):
+        pre = sums[at] + first[at] + bias[...]
+        threshold = code[...].astype(jnp.float32) / 16.0
+        ramped = jnp.clip((pre - threshold) / RAMP_WIDTH, 0.0, 1.0)
         active = (pre * ramped).astype(jnp.bfloat16)
         probed = jnp.dot(active, probe[...], preferred_element_type=jnp.float32)
         partial = probed if partial is None else partial + probed
@@ -293,7 +332,8 @@
     out_ref[...] = ordered[...].astype(jnp.bfloat16)
 
 
-def encode_first(own, other, enc):
+def encode_first(near, far, enc):
+    own = near[0]
     rows, block, latents = 4 * own.shape[2], own.shape[3], enc[0].shape[1]
     weights = (2, 4, block, latents)
     hbm = pl.BlockSpec(memory_space=pltpu.HBM)
@@ -303,27 +343,27 @@
             jax.ShapeDtypeStruct((2, rows, latents), jnp.float32),
             jax.ShapeDtypeStruct(weights, enc[0].dtype),
         ),
-        in_specs=[*vmem(2), hbm, hbm],
+        in_specs=[*vmem(4), hbm, hbm],
         out_specs=tuple(vmem(2)),
         scratch_shapes=[pltpu.VMEM(weights, enc[0].dtype), pltpu.SemaphoreType.DMA((2, 8))],
-        compiler_params=pltpu.CompilerParams(vmem_limit_bytes=48 * 1024 * 1024),
+        compiler_params=pltpu.CompilerParams(vmem_limit_bytes=50 * 1024 * 1024),
         cost_estimate=cost(2e-6),
         name="encode_first",
-    )(own, other, *enc)
-
-
-def encode_second(own, upper, lower, first, weights, bias, threshold, probe):
-    columns = probe[0].shape[1]
+    )(*near, *far, *enc)
+
+
+def encode_second(near, far, first, weights, own, other):
+    columns = own[2].shape[1]
     return pl.pallas_call(
         encode_second_kernel,
         out_shape=jax.ShapeDtypeStruct((16, 8, columns), jnp.bfloat16),
-        in_specs=vmem(9),
+        in_specs=vmem(14),
         out_specs=pl.BlockSpec(memory_space=pltpu.VMEM),
         scratch_shapes=[pltpu.VMEM((16, 8, columns), jnp.float32)],
         compiler_params=pltpu.CompilerParams(vmem_limit_bytes=24 * 1024 * 1024),
         cost_estimate=cost(2e-6),
         name="encode_second",
-    )(own, upper, lower, first, weights, bias, threshold, *probe)
+    )(*near, *far, first, weights, *own, *other)
 
 
 def finish_kernel(parts, probe_bias, head_weight, head_bias, scores_ref, logits_ref):
@@ -382,27 +422,34 @@
     enc_other = xor(enc_weight, 1)
     proj_c = xor(proj, 1)
     probe_other = xor(probe_weight, 1)
-    levels = jnp.stack([enc_bias, threshold_code.astype(jnp.float32) / 16.0])
-    levels_other = xor(levels, 1)
-    bias = jnp.stack([levels[0], levels_other[0]])
-    threshold = jnp.stack([levels[1], levels_other[1]])
+    bias_other, code_other = xor(enc_bias, 1), xor(threshold_code, 1)
     kept = residual.T
     kept_other = xor(kept, 1)
 
-    sent, kept_rows = attend_shares(
-        queries, key_cache, value_cache, new_key, new_value, lengths, kept, kept_other
-    )
+    sent = attend_shares(queries, key_cache, value_cache, new_key, new_value, lengths)
+    kept_rows, token = keep(kept, kept_other, (probe_other, bias_other, code_other))
+    sent = after(sent, token, 56 * 1024 * 1024)
     taken = lax.all_to_all(sent, ALL, 0, 0, tiled=True)
     proj_y = after(proj_y, taken)
     proj_yc = xor(proj_y, 1)
     near, far = project_near(taken, proj, proj_c, kept_rows)
     stream = project_far(far, proj_y, proj_yc, near)
-    along_z = jnp.stack([stream, xor(stream, 4), xor(stream, 8), xor(stream, 12)], axis=1)
-    over_y, over_x = xor(along_z, 16), xor(along_z, 2)
-    upper, lower = xor(over_x[0], 16), xor(over_y[1], 2)
-    first, weights = encode_first(along_z, over_y, (enc_weight, enc_other))
+    along_z = [stream, xor(stream, 4), xor(stream, 8), xor(stream, 12)]
+
+    def spread(mine):
+        over_y, over_x = xor(mine, 16), xor(mine, 2)
+        return (mine, over_y), (over_x, xor(over_x[0], 16), xor(over_y[1], 2))
+
+    first_near, second_near = spread(jnp.stack(along_z[:2], axis=1))
+    first_far, second_far = spread(after(jnp.stack(along_z[2:], axis=1), second_near[0]))
+    first, weights = encode_first(first_near, first_far, (enc_weight, enc_other))
     partial = encode_second(
-        over_x, upper, lower, first, weights, bias, threshold, (probe_weight, probe_other)
+        second_near,
+        second_far,
+        first,
+        weights,
+        (enc_bias[None], threshold_code[None], probe_weight),
+        (bias_other[None], code_other[None], probe_other),
     )
     parts = lax.all_to_all(partial, PLANE, 0, 0, tiled=True)
     return finish(parts, probe_bias, head_weight, head_bias)

time: 70.7 us -> 65.8 us (0.931)
  waiting for transfers between devices: 24.6 us -> 16.8 us
  starting transfers between devices: 18 us -> 24.2 us
  local copies, waits for them, and re-layouts: 2.72 us -> 0.66 us
  Pallas kernels: 11.9 us -> 11.1 us
    ppermute x14 -> x19, waiting for transfers between devices: 15.8 us -> 8.2 us  [xor(): return lax.ppermute(value, ALL, [(i, i ^ bits) for i in range(32)])]
    ppermute x14 -> x19, starting transfers between devices: 12.2 us -> 19.3 us  [xor(): return lax.ppermute(value, ALL, [(i, i ^ bits) for i in range(32)])]
    unnamed x20 -> x18, local copies, waits for them, and re-layouts: 2.69 us -> 0.63 us
    pallas_call x1, Pallas kernels: 1.6 us -> 0.55 us  [project_near(): pl.pallas_call(project_near_kernel, out_shape=(jax.ShapeDtypeStruct(kept....]
    all_to_all x1, starting transfers between devices: 5.83 us -> 4.89 us  [chip_body(): taken = lax.all_to_all(sent, ALL, 0, 0, tiled=True)]
    pallas_call x1 -> x2, Pallas kernels: 6.1 us -> 6.09 us  [the longest x1 5.82 us: attend_shares(): pl.pallas_call(attend_kernel, out_shape=jax.ShapeDtypeStruct((32, 4, widt...]
  transfers between devices with their start and end apart: 15 -> 20, of which waited for: 7 -> 7; matrix products, arithmetic and copies ran while one was open for 0% -> 0% of each run, Pallas kernels for 15% -> 15%
where the time goes in v3:
time: 65.8 us; the launch traced here: 65.4 us
  starting transfers between devices  24.2 us (37%)
  waiting for transfers between devices  16.8 us (26%)
  blocking collectives  11.6 us (18%)
  Pallas kernels  11.1 us (17%)
  between operations  0.88 us (1%)
  local copies, waits for them, and re-layouts  0.66 us (1%)
    ppermute x19, starting transfers between devices, xor(): return lax.ppermute(value, ALL, [(i, i ^ bits) for i in range(32)])  19.3 us
    all_to_all x1, blocking collectives, chip_body(): parts = lax.all_to_all(partial, PLANE, 0, 0, tiled=True)  11.6 us
    all_to_all x1, waiting for transfers between devices, chip_body(): taken = lax.all_to_all(sent, ALL, 0, 0, tiled=True)  8.65 us
    ppermute x19, waiting for transfers between devices, xor(): return lax.ppermute(value, ALL, [(i, i ^ bits) for i in range(32)])  8.2 us
    pallas_call x1, Pallas kernels, attend_shares(): pl.pallas_call(attend_kernel, out_shape=jax.ShapeDtypeStruct((32, 4, widt...  5.82 us
    all_to_all x1, starting transfers between devices, chip_body(): taken = lax.all_to_all(sent, ALL, 0, 0, tiled=True)  4.89 us
    pallas_call x1, Pallas kernels, encode_first(): pl.pallas_call(encode_first_kernel, out_shape=(jax.ShapeDtypeStruct((2, r...  2.43 us
  transfers between devices with their start and end apart: 20, of which 7 were waited for; matrix products, arithmetic and copies ran while one was open for 0% of the time, Pallas kernels for 15%

profile of v3, /device:TPU:0, one launch (start us, length us, event | category | flops | bytes accessed | tf_op | source)
XLA Modules:
  0.0 65.4 jit_solution(4143056309217345962)
XLA Ops:
  0.6 0.5 collective-permute-start
  1.2 0.1 collective-permute-start.1
  1.2 2.9 %collective-permute-start.5 = (bf16[288,1024]{1,0:T(8,128)(2,1)}, bf16[288,1024]{1,0:T(8,128)(2,1)S(1)}, u32[]{:S(2)}, u32[]{:S(2)}) collective-permute-start(bf16[288,1024]{1,0:T(8,128)(2,1)} %bitcast.21), channel_id=1, source_target_pairs={{0,16},{1,17},{2,18},{3,19},{4,20},{5,21},{6,22},{7,23},{8,24},{9,... | collective-permute-start | bytes 1769480 | tf_op jit(solution)/shard_map/ppermute | solution.py:46
  4.2 0.0 collective-permute-start.2
  4.2 0.5 collective-permute-start.3
  4.7 5.8 %attend.1.value_ref = bf16[32,4,1024]{2,1,0:T(4,128)(2,1)} custom-call(s32[16]{0:T(128)} %lengths.1, bf16[16,1024]{1,0:T(8,128)(2,1)} %queries.1, bf16[16,512]{1,0:T(8,128)(2,1)} %new_key.1, bf16[16,512]{1,0:T(8,128)(2,1)} %new_value.1, bf16[16,256,512]{2,1,0:T(8,128)(2,1)} %keys_at.1, bf16[16,256,512]{2,1,0:T(8,128)(2,1)} %values_at.1), custom_call_target="tpu_custom_call" | custom-call | bytes 44280000 | tf_op jit(solution)/shard_map/attend/pallas_call | solution.py:133
  10.5 0.0 collective-permute-done.2.rest_1_
  10.5 0.0 collective-permute-done.3.rest_2_
  10.5 0.0 collective-permute-done.1.rest_0_.probe_other
  10.6 0.0 collective-permute-done.kept_other
  10.6 0.0 copy-done.1
  10.6 0.3 keep.1
  10.8 0.0 copy-start.4
  10.9 0.6 copy-done.4
  11.4 4.9 %all-to-all-start = ((bf16[32,4,1024]{2,1,0:T(4,128)(2,1)}), bf16[32,4,1024]{2,1,0:T(4,128)(2,1)S(1)}, u32[]{:S(2)}, u32[]{:S(2)}) async-start(bf16[32,4,1024]{2,1,0:T(4,128)(2,1)} %after.3), calls=%async_computation | async-start | bytes 524288 | tf_op jit(solution)/shard_map/all_to_all | solution.py:432
  16.3 0.3 collective-permute-start.18
  16.7 0.0 copy-done
  16.7 0.3 collective-permute-start.4
  16.9 1.1 %collective-permute-done.5.value_ref = bf16[288,1024]{1,0:T(8,128)(2,1)S(1)} collective-permute-done((bf16[288,1024]{1,0:T(8,128)(2,1)}, bf16[288,1024]{1,0:T(8,128)(2,1)S(1)}, u32[]{:S(2)}, u32[]{:S(2)}) %collective-permute-start.5) | collective-permute-done | bytes 589856 | tf_op jit(solution)/shard_map/ppermute | solution.py:46
  18.0 8.6 %all-to-all-done.taken.other_ref = bf16[32,4,1024]{2,1,0:T(4,128)(2,1)S(1)} async-done(((bf16[32,4,1024]{2,1,0:T(4,128)(2,1)}), bf16[32,4,1024]{2,1,0:T(4,128)(2,1)S(1)}, u32[]{:S(2)}, u32[]{:S(2)}) %all-to-all-start) | async-done | bytes 262176 | tf_op jit(solution)/shard_map/all_to_all | solution.py:432
  26.6 0.3 collective-permute-start.6
  26.9 0.0 collective-permute-done.4.weight_other
  26.9 0.5 project_near.1
  27.5 1.1 %collective-permute-done.6.weight_other = bf16[288,1024]{1,0:T(8,128)(2,1)S(1)} collective-permute-done((bf16[288,1024]{1,0:T(8,128)(2,1)S(1)}, bf16[288,1024]{1,0:T(8,128)(2,1)S(1)}, u32[]{:S(2)}, u32[]{:S(2)}) %collective-permute-start.6) | collective-permute-done | bytes 589856 | tf_op jit(solution)/shard_map/ppermute | solution.py:46
  28.6 0.6 project_far.1
  29.2 1.2 %collective-permute-start.7 = (bf16[2,32,576]{2,1,0:T(8,128)(2,1)S(1)}, bf16[2,32,576]{2,1,0:T(8,128)(2,1)S(1)}, u32[]{:S(2)}, u32[]{:S(2)}) collective-permute-start(bf16[2,32,576]{2,1,0:T(8,128)(2,1)S(1)} %project_far.1), channel_id=1, source_target_pairs={{0,4},{1,5},{2,6},{3,7},{4,0},{5,1},{6,2},{7,3},{8,12},{9,13},{10,... | collective-permute-start | bytes 221192 | tf_op jit(solution)/shard_map/ppermute | solution.py:46
  30.4 1.4 %collective-permute-start.12 = (bf16[2,32,576]{2,1,0:T(8,128)(2,1)S(1)}, bf16[2,32,576]{2,1,0:T(8,128)(2,1)S(1)}, u32[]{:S(2)}, u32[]{:S(2)}) collective-permute-start(bf16[2,32,576]{2,1,0:T(8,128)(2,1)S(1)} %project_far.1), channel_id=1, source_target_pairs={{0,8},{1,9},{2,10},{3,11},{4,12},{5,13},{6,14},{7,15},{8,0},{9,1},... | collective-permute-start | bytes 221192 | tf_op jit(solution)/shard_map/ppermute | solution.py:46
  31.8 1.8 %collective-permute-start.13 = (bf16[2,32,576]{2,1,0:T(8,128)(2,1)S(1)}, bf16[2,32,576]{2,1,0:T(8,128)(2,1)S(1)}, u32[]{:S(2)}, u32[]{:S(2)}) collective-permute-start(bf16[2,32,576]{2,1,0:T(8,128)(2,1)S(1)} %project_far.1), channel_id=1, source_target_pairs={{0,12},{1,13},{2,14},{3,15},{4,8},{5,9},{6,10},{7,11},{8,4},{9,5},... | collective-permute-start | bytes 221192 | tf_op jit(solution)/shard_map/ppermute | solution.py:46
  33.7 0.9 %collective-permute-done.7 = bf16[2,32,576]{2,1,0:T(8,128)(2,1)S(1)} collective-permute-done((bf16[2,32,576]{2,1,0:T(8,128)(2,1)S(1)}, bf16[2,32,576]{2,1,0:T(8,128)(2,1)S(1)}, u32[]{:S(2)}, u32[]{:S(2)}) %collective-permute-start.7) | collective-permute-done | bytes 73760 | tf_op jit(solution)/shard_map/ppermute | solution.py:46
  34.6 1.8 %collective-permute-start.8 = (bf16[2,2,32,576]{3,2,1,0:T(8,128)(2,1)S(1)}, bf16[2,2,32,576]{3,2,1,0:T(8,128)(2,1)S(1)}, u32[]{:S(2)}, u32[]{:S(2)}) collective-permute-start(bf16[2,2,32,576]{3,2,1,0:T(8,128)(2,1)S(1)} %pad_maximum_fusion.own), channel_id=1, source_target_pairs={{0,2},{1,3},{2,0},{3,1},{4,6},{5,7},{6,4},{7,5},{8,10},{9,11},{10,... | collective-permute-start | bytes 442376 | tf_op jit(solution)/shard_map/ppermute | solution.py:46
  36.4 0.5 collective-permute-start.10
  37.0 2.7 %collective-permute-done.12 = bf16[2,32,576]{2,1,0:T(8,128)(2,1)S(1)} collective-permute-done((bf16[2,32,576]{2,1,0:T(8,128)(2,1)S(1)}, bf16[2,32,576]{2,1,0:T(8,128)(2,1)S(1)}, u32[]{:S(2)}, u32[]{:S(2)}) %collective-permute-start.12) | collective-permute-done | bytes 73760 | tf_op jit(solution)/shard_map/ppermute | solution.py:46
  39.6 0.0 collective-permute-done.13
  39.7 0.3 collective-permute-done.8.other_ref.own
  40.0 0.5 collective-permute-start.16
  40.5 1.8 %collective-permute-start.14 = (bf16[2,2,32,576]{3,2,1,0:T(8,128)(2,1)S(1)}, bf16[2,2,32,576]{3,2,1,0:T(8,128)(2,1)S(1)}, u32[]{:S(2)}, u32[]{:S(2)}) collective-permute-start(bf16[2,2,32,576]{3,2,1,0:T(8,128)(2,1)S(1)} %after.5.own_far), channel_id=1, source_target_pairs={{0,2},{1,3},{2,0},{3,1},{4,6},{5,7},{6,4},{7,5},{8,10},{9,11},{10,... | collective-permute-start | bytes 442376 | tf_op jit(solution)/shard_map/ppermute | solution.py:46
  42.3 0.0 collective-permute-done.10.other
  42.3 0.3 collective-permute-start.11
  42.6 1.6 %collective-permute-start.9 = (bf16[2,32,576]{2,1,0:T(8,128)(2,1)S(1)}, bf16[2,32,576]{2,1,0:T(8,128)(2,1)S(1)}, u32[]{:S(2)}, u32[]{:S(2)}) collective-permute-start(bf16[2,32,576]{2,1,0:T(8,128)(2,1)S(1)} %slice_bitcast_fusion.3), channel_id=1, source_target_pairs={{0,16},{1,17},{2,18},{3,19},{4,20},{5,21},{6,22},{7,23},{8,24},{9,... | collective-permute-start | bytes 221192 | tf_op jit(solution)/shard_map/ppermute | solution.py:46
  44.2 2.1 %collective-permute-done.14.own_far = bf16[2,2,32,576]{3,2,1,0:T(8,128)(2,1)S(1)} collective-permute-done((bf16[2,2,32,576]{3,2,1,0:T(8,128)(2,1)S(1)}, bf16[2,2,32,576]{3,2,1,0:T(8,128)(2,1)S(1)}, u32[]{:S(2)}, u32[]{:S(2)}) %collective-permute-start.14) | collective-permute-done | bytes 147488 | tf_op jit(solution)/shard_map/ppermute | solution.py:46
  46.3 1.2 %collective-permute-start.15 = (bf16[2,32,576]{2,1,0:T(8,128)(2,1)S(1)}, bf16[2,32,576]{2,1,0:T(8,128)(2,1)S(1)}, u32[]{:S(2)}, u32[]{:S(2)}) collective-permute-start(bf16[2,32,576]{2,1,0:T(8,128)(2,1)S(1)} %slice_bitcast_fusion.1), channel_id=1, source_target_pairs={{0,16},{1,17},{2,18},{3,19},{4,20},{5,21},{6,22},{7,23},{8,24},{9,... | collective-permute-start | bytes 221192 | tf_op jit(solution)/shard_map/ppermute | solution.py:46
  47.5 0.0 collective-permute-done.16.other_far
  47.5 0.0 copy-start.2
  47.5 0.0 copy-start.5
  47.5 0.0 copy-start.6
  47.5 2.2 %collective-permute-start.17 = (bf16[2,32,576]{2,1,0:T(8,128)(2,1)S(1)}, bf16[2,32,576]{2,1,0:T(8,128)(2,1)S(1)}, u32[]{:S(2)}, u32[]{:S(2)}) collective-permute-start(bf16[2,32,576]{2,1,0:T(8,128)(2,1)S(1)} %slice_bitcast_fusion), channel_id=1, source_target_pairs={{0,2},{1,3},{2,0},{3,1},{4,6},{5,7},{6,4},{7,5},{8,10},{9,11},{10,... | collective-permute-start | bytes 221192 | tf_op jit(solution)/shard_map/ppermute | solution.py:46
  49.7 0.0 collective-permute-done.18.enc_other
  49.7 2.4 %encode_first.1 = (f32[2,128,256]{2,1,0:T(8,128)S(1)}, bf16[2,4,576,256]{3,2,1,0:T(8,128)(2,1)S(1)}) custom-call(bf16[2,2,32,576]{3,2,1,0:T(8,128)(2,1)S(1)} %pad_maximum_fusion.own, bf16[2,2,32,576]{3,2,1,0:T(8,128)(2,1)S(1)} %collective-permute-done.10.other, bf16[2,2,32,576]{3,2,1,0:T(8,128)(2,1)S(1)} %after.5.own_far, ...), custom_call_target="tpu_custom_call" | custom-call | bytes 7380000 | tf_op jit(solution)/shard_map/encode_first/pallas_call | solution.py:340
  52.2 0.0 copy-start.3
  52.2 0.0 copy-start.7
  52.2 0.0 copy-start.8
  52.2 0.0 collective-permute-done.11.lower
  52.2 0.0 collective-permute-done.9.upper
  52.2 0.0 collective-permute-done.15.upper_far
  52.3 0.0 collective-permute-done.17.lower_far
  52.3 0.0 copy-done.2
  52.3 0.0 copy-done.5
  52.3 0.0 copy-done.6
  52.3 0.7 %encode_second.1 = bf16[16,8,256]{2,1,0:T(8,128)(2,1)S(1)} custom-call(bf16[2,2,32,576]{3,2,1,0:T(8,128)(2,1)S(1)} %collective-permute-done.8.other_ref.own, bf16[2,32,576]{2,1,0:T(8,128)(2,1)S(1)} %collective-permute-done.9.upper, bf16[2,32,576]{2,1,0:T(8,128)(2,1)S(1)} %collective-permute-done.11.lower, ...), custom_call_target="tpu_custom_call" | custom-call | bytes 7380000 | tf_op jit(solution)/shard_map/encode_second/pallas_call | solution.py:357
  53.0 11.6 %all_to_all.10.parts = bf16[16,8,256]{2,1,0:T(8,128)(2,1)S(1)} all-to-all(bf16[16,8,256]{2,1,0:T(8,128)(2,1)S(1)} %encode_second.1), channel_id=1, replica_groups=mesh['y'=2,'z'=4,'x'=2,'c'=2] {'y','z','x'}, dimensions={0} | all-to-all | bytes 131072 | tf_op jit(solution)/shard_map/all_to_all | solution.py:454
  64.7 0.0 copy-done.3
  64.7 0.0 copy-done.7
  64.7 0.0 copy-done.8
  64.7 0.8 %finish.1 = (f32[8,256]{1,0:T(8,128)}, f32[8,16]{1,0:T(8,128)}) custom-call(bf16[16,8,256]{2,1,0:T(8,128)(2,1)S(1)} %all_to_all.10.parts, f32[1,256]{1,0:T(1,128)S(1)} %bitcast.32, f32[16,256]{1,0:T(8,128)S(1)} %bitcast.27, f32[1,16]{1,0:T(1,128)S(1)} %bitcast.33), custom_call_target="tpu_custom_call" | custom-call | tf_op jit(solution)/shard_map/finish/pallas_call | solution.py:390
  (11 shorter events, 0.1 us)
Async XLA Ops:
  0.6 9.9 %collective-permute-start = (bf16[288,256]{1,0:T(8,128)(2,1)}, bf16[288,256]{1,0:T(8,128)(2,1)S(1)}, u32[]{:S(2)}, u32[]{:S(2)}) collective-permute-start(bf16[288,256]{1,0:T(8,128)(2,1)} %bitcast.25), channel_id=1, source_target_pairs={{0,1},{1,0},{2,3},{3,2},{4,5},{5,4},{6,7},{7,6},{8,9},{9,8},{10,11... | collective-permute-start | bytes 442376 | tf_op jit(solution)/shard_map/ppermute | solution.py:46
  1.2 9.4 %collective-permute-start.1 = (bf16[256,256]{1,0:T(8,128)(2,1)}, bf16[256,256]{1,0:T(8,128)(2,1)S(1)}, u32[]{:S(2)}, u32[]{:S(2)}) collective-permute-start(bf16[256,256]{1,0:T(8,128)(2,1)} %probe_own.1), channel_id=1, source_target_pairs={{0,1},{1,0},{2,3},{3,2},{4,5},{5,4},{6,7},{7,6},{8,9},{9,8},{10,11... | collective-permute-start | bytes 393224 | tf_op jit(solution)/shard_map/ppermute | solution.py:46
  1.2 9.3 %copy-start.1 = (bf16[256,288]{0,1:T(8,128)(2,1)S(1)}, bf16[256,288]{0,1:T(8,128)(2,1)}, u32[]{:S(2)}) copy-start(bf16[256,288]{0,1:T(8,128)(2,1)} %param.22) | copy-start | bytes 442372
  1.2 15.4 %copy-start = (bf16[1024,288]{0,1:T(8,128)(2,1)S(1)}, bf16[1024,288]{0,1:T(8,128)(2,1)}, u32[]{:S(2)}) copy-start(bf16[1024,288]{0,1:T(8,128)(2,1)} %param.21) | copy-start | bytes 1769476
  1.2 16.8 %collective-permute-start.5 = (bf16[288,1024]{1,0:T(8,128)(2,1)}, bf16[288,1024]{1,0:T(8,128)(2,1)S(1)}, u32[]{:S(2)}, u32[]{:S(2)}) collective-permute-start(bf16[288,1024]{1,0:T(8,128)(2,1)} %bitcast.21), channel_id=1, source_target_pairs={{0,16},{1,17},{2,18},{3,19},{4,20},{5,21},{6,22},{7,23},{8,24},{9,... | collective-permute-start | bytes 1769480 | tf_op jit(solution)/shard_map/ppermute | solution.py:46
  4.2 6.3 %collective-permute-start.2 = (f32[256]{0:T(256)}, f32[256]{0:T(256)S(1)}, u32[]{:S(2)}, u32[]{:S(2)}) collective-permute-start(f32[256]{0:T(256)} %param.24), channel_id=1, source_target_pairs={{0,1},{1,0},{2,3},{3,2},{4,5},{5,4},{6,7},{7,6},{8,9},{9,8},{10,11... | collective-permute-start | bytes 3080 | tf_op jit(solution)/shard_map/ppermute | solution.py:46
  4.2 6.3 %collective-permute-start.3 = (s32[256]{0:T(256)}, s32[256]{0:T(256)S(1)}, u32[]{:S(2)}, u32[]{:S(2)}) collective-permute-start(s32[256]{0:T(256)} %param.25), channel_id=1, source_target_pairs={{0,1},{1,0},{2,3},{3,2},{4,5},{5,4},{6,7},{7,6},{8,9},{9,8},{10,11... | collective-permute-start | bytes 3080 | tf_op jit(solution)/shard_map/ppermute | solution.py:46
  10.8 0.6 copy-start.4
  11.4 15.2 %all-to-all-start = ((bf16[32,4,1024]{2,1,0:T(4,128)(2,1)}), bf16[32,4,1024]{2,1,0:T(4,128)(2,1)S(1)}, u32[]{:S(2)}, u32[]{:S(2)}) async-start(bf16[32,4,1024]{2,1,0:T(4,128)(2,1)} %after.3), calls=%async_computation | async-start | bytes 524288 | tf_op jit(solution)/shard_map/all_to_all | solution.py:432
  16.3 33.4 %collective-permute-start.18 = (bf16[4608,256]{1,0:T(8,128)(2,1)}, bf16[4608,256]{1,0:T(8,128)(2,1)}, u32[]{:S(2)}, u32[]{:S(2)}) collective-permute-start(bf16[4608,256]{1,0:T(8,128)(2,1)} %enc_own.1), channel_id=1, source_target_pairs={{0,1},{1,0},{2,3},{3,2},{4,5},{5,4},{6,7},{7,6},{8,9},{9,8},{10,11... | collective-permute-start | bytes 7077896 | tf_op jit(solution)/shard_map/ppermute | solution.py:46
  16.7 10.3 %collective-permute-start.4 = (bf16[288,1024]{1,0:T(8,128)(2,1)S(1)}, bf16[288,1024]{1,0:T(8,128)(2,1)S(1)}, u32[]{:S(2)}, u32[]{:S(2)}) collective-permute-start(bf16[288,1024]{1,0:T(8,128)(2,1)S(1)} %bitcast.22), channel_id=1, source_target_pairs={{0,1},{1,0},{2,3},{3,2},{4,5},{5,4},{6,7},{7,6},{8,9},{9,8},{10,11... | collective-permute-start | bytes 1769480 | tf_op jit(solution)/shard_map/ppermute | solution.py:46
  26.6 2.0 %collective-permute-start.6 = (bf16[288,1024]{1,0:T(8,128)(2,1)S(1)}, bf16[288,1024]{1,0:T(8,128)(2,1)S(1)}, u32[]{:S(2)}, u32[]{:S(2)}) collective-permute-start(bf16[288,1024]{1,0:T(8,128)(2,1)S(1)} %after.4.weight_own), channel_id=1, source_target_pairs={{0,1},{1,0},{2,3},{3,2},{4,5},{5,4},{6,7},{7,6},{8,9},{9,8},{10,11... | collective-permute-start | bytes 1769480 | tf_op jit(solution)/shard_map/ppermute | solution.py:46
  29.2 5.3 %collective-permute-start.7 = (bf16[2,32,576]{2,1,0:T(8,128)(2,1)S(1)}, bf16[2,32,576]{2,1,0:T(8,128)(2,1)S(1)}, u32[]{:S(2)}, u32[]{:S(2)}) collective-permute-start(bf16[2,32,576]{2,1,0:T(8,128)(2,1)S(1)} %project_far.1), channel_id=1, source_target_pairs={{0,4},{1,5},{2,6},{3,7},{4,0},{5,1},{6,2},{7,3},{8,12},{9,13},{10,... | collective-permute-start | bytes 221192 | tf_op jit(solution)/shard_map/ppermute | solution.py:46
  30.4 9.2 %collective-permute-start.12 = (bf16[2,32,576]{2,1,0:T(8,128)(2,1)S(1)}, bf16[2,32,576]{2,1,0:T(8,128)(2,1)S(1)}, u32[]{:S(2)}, u32[]{:S(2)}) collective-permute-start(bf16[2,32,576]{2,1,0:T(8,128)(2,1)S(1)} %project_far.1), channel_id=1, source_target_pairs={{0,8},{1,9},{2,10},{3,11},{4,12},{5,13},{6,14},{7,15},{8,0},{9,1},... | collective-permute-start | bytes 221192 | tf_op jit(solution)/shard_map/ppermute | solution.py:46
  31.8 7.8 %collective-permute-start.13 = (bf16[2,32,576]{2,1,0:T(8,128)(2,1)S(1)}, bf16[2,32,576]{2,1,0:T(8,128)(2,1)S(1)}, u32[]{:S(2)}, u32[]{:S(2)}) collective-permute-start(bf16[2,32,576]{2,1,0:T(8,128)(2,1)S(1)} %project_far.1), channel_id=1, source_target_pairs={{0,12},{1,13},{2,14},{3,15},{4,8},{5,9},{6,10},{7,11},{8,4},{9,5},... | collective-permute-start | bytes 221192 | tf_op jit(solution)/shard_map/ppermute | solution.py:46
  34.6 5.4 %collective-permute-start.8 = (bf16[2,2,32,576]{3,2,1,0:T(8,128)(2,1)S(1)}, bf16[2,2,32,576]{3,2,1,0:T(8,128)(2,1)S(1)}, u32[]{:S(2)}, u32[]{:S(2)}) collective-permute-start(bf16[2,2,32,576]{3,2,1,0:T(8,128)(2,1)S(1)} %pad_maximum_fusion.own), channel_id=1, source_target_pairs={{0,2},{1,3},{2,0},{3,1},{4,6},{5,7},{6,4},{7,5},{8,10},{9,11},{10,... | collective-permute-start | bytes 442376 | tf_op jit(solution)/shard_map/ppermute | solution.py:46
  36.4 5.9 %collective-permute-start.10 = (bf16[2,2,32,576]{3,2,1,0:T(8,128)(2,1)S(1)}, bf16[2,2,32,576]{3,2,1,0:T(8,128)(2,1)S(1)}, u32[]{:S(2)}, u32[]{:S(2)}) collective-permute-start(bf16[2,2,32,576]{3,2,1,0:T(8,128)(2,1)S(1)} %pad_maximum_fusion.own), channel_id=1, source_target_pairs={{0,16},{1,17},{2,18},{3,19},{4,20},{5,21},{6,22},{7,23},{8,24},{9,... | collective-permute-start | bytes 442376 | tf_op jit(solution)/shard_map/ppermute | solution.py:46
  40.0 7.5 %collective-permute-start.16 = (bf16[2,2,32,576]{3,2,1,0:T(8,128)(2,1)S(1)}, bf16[2,2,32,576]{3,2,1,0:T(8,128)(2,1)S(1)}, u32[]{:S(2)}, u32[]{:S(2)}) collective-permute-start(bf16[2,2,32,576]{3,2,1,0:T(8,128)(2,1)S(1)} %after.5.own_far), channel_id=1, source_target_pairs={{0,16},{1,17},{2,18},{3,19},{4,20},{5,21},{6,22},{7,23},{8,24},{9,... | collective-permute-start | bytes 442376 | tf_op jit(solution)/shard_map/ppermute | solution.py:46
  40.5 5.8 %collective-permute-start.14 = (bf16[2,2,32,576]{3,2,1,0:T(8,128)(2,1)S(1)}, bf16[2,2,32,576]{3,2,1,0:T(8,128)(2,1)S(1)}, u32[]{:S(2)}, u32[]{:S(2)}) collective-permute-start(bf16[2,2,32,576]{3,2,1,0:T(8,128)(2,1)S(1)} %after.5.own_far), channel_id=1, source_target_pairs={{0,2},{1,3},{2,0},{3,1},{4,6},{5,7},{6,4},{7,5},{8,10},{9,11},{10,... | collective-permute-start | bytes 442376 | tf_op jit(solution)/shard_map/ppermute | solution.py:46
  42.3 9.9 %collective-permute-start.11 = (bf16[2,32,576]{2,1,0:T(8,128)(2,1)S(1)}, bf16[2,32,576]{2,1,0:T(8,128)(2,1)S(1)}, u32[]{:S(2)}, u32[]{:S(2)}) collective-permute-start(bf16[2,32,576]{2,1,0:T(8,128)(2,1)S(1)} %slice_bitcast_fusion.2), channel_id=1, source_target_pairs={{0,2},{1,3},{2,0},{3,1},{4,6},{5,7},{6,4},{7,5},{8,10},{9,11},{10,... | collective-permute-start | bytes 221192 | tf_op jit(solution)/shard_map/ppermute | solution.py:46
  42.6 9.6 %collective-permute-start.9 = (bf16[2,32,576]{2,1,0:T(8,128)(2,1)S(1)}, bf16[2,32,576]{2,1,0:T(8,128)(2,1)S(1)}, u32[]{:S(2)}, u32[]{:S(2)}) collective-permute-start(bf16[2,32,576]{2,1,0:T(8,128)(2,1)S(1)} %slice_bitcast_fusion.3), channel_id=1, source_target_pairs={{0,16},{1,17},{2,18},{3,19},{4,20},{5,21},{6,22},{7,23},{8,24},{9,... | collective-permute-start | bytes 221192 | tf_op jit(solution)/shard_map/ppermute | solution.py:46
  46.3 6.0 %collective-permute-start.15 = (bf16[2,32,576]{2,1,0:T(8,128)(2,1)S(1)}, bf16[2,32,576]{2,1,0:T(8,128)(2,1)S(1)}, u32[]{:S(2)}, u32[]{:S(2)}) collective-permute-start(bf16[2,32,576]{2,1,0:T(8,128)(2,1)S(1)} %slice_bitcast_fusion.1), channel_id=1, source_target_pairs={{0,16},{1,17},{2,18},{3,19},{4,20},{5,21},{6,22},{7,23},{8,24},{9,... | collective-permute-start | bytes 221192 | tf_op jit(solution)/shard_map/ppermute | solution.py:46
  47.5 4.8 %copy-start.2 = (bf16[256,256]{1,0:T(8,128)(2,1)S(1)}, bf16[256,256]{1,0:T(8,128)(2,1)}, u32[]{:S(2)}) copy-start(bf16[256,256]{1,0:T(8,128)(2,1)} %probe_own.1) | copy-start | bytes 393220
  47.5 4.8 %copy-start.5 = (f32[256]{0:T(256)S(1)}, f32[256]{0:T(256)}, u32[]{:S(2)}) copy-start(f32[256]{0:T(256)} %param.24) | copy-start | bytes 3076
  47.5 4.8 %copy-start.6 = (s32[256]{0:T(256)S(1)}, s32[256]{0:T(256)}, u32[]{:S(2)}) copy-start(s32[256]{0:T(256)} %param.25) | copy-start | bytes 3076
  47.5 4.7 %collective-permute-start.17 = (bf16[2,32,576]{2,1,0:T(8,128)(2,1)S(1)}, bf16[2,32,576]{2,1,0:T(8,128)(2,1)S(1)}, u32[]{:S(2)}, u32[]{:S(2)}) collective-permute-start(bf16[2,32,576]{2,1,0:T(8,128)(2,1)S(1)} %slice_bitcast_fusion), channel_id=1, source_target_pairs={{0,2},{1,3},{2,0},{3,1},{4,6},{5,7},{6,4},{7,5},{8,10},{9,11},{10,... | collective-permute-start | bytes 221192 | tf_op jit(solution)/shard_map/ppermute | solution.py:46
  52.2 12.5 %copy-start.3 = (f32[256,16]{0,1:T(8,128)S(1)}, f32[256,16]{0,1:T(8,128)}, u32[]{:S(2)}) copy-start(f32[256,16]{0,1:T(8,128)} %param.28) | copy-start | bytes 49156
  52.2 12.5 %copy-start.7 = (f32[256]{0:T(256)S(1)}, f32[256]{0:T(256)}, u32[]{:S(2)}) copy-start(f32[256]{0:T(256)} %param.27) | copy-start | bytes 3076
  52.2 12.5 %copy-start.8 = (f32[16]{0:T(128)S(1)}, f32[16]{0:T(128)}, u32[]{:S(2)}) copy-start(f32[16]{0:T(128)} %param.29) | copy-start | bytes 196

commit v4 on v3

--- a/solution.py
+++ b/solution.py
@@ -11,6 +11,7 @@
 SOFT_CAP = 50.0
 QUERY_SCALE = 1.0 / 12.0
 RAMP_WIDTH = 0.25
+ACROSS = (((1,), (1,)), ((), ()))
 
 ALL = ("y", "z", "x", "c")
 PLANE = ("y", "z", "x")
@@ -72,13 +73,21 @@
     head_count = queries.shape[1] // HEAD
     kv_heads = kv_width // HEAD
     group = 4
+    groups = [range(at, at + group) for at in range(0, row_count, group)]
     copies = []
-    for at in range(row_count // group):
+    for at in range(len(groups)):
         rows = pl.ds(at * group, group)
-        copies.append(pltpu.make_async_copy(keys_at.at[rows], keys.at[rows], arrived.at[0, at]))
-        copies.append(pltpu.make_async_copy(values_at.at[rows], values.at[rows], arrived.at[1, at]))
-    for copy in copies:
-        copy.start()
+        copies.append(
+            (
+                pltpu.make_async_copy(keys_at.at[rows], keys.at[rows], arrived.at[0, at]),
+                pltpu.make_async_copy(values_at.at[rows], values.at[rows], arrived.at[1, at]),
+            )
+        )
+    copies[0][0].start()
+    for at in range(len(groups)):
+        if at + 1 < len(groups):
+            copies[at + 1][0].start()
+        copies[at][1].start()
     for head in range(head_count):
         heads[pl.ds(head, row_count, stride=head_count), :] = queries[:, head * HEAD : (head + 1) * HEAD].astype(
             jnp.float32
@@ -93,38 +102,41 @@
     def cap(score):
         return jnp.exp(SOFT_CAP * jnp.tanh(score * (QUERY_SCALE / SOFT_CAP)))
 
-    for at in range(row_count // group):
-        copies[2 * at].wait()
-        weights, own_weights = [], []
-        for row in range(at * group, (at + 1) * group):
-            query = heads[row * head_count : (row + 1) * head_count, :]
-            spread = jnp.where(in_block, jnp.concatenate([query] * kv_heads, axis=1), 0.0)
-            scores = lax.dot_general(
-                spread.astype(jnp.bfloat16),
-                keys[row],
-                (((1,), (1,)), ((), ())),
-                preferred_element_type=jnp.float32,
-            )
-            own = cap(jnp.sum(spread * fresh_key[row : row + 1, :], axis=1, keepdims=True))
-            exps = jnp.where(place < lengths[row], cap(scores), 0.0)
-            scale = 1.0 / (jnp.sum(exps, axis=1, keepdims=True) + own)
-            weights.append((exps * scale).astype(jnp.bfloat16))
-            own_weights.append((own * scale).astype(jnp.bfloat16).astype(jnp.float32))
-        copies[2 * at + 1].wait()
-        for nth, row in enumerate(range(at * group, (at + 1) * group)):
-            mixture = jnp.dot(weights[nth], values[row], preferred_element_type=jnp.float32)
-            mixture = jnp.where(in_block, mixture + own_weights[nth] * fresh_value[row : row + 1, :], 0.0)
-            folded = mixture[:, :HEAD]
-            for kv_head in range(1, kv_heads):
-                folded = folded + mixture[:, kv_head * HEAD : (kv_head + 1) * HEAD]
-            heads[row * head_count : (row + 1) * head_count, :] = folded
-    for head in range(head_count):
-        mixed[:, head * HEAD : (head + 1) * HEAD] = heads[pl.ds(head, row_count, stride=head_count), :]
-    for to_y in range(2):
-        for to_c in range(2):
-            share = mixed[8 * to_c + 4 * to_y : 8 * to_c + 4 * to_y + 4, :].astype(jnp.bfloat16)
-            for zx in range(8):
-                out_ref[to_y * 16 + zx * 2 + to_c] = share
+    def weigh(row):
+        query = heads[row * head_count : (row + 1) * head_count, :]
+        spread = jnp.where(in_block, jnp.concatenate([query] * kv_heads, axis=1), 0.0)
+        scores = lax.dot_general(
+            spread.astype(jnp.bfloat16), keys[row], ACROSS, preferred_element_type=jnp.float32
+        )
+        own = cap(jnp.sum(spread * fresh_key[row : row + 1, :], axis=1, keepdims=True))
+        exps = jnp.where(place < lengths[row], cap(scores), 0.0)
+        scale = 1.0 / (jnp.sum(exps, axis=1, keepdims=True) + own)
+        return (exps * scale).astype(jnp.bfloat16), (own * scale).astype(jnp.bfloat16).astype(jnp.float32)
+
+    def mix(row, weights, own_weight):
+        mixture = jnp.dot(weights, values[row], preferred_element_type=jnp.float32)
+        mixture = jnp.where(in_block, mixture + own_weight * fresh_value[row : row + 1, :], 0.0)
+        folded = mixture[:, :HEAD]
+        for kv_head in range(1, kv_heads):
+            folded = folded + mixture[:, kv_head * HEAD : (kv_head + 1) * HEAD]
+        return folded
+
+    copies[0][0].wait()
+    weighed = [weigh(row) for row in groups[0]]
+    for at in range(len(groups)):
+        copies[at][1].wait()
+        if at + 1 < len(groups):
+            copies[at + 1][0].wait()
+            following = [weigh(row) for row in groups[at + 1]]
+        folded = [mix(row, *weighed[nth]) for nth, row in enumerate(groups[at])]
+        mixed[...] = jnp.concatenate(folded, axis=0)
+        share = [mixed[pl.ds(head, group, stride=head_count), :] for head in range(head_count)]
+        share = jnp.concatenate(share, axis=1).astype(jnp.bfloat16)
+        to_c, to_y = at // 2, at % 2
+        for zx in range(8):
+            out_ref[to_y * 16 + zx * 2 + to_c] = share
+        if at + 1 < len(groups):
+            weighed = following
 
 
 def attend_shares(queries, key_cache, value_cache, new_key, new_value, lengths):
@@ -139,7 +151,7 @@
             pltpu.VMEM(key_cache.shape, key_cache.dtype),
             pltpu.VMEM(value_cache.shape, value_cache.dtype),
             pltpu.VMEM((rows * width // HEAD, HEAD), jnp.float32),
-            pltpu.VMEM((rows, width), jnp.float32),
+            pltpu.VMEM((4 * width // HEAD, HEAD), jnp.float32),
             pltpu.SemaphoreType.DMA((2, rows // 4)),
         ],
         compiler_params=pltpu.CompilerParams(vmem_limit_bytes=56 * 1024 * 1024),
@@ -148,12 +160,8 @@
     )(lengths, queries, new_key, new_value, key_cache, value_cache)
 
 
-ACROSS = (((1,), (1,)), ((), ()))
-
-
 def keep_kernel(kept_own, kept_other, *rest):
-    out_ref, token_ref, turned = rest[-3:]
-    token_ref[...] = jnp.zeros_like(token_ref)
+    out_ref, _, turned = rest[-3:]
     y, c = lax.axis_index("y"), lax.axis_index("c")
     for at, kept in enumerate((kept_own, kept_other)):
         turned[...] = kept[...].astype(jnp.float32).T
@@ -171,7 +179,7 @@
             jax.ShapeDtypeStruct((8, 128), jnp.float32),
         ),
         in_specs=vmem(2) + [pl.BlockSpec(memory_space=pl.ANY)] * len(ready),
-        out_specs=tuple(vmem(2)),
+        out_specs=(*vmem(1), pl.BlockSpec(memory_space=pl.ANY)),
         scratch_shapes=[pltpu.VMEM((rows, features), jnp.float32)],
         compiler_params=pltpu.CompilerParams(vmem_limit_bytes=4 * 1024 * 1024),
         cost_estimate=cost(1e-6),
@@ -179,20 +187,20 @@
     )(kept_own, kept_other, *ready)
 
 
-def after(value, other, limit=1024 * 1024):
-    def kernel(value_ref, other_ref, out_ref):
+def after(value, *others):
+    def kernel(*refs):
         pass
 
     anywhere = pl.BlockSpec(memory_space=pl.ANY)
     return pl.pallas_call(
         kernel,
         out_shape=jax.ShapeDtypeStruct(value.shape, value.dtype),
-        in_specs=[anywhere] * 2,
+        in_specs=[anywhere] * (1 + len(others)),
         out_specs=anywhere,
         input_output_aliases={0: 0},
-        compiler_params=pltpu.CompilerParams(vmem_limit_bytes=limit),
+        compiler_params=pltpu.CompilerParams(vmem_limit_bytes=1024 * 1024),
         name="after",
-    )(value, other)
+    )(value, *others)
 
 
 def project_near_kernel(taken, weight_own, weight_other, kept, out_ref, far_ref, rows):
@@ -428,9 +436,8 @@
 
     sent = attend_shares(queries, key_cache, value_cache, new_key, new_value, lengths)
     kept_rows, token = keep(kept, kept_other, (probe_other, bias_other, code_other))
-    sent = after(sent, token, 56 * 1024 * 1024)
     taken = lax.all_to_all(sent, ALL, 0, 0, tiled=True)
-    proj_y = after(proj_y, taken)
+    proj_y = after(proj_y, taken, token)
     proj_yc = xor(proj_y, 1)
     near, far = project_near(taken, proj, proj_c, kept_rows)
     stream = project_far(far, proj_y, proj_yc, near)

time: 65.8 us -> 63.5 us (0.965)
  waiting for transfers between devices: 16.8 us -> 15.4 us
    all_to_all x1, waiting for transfers between devices: 8.65 us -> 3.97 us  [chip_body(): taken = lax.all_to_all(sent, ALL, 0, 0, tiled=True)]
    ppermute x19, waiting for transfers between devices: 8.2 us -> 11.4 us  [xor(): return lax.ppermute(value, ALL, [(i, i ^ bits) for i in range(32)])]
  transfers between devices with their start and end apart: 20 -> 20, of which waited for: 7 -> 8; matrix products, arithmetic and copies ran while one was open for 0% -> 0% of each run, Pallas kernels for 15% -> 15%
where the time goes in v4:
time: 63.5 us; the launch traced here: 63.2 us
  starting transfers between devices  24.4 us (38%)
  waiting for transfers between devices  15.4 us (24%)
  blocking collectives  11.6 us (18%)
  Pallas kernels  10.8 us (17%)
  between operations  0.82 us (1%)
    ppermute x19, starting transfers between devices, xor(): return lax.ppermute(value, ALL, [(i, i ^ bits) for i in range(32)])  19.5 us
    all_to_all x1, blocking collectives, chip_body(): parts = lax.all_to_all(partial, PLANE, 0, 0, tiled=True)  11.6 us
    ppermute x19, waiting for transfers between devices, xor(): return lax.ppermute(value, ALL, [(i, i ^ bits) for i in range(32)])  11.4 us
    pallas_call x1, Pallas kernels, attend_shares(): pl.pallas_call(attend_kernel, out_shape=jax.ShapeDtypeStruct((32, 4, widt...  5.5 us
    all_to_all x1, starting transfers between devices, chip_body(): taken = lax.all_to_all(sent, ALL, 0, 0, tiled=True)  4.9 us
    all_to_all x1, waiting for transfers between devices, chip_body(): taken = lax.all_to_all(sent, ALL, 0, 0, tiled=True)  3.97 us
    pallas_call x1, Pallas kernels, encode_first(): pl.pallas_call(encode_first_kernel, out_shape=(jax.ShapeDtypeStruct((2, r...  2.43 us
  transfers between devices with their start and end apart: 20, of which 8 were waited for; matrix products, arithmetic and copies ran while one was open for 0% of the time, Pallas kernels for 15%

profile of v4, /device:TPU:0, one launch (start us, length us, event | category | flops | bytes accessed | tf_op | source)
XLA Modules:
  0.0 63.2 jit_solution(16191231994095387678)
XLA Ops:
  0.6 0.0 copy-start.1
  0.6 0.0 copy-start.2
  0.7 0.0 copy-start.4
  0.7 0.0 copy-start.5
  0.7 0.0 copy-start
  0.7 3.0 %collective-permute-start.5 = (bf16[288,1024]{1,0:T(8,128)(2,1)}, bf16[288,1024]{1,0:T(8,128)(2,1)S(1)}, u32[]{:S(2)}, u32[]{:S(2)}) collective-permute-start(bf16[288,1024]{1,0:T(8,128)(2,1)} %bitcast.21), channel_id=1, source_target_pairs={{0,16},{1,17},{2,18},{3,19},{4,20},{5,21},{6,22},{7,23},{8,24},{9,... | collective-permute-start | bytes 1769480 | tf_op jit(solution)/shard_map/ppermute | solution.py:47
  3.7 5.5 %attend.1 = bf16[32,4,1024]{2,1,0:T(4,128)(2,1)} custom-call(s32[16]{0:T(128)} %lengths.1, bf16[16,1024]{1,0:T(8,128)(2,1)} %queries.1, bf16[16,512]{1,0:T(8,128)(2,1)} %new_key.1, bf16[16,512]{1,0:T(8,128)(2,1)} %new_value.1, bf16[16,256,512]{2,1,0:T(8,128)(2,1)} %keys_at.1, bf16[16,256,512]{2,1,0:T(8,128)(2,1)} %values_at.1), custom_call_target="tpu_custom_call" | custom-call | bytes 44280000 | tf_op jit(solution)/shard_map/attend/pallas_call | solution.py:145
  9.2 4.9 %all-to-all-start = ((bf16[32,4,1024]{2,1,0:T(4,128)(2,1)}), bf16[32,4,1024]{2,1,0:T(4,128)(2,1)S(1)}, u32[]{:S(2)}, u32[]{:S(2)}) async-start(bf16[32,4,1024]{2,1,0:T(4,128)(2,1)} %attend.1), calls=%async_computation | async-start | bytes 524288 | tf_op jit(solution)/shard_map/all_to_all | solution.py:439
  14.1 0.3 collective-permute-start.18
  14.5 0.0 copy-done.1
  14.5 0.3 collective-permute-start.1
  14.7 0.0 copy-done.2
  14.7 0.3 collective-permute-start.2
  15.0 0.0 copy-done.4
  15.0 0.3 collective-permute-start.3
  15.2 3.5 %collective-permute-done.3.rest_1_ = f32[256]{0:T(256)S(1)} collective-permute-done((f32[256]{0:T(256)S(1)}, f32[256]{0:T(256)S(1)}, u32[]{:S(2)}, u32[]{:S(2)}) %collective-permute-start.3) | collective-permute-done | bytes 1056 | tf_op jit(solution)/shard_map/ppermute | solution.py:47
  18.7 0.0 copy-done.5
  18.7 0.3 collective-permute-start.4
  19.0 0.8 %collective-permute-done.4.rest_2_ = s32[256]{0:T(256)S(1)} collective-permute-done((s32[256]{0:T(256)S(1)}, s32[256]{0:T(256)S(1)}, u32[]{:S(2)}, u32[]{:S(2)}) %collective-permute-start.4) | collective-permute-done | bytes 1056 | tf_op jit(solution)/shard_map/ppermute | solution.py:47
  19.9 0.0 copy-done
  19.9 0.3 collective-permute-start
  20.2 0.0 collective-permute-done.2.rest_0_.probe_other
  20.2 0.0 collective-permute-done.1.kept_other
  20.2 0.3 keep.1
  20.5 4.0 %all-to-all-done.taken.refs_1_ = bf16[32,4,1024]{2,1,0:T(4,128)(2,1)S(1)} async-done(((bf16[32,4,1024]{2,1,0:T(4,128)(2,1)}), bf16[32,4,1024]{2,1,0:T(4,128)(2,1)S(1)}, u32[]{:S(2)}, u32[]{:S(2)}) %all-to-all-start) | async-done | bytes 262176 | tf_op jit(solution)/shard_map/all_to_all | solution.py:439
  24.4 0.0 collective-permute-done.5.refs_0_
  24.4 0.3 collective-permute-start.6
  24.7 0.0 collective-permute-done.weight_other
  24.7 0.5 project_near.1
  25.3 1.1 %collective-permute-done.6.weight_other = bf16[288,1024]{1,0:T(8,128)(2,1)S(1)} collective-permute-done((bf16[288,1024]{1,0:T(8,128)(2,1)S(1)}, bf16[288,1024]{1,0:T(8,128)(2,1)S(1)}, u32[]{:S(2)}, u32[]{:S(2)}) %collective-permute-start.6) | collective-permute-done | bytes 589856 | tf_op jit(solution)/shard_map/ppermute | solution.py:47
  26.4 0.6 project_far.1
  27.0 1.2 %collective-permute-start.7 = (bf16[2,32,576]{2,1,0:T(8,128)(2,1)S(1)}, bf16[2,32,576]{2,1,0:T(8,128)(2,1)S(1)}, u32[]{:S(2)}, u32[]{:S(2)}) collective-permute-start(bf16[2,32,576]{2,1,0:T(8,128)(2,1)S(1)} %project_far.1), channel_id=1, source_target_pairs={{0,4},{1,5},{2,6},{3,7},{4,0},{5,1},{6,2},{7,3},{8,12},{9,13},{10,... | collective-permute-start | bytes 221192 | tf_op jit(solution)/shard_map/ppermute | solution.py:47
  28.2 1.4 %collective-permute-start.12 = (bf16[2,32,576]{2,1,0:T(8,128)(2,1)S(1)}, bf16[2,32,576]{2,1,0:T(8,128)(2,1)S(1)}, u32[]{:S(2)}, u32[]{:S(2)}) collective-permute-start(bf16[2,32,576]{2,1,0:T(8,128)(2,1)S(1)} %project_far.1), channel_id=1, source_target_pairs={{0,8},{1,9},{2,10},{3,11},{4,12},{5,13},{6,14},{7,15},{8,0},{9,1},... | collective-permute-start | bytes 221192 | tf_op jit(solution)/shard_map/ppermute | solution.py:47
  29.6 1.8 %collective-permute-start.13 = (bf16[2,32,576]{2,1,0:T(8,128)(2,1)S(1)}, bf16[2,32,576]{2,1,0:T(8,128)(2,1)S(1)}, u32[]{:S(2)}, u32[]{:S(2)}) collective-permute-start(bf16[2,32,576]{2,1,0:T(8,128)(2,1)S(1)} %project_far.1), channel_id=1, source_target_pairs={{0,12},{1,13},{2,14},{3,15},{4,8},{5,9},{6,10},{7,11},{8,4},{9,5},... | collective-permute-start | bytes 221192 | tf_op jit(solution)/shard_map/ppermute | solution.py:47
  31.5 0.9 %collective-permute-done.7 = bf16[2,32,576]{2,1,0:T(8,128)(2,1)S(1)} collective-permute-done((bf16[2,32,576]{2,1,0:T(8,128)(2,1)S(1)}, bf16[2,32,576]{2,1,0:T(8,128)(2,1)S(1)}, u32[]{:S(2)}, u32[]{:S(2)}) %collective-permute-start.7) | collective-permute-done | bytes 73760 | tf_op jit(solution)/shard_map/ppermute | solution.py:47
  32.4 1.8 %collective-permute-start.8 = (bf16[2,2,32,576]{3,2,1,0:T(8,128)(2,1)S(1)}, bf16[2,2,32,576]{3,2,1,0:T(8,128)(2,1)S(1)}, u32[]{:S(2)}, u32[]{:S(2)}) collective-permute-start(bf16[2,2,32,576]{3,2,1,0:T(8,128)(2,1)S(1)} %pad_maximum_fusion.own), channel_id=1, source_target_pairs={{0,2},{1,3},{2,0},{3,1},{4,6},{5,7},{6,4},{7,5},{8,10},{9,11},{10,... | collective-permute-start | bytes 442376 | tf_op jit(solution)/shard_map/ppermute | solution.py:47
  34.2 0.5 collective-permute-start.10
  34.7 2.7 %collective-permute-done.12 = bf16[2,32,576]{2,1,0:T(8,128)(2,1)S(1)} collective-permute-done((bf16[2,32,576]{2,1,0:T(8,128)(2,1)S(1)}, bf16[2,32,576]{2,1,0:T(8,128)(2,1)S(1)}, u32[]{:S(2)}, u32[]{:S(2)}) %collective-permute-start.12) | collective-permute-done | bytes 73760 | tf_op jit(solution)/shard_map/ppermute | solution.py:47
  37.4 0.0 collective-permute-done.13
  37.5 0.3 collective-permute-done.8.refs_1_.own
  37.8 0.5 collective-permute-start.16
  38.3 1.8 %collective-permute-start.14 = (bf16[2,2,32,576]{3,2,1,0:T(8,128)(2,1)S(1)}, bf16[2,2,32,576]{3,2,1,0:T(8,128)(2,1)S(1)}, u32[]{:S(2)}, u32[]{:S(2)}) collective-permute-start(bf16[2,2,32,576]{3,2,1,0:T(8,128)(2,1)S(1)} %after.3.own_far), channel_id=1, source_target_pairs={{0,2},{1,3},{2,0},{3,1},{4,6},{5,7},{6,4},{7,5},{8,10},{9,11},{10,... | collective-permute-start | bytes 442376 | tf_op jit(solution)/shard_map/ppermute | solution.py:47
  40.1 0.0 collective-permute-done.10.other
  40.1 0.3 collective-permute-start.11
  40.4 1.6 %collective-permute-start.9 = (bf16[2,32,576]{2,1,0:T(8,128)(2,1)S(1)}, bf16[2,32,576]{2,1,0:T(8,128)(2,1)S(1)}, u32[]{:S(2)}, u32[]{:S(2)}) collective-permute-start(bf16[2,32,576]{2,1,0:T(8,128)(2,1)S(1)} %slice_bitcast_fusion.3), channel_id=1, source_target_pairs={{0,16},{1,17},{2,18},{3,19},{4,20},{5,21},{6,22},{7,23},{8,24},{9,... | collective-permute-start | bytes 221192 | tf_op jit(solution)/shard_map/ppermute | solution.py:47
  42.0 2.1 %collective-permute-done.14.own_far = bf16[2,2,32,576]{3,2,1,0:T(8,128)(2,1)S(1)} collective-permute-done((bf16[2,2,32,576]{3,2,1,0:T(8,128)(2,1)S(1)}, bf16[2,2,32,576]{3,2,1,0:T(8,128)(2,1)S(1)}, u32[]{:S(2)}, u32[]{:S(2)}) %collective-permute-start.14) | collective-permute-done | bytes 147488 | tf_op jit(solution)/shard_map/ppermute | solution.py:47
  44.1 1.2 %collective-permute-start.15 = (bf16[2,32,576]{2,1,0:T(8,128)(2,1)S(1)}, bf16[2,32,576]{2,1,0:T(8,128)(2,1)S(1)}, u32[]{:S(2)}, u32[]{:S(2)}) collective-permute-start(bf16[2,32,576]{2,1,0:T(8,128)(2,1)S(1)} %slice_bitcast_fusion.1), channel_id=1, source_target_pairs={{0,16},{1,17},{2,18},{3,19},{4,20},{5,21},{6,22},{7,23},{8,24},{9,... | collective-permute-start | bytes 221192 | tf_op jit(solution)/shard_map/ppermute | solution.py:47
  45.3 0.0 collective-permute-done.16.other_far
  45.3 2.3 %collective-permute-start.17 = (bf16[2,32,576]{2,1,0:T(8,128)(2,1)S(1)}, bf16[2,32,576]{2,1,0:T(8,128)(2,1)S(1)}, u32[]{:S(2)}, u32[]{:S(2)}) collective-permute-start(bf16[2,32,576]{2,1,0:T(8,128)(2,1)S(1)} %slice_bitcast_fusion), channel_id=1, source_target_pairs={{0,2},{1,3},{2,0},{3,1},{4,6},{5,7},{6,4},{7,5},{8,10},{9,11},{10,... | collective-permute-start | bytes 221192 | tf_op jit(solution)/shard_map/ppermute | solution.py:47
  47.5 0.0 collective-permute-done.18.enc_other
  47.5 2.4 %encode_first.1 = (f32[2,128,256]{2,1,0:T(8,128)S(1)}, bf16[2,4,576,256]{3,2,1,0:T(8,128)(2,1)S(1)}) custom-call(bf16[2,2,32,576]{3,2,1,0:T(8,128)(2,1)S(1)} %pad_maximum_fusion.own, bf16[2,2,32,576]{3,2,1,0:T(8,128)(2,1)S(1)} %collective-permute-done.10.other, bf16[2,2,32,576]{3,2,1,0:T(8,128)(2,1)S(1)} %after.3.own_far, ...), custom_call_target="tpu_custom_call" | custom-call | bytes 7380000 | tf_op jit(solution)/shard_map/encode_first/pallas_call | solution.py:348
  50.0 0.0 copy-start.3
  50.0 0.0 copy-start.6
  50.0 0.0 copy-start.7
  50.0 0.0 collective-permute-done.11.lower
  50.0 0.0 collective-permute-done.9.upper
  50.0 0.0 collective-permute-done.15.upper_far
  50.1 0.0 collective-permute-done.17.lower_far
  50.1 0.7 %encode_second.1 = bf16[16,8,256]{2,1,0:T(8,128)(2,1)S(1)} custom-call(bf16[2,2,32,576]{3,2,1,0:T(8,128)(2,1)S(1)} %collective-permute-done.8.refs_1_.own, bf16[2,32,576]{2,1,0:T(8,128)(2,1)S(1)} %collective-permute-done.9.upper, bf16[2,32,576]{2,1,0:T(8,128)(2,1)S(1)} %collective-permute-done.11.lower, ...), custom_call_target="tpu_custom_call" | custom-call | bytes 7380000 | tf_op jit(solution)/shard_map/encode_second/pallas_call | solution.py:365
  50.8 11.6 %all_to_all.10.parts = bf16[16,8,256]{2,1,0:T(8,128)(2,1)S(1)} all-to-all(bf16[16,8,256]{2,1,0:T(8,128)(2,1)S(1)} %encode_second.1), channel_id=1, replica_groups=mesh['y'=2,'z'=4,'x'=2,'c'=2] {'y','z','x'}, dimensions={0} | all-to-all | bytes 131072 | tf_op jit(solution)/shard_map/all_to_all | solution.py:461
  62.4 0.0 copy-done.3
  62.4 0.0 copy-done.6
  62.4 0.0 copy-done.7
  62.4 0.8 %finish.1 = (f32[8,256]{1,0:T(8,128)}, f32[8,16]{1,0:T(8,128)}) custom-call(bf16[16,8,256]{2,1,0:T(8,128)(2,1)S(1)} %all_to_all.10.parts, f32[1,256]{1,0:T(1,128)S(1)} %bitcast.32, f32[16,256]{1,0:T(8,128)S(1)} %bitcast.27, f32[1,16]{1,0:T(1,128)S(1)} %bitcast.33), custom_call_target="tpu_custom_call" | custom-call | tf_op jit(solution)/shard_map/finish/pallas_call | solution.py:398
  (8 shorter events, 0.1 us)
Async XLA Ops:
  0.6 13.8 %copy-start.1 = (bf16[256,288]{0,1:T(8,128)(2,1)S(1)}, bf16[256,288]{0,1:T(8,128)(2,1)}, u32[]{:S(2)}) copy-start(bf16[256,288]{0,1:T(8,128)(2,1)} %param.22) | copy-start | bytes 442372
  0.6 14.1 %copy-start.2 = (bf16[256,256]{1,0:T(8,128)(2,1)S(1)}, bf16[256,256]{1,0:T(8,128)(2,1)}, u32[]{:S(2)}) copy-start(bf16[256,256]{1,0:T(8,128)(2,1)} %probe_own.1) | copy-start | bytes 393220
  0.7 14.3 %copy-start.4 = (f32[256]{0:T(256)S(1)}, f32[256]{0:T(256)}, u32[]{:S(2)}) copy-start(f32[256]{0:T(256)} %param.24) | copy-start | bytes 3076
  0.7 18.0 %copy-start.5 = (s32[256]{0:T(256)S(1)}, s32[256]{0:T(256)}, u32[]{:S(2)}) copy-start(s32[256]{0:T(256)} %param.25) | copy-start | bytes 3076
  0.7 19.2 %copy-start = (bf16[1024,288]{0,1:T(8,128)(2,1)S(1)}, bf16[1024,288]{0,1:T(8,128)(2,1)}, u32[]{:S(2)}) copy-start(bf16[1024,288]{0,1:T(8,128)(2,1)} %param.21) | copy-start | bytes 1769476
  0.7 23.8 %collective-permute-start.5 = (bf16[288,1024]{1,0:T(8,128)(2,1)}, bf16[288,1024]{1,0:T(8,128)(2,1)S(1)}, u32[]{:S(2)}, u32[]{:S(2)}) collective-permute-start(bf16[288,1024]{1,0:T(8,128)(2,1)} %bitcast.21), channel_id=1, source_target_pairs={{0,16},{1,17},{2,18},{3,19},{4,20},{5,21},{6,22},{7,23},{8,24},{9,... | collective-permute-start | bytes 1769480 | tf_op jit(solution)/shard_map/ppermute | solution.py:47
  9.2 15.2 %all-to-all-start = ((bf16[32,4,1024]{2,1,0:T(4,128)(2,1)}), bf16[32,4,1024]{2,1,0:T(4,128)(2,1)S(1)}, u32[]{:S(2)}, u32[]{:S(2)}) async-start(bf16[32,4,1024]{2,1,0:T(4,128)(2,1)} %attend.1), calls=%async_computation | async-start | bytes 524288 | tf_op jit(solution)/shard_map/all_to_all | solution.py:439
  14.1 33.4 %collective-permute-start.18 = (bf16[4608,256]{1,0:T(8,128)(2,1)}, bf16[4608,256]{1,0:T(8,128)(2,1)}, u32[]{:S(2)}, u32[]{:S(2)}) collective-permute-start(bf16[4608,256]{1,0:T(8,128)(2,1)} %enc_own.1), channel_id=1, source_target_pairs={{0,1},{1,0},{2,3},{3,2},{4,5},{5,4},{6,7},{7,6},{8,9},{9,8},{10,11... | collective-permute-start | bytes 7077896 | tf_op jit(solution)/shard_map/ppermute | solution.py:47
  14.5 5.7 %collective-permute-start.1 = (bf16[288,256]{1,0:T(8,128)(2,1)S(1)}, bf16[288,256]{1,0:T(8,128)(2,1)S(1)}, u32[]{:S(2)}, u32[]{:S(2)}) collective-permute-start(bf16[288,256]{1,0:T(8,128)(2,1)S(1)} %bitcast.25), channel_id=1, source_target_pairs={{0,1},{1,0},{2,3},{3,2},{4,5},{5,4},{6,7},{7,6},{8,9},{9,8},{10,11... | collective-permute-start | bytes 442376 | tf_op jit(solution)/shard_map/ppermute | solution.py:47
  14.7 5.5 %collective-permute-start.2 = (bf16[256,256]{1,0:T(8,128)(2,1)S(1)}, bf16[256,256]{1,0:T(8,128)(2,1)S(1)}, u32[]{:S(2)}, u32[]{:S(2)}) collective-permute-start(bf16[256,256]{1,0:T(8,128)(2,1)S(1)} %copy-done.2), channel_id=1, source_target_pairs={{0,1},{1,0},{2,3},{3,2},{4,5},{5,4},{6,7},{7,6},{8,9},{9,8},{10,11... | collective-permute-start | bytes 393224 | tf_op jit(solution)/shard_map/ppermute | solution.py:47
  15.0 3.7 %collective-permute-start.3 = (f32[256]{0:T(256)S(1)}, f32[256]{0:T(256)S(1)}, u32[]{:S(2)}, u32[]{:S(2)}) collective-permute-start(f32[256]{0:T(256)S(1)} %copy-done.4), channel_id=1, source_target_pairs={{0,1},{1,0},{2,3},{3,2},{4,5},{5,4},{6,7},{7,6},{8,9},{9,8},{10,11... | collective-permute-start | bytes 3080 | tf_op jit(solution)/shard_map/ppermute | solution.py:47
  18.7 1.1 %collective-permute-start.4 = (s32[256]{0:T(256)S(1)}, s32[256]{0:T(256)S(1)}, u32[]{:S(2)}, u32[]{:S(2)}) collective-permute-start(s32[256]{0:T(256)S(1)} %copy-done.5), channel_id=1, source_target_pairs={{0,1},{1,0},{2,3},{3,2},{4,5},{5,4},{6,7},{7,6},{8,9},{9,8},{10,11... | collective-permute-start | bytes 3080 | tf_op jit(solution)/shard_map/ppermute | solution.py:47
  19.9 4.9 %collective-permute-start = (bf16[288,1024]{1,0:T(8,128)(2,1)S(1)}, bf16[288,1024]{1,0:T(8,128)(2,1)S(1)}, u32[]{:S(2)}, u32[]{:S(2)}) collective-permute-start(bf16[288,1024]{1,0:T(8,128)(2,1)S(1)} %bitcast.22), channel_id=1, source_target_pairs={{0,1},{1,0},{2,3},{3,2},{4,5},{5,4},{6,7},{7,6},{8,9},{9,8},{10,11... | collective-permute-start | bytes 1769480 | tf_op jit(solution)/shard_map/ppermute | solution.py:47
  24.4 2.0 %collective-permute-start.6 = (bf16[288,1024]{1,0:T(8,128)(2,1)S(1)}, bf16[288,1024]{1,0:T(8,128)(2,1)S(1)}, u32[]{:S(2)}, u32[]{:S(2)}) collective-permute-start(bf16[288,1024]{1,0:T(8,128)(2,1)S(1)} %after.2.weight_own), channel_id=1, source_target_pairs={{0,1},{1,0},{2,3},{3,2},{4,5},{5,4},{6,7},{7,6},{8,9},{9,8},{10,11... | collective-permute-start | bytes 1769480 | tf_op jit(solution)/shard_map/ppermute | solution.py:47
  27.0 5.3 %collective-permute-start.7 = (bf16[2,32,576]{2,1,0:T(8,128)(2,1)S(1)}, bf16[2,32,576]{2,1,0:T(8,128)(2,1)S(1)}, u32[]{:S(2)}, u32[]{:S(2)}) collective-permute-start(bf16[2,32,576]{2,1,0:T(8,128)(2,1)S(1)} %project_far.1), channel_id=1, source_target_pairs={{0,4},{1,5},{2,6},{3,7},{4,0},{5,1},{6,2},{7,3},{8,12},{9,13},{10,... | collective-permute-start | bytes 221192 | tf_op jit(solution)/shard_map/ppermute | solution.py:47
  28.2 9.2 %collective-permute-start.12 = (bf16[2,32,576]{2,1,0:T(8,128)(2,1)S(1)}, bf16[2,32,576]{2,1,0:T(8,128)(2,1)S(1)}, u32[]{:S(2)}, u32[]{:S(2)}) collective-permute-start(bf16[2,32,576]{2,1,0:T(8,128)(2,1)S(1)} %project_far.1), channel_id=1, source_target_pairs={{0,8},{1,9},{2,10},{3,11},{4,12},{5,13},{6,14},{7,15},{8,0},{9,1},... | collective-permute-start | bytes 221192 | tf_op jit(solution)/shard_map/ppermute | solution.py:47
  29.6 7.8 %collective-permute-start.13 = (bf16[2,32,576]{2,1,0:T(8,128)(2,1)S(1)}, bf16[2,32,576]{2,1,0:T(8,128)(2,1)S(1)}, u32[]{:S(2)}, u32[]{:S(2)}) collective-permute-start(bf16[2,32,576]{2,1,0:T(8,128)(2,1)S(1)} %project_far.1), channel_id=1, source_target_pairs={{0,12},{1,13},{2,14},{3,15},{4,8},{5,9},{6,10},{7,11},{8,4},{9,5},... | collective-permute-start | bytes 221192 | tf_op jit(solution)/shard_map/ppermute | solution.py:47
  32.4 5.4 %collective-permute-start.8 = (bf16[2,2,32,576]{3,2,1,0:T(8,128)(2,1)S(1)}, bf16[2,2,32,576]{3,2,1,0:T(8,128)(2,1)S(1)}, u32[]{:S(2)}, u32[]{:S(2)}) collective-permute-start(bf16[2,2,32,576]{3,2,1,0:T(8,128)(2,1)S(1)} %pad_maximum_fusion.own), channel_id=1, source_target_pairs={{0,2},{1,3},{2,0},{3,1},{4,6},{5,7},{6,4},{7,5},{8,10},{9,11},{10,... | collective-permute-start | bytes 442376 | tf_op jit(solution)/shard_map/ppermute | solution.py:47
  34.2 5.9 %collective-permute-start.10 = (bf16[2,2,32,576]{3,2,1,0:T(8,128)(2,1)S(1)}, bf16[2,2,32,576]{3,2,1,0:T(8,128)(2,1)S(1)}, u32[]{:S(2)}, u32[]{:S(2)}) collective-permute-start(bf16[2,2,32,576]{3,2,1,0:T(8,128)(2,1)S(1)} %pad_maximum_fusion.own), channel_id=1, source_target_pairs={{0,16},{1,17},{2,18},{3,19},{4,20},{5,21},{6,22},{7,23},{8,24},{9,... | collective-permute-start | bytes 442376 | tf_op jit(solution)/shard_map/ppermute | solution.py:47
  37.8 7.5 %collective-permute-start.16 = (bf16[2,2,32,576]{3,2,1,0:T(8,128)(2,1)S(1)}, bf16[2,2,32,576]{3,2,1,0:T(8,128)(2,1)S(1)}, u32[]{:S(2)}, u32[]{:S(2)}) collective-permute-start(bf16[2,2,32,576]{3,2,1,0:T(8,128)(2,1)S(1)} %after.3.own_far), channel_id=1, source_target_pairs={{0,16},{1,17},{2,18},{3,19},{4,20},{5,21},{6,22},{7,23},{8,24},{9,... | collective-permute-start | bytes 442376 | tf_op jit(solution)/shard_map/ppermute | solution.py:47
  38.3 5.8 %collective-permute-start.14 = (bf16[2,2,32,576]{3,2,1,0:T(8,128)(2,1)S(1)}, bf16[2,2,32,576]{3,2,1,0:T(8,128)(2,1)S(1)}, u32[]{:S(2)}, u32[]{:S(2)}) collective-permute-start(bf16[2,2,32,576]{3,2,1,0:T(8,128)(2,1)S(1)} %after.3.own_far), channel_id=1, source_target_pairs={{0,2},{1,3},{2,0},{3,1},{4,6},{5,7},{6,4},{7,5},{8,10},{9,11},{10,... | collective-permute-start | bytes 442376 | tf_op jit(solution)/shard_map/ppermute | solution.py:47
  40.1 9.9 %collective-permute-start.11 = (bf16[2,32,576]{2,1,0:T(8,128)(2,1)S(1)}, bf16[2,32,576]{2,1,0:T(8,128)(2,1)S(1)}, u32[]{:S(2)}, u32[]{:S(2)}) collective-permute-start(bf16[2,32,576]{2,1,0:T(8,128)(2,1)S(1)} %slice_bitcast_fusion.2), channel_id=1, source_target_pairs={{0,2},{1,3},{2,0},{3,1},{4,6},{5,7},{6,4},{7,5},{8,10},{9,11},{10,... | collective-permute-start | bytes 221192 | tf_op jit(solution)/shard_map/ppermute | solution.py:47
  40.4 9.6 %collective-permute-start.9 = (bf16[2,32,576]{2,1,0:T(8,128)(2,1)S(1)}, bf16[2,32,576]{2,1,0:T(8,128)(2,1)S(1)}, u32[]{:S(2)}, u32[]{:S(2)}) collective-permute-start(bf16[2,32,576]{2,1,0:T(8,128)(2,1)S(1)} %slice_bitcast_fusion.3), channel_id=1, source_target_pairs={{0,16},{1,17},{2,18},{3,19},{4,20},{5,21},{6,22},{7,23},{8,24},{9,... | collective-permute-start | bytes 221192 | tf_op jit(solution)/shard_map/ppermute | solution.py:47
  44.1 6.0 %collective-permute-start.15 = (bf16[2,32,576]{2,1,0:T(8,128)(2,1)S(1)}, bf16[2,32,576]{2,1,0:T(8,128)(2,1)S(1)}, u32[]{:S(2)}, u32[]{:S(2)}) collective-permute-start(bf16[2,32,576]{2,1,0:T(8,128)(2,1)S(1)} %slice_bitcast_fusion.1), channel_id=1, source_target_pairs={{0,16},{1,17},{2,18},{3,19},{4,20},{5,21},{6,22},{7,23},{8,24},{9,... | collective-permute-start | bytes 221192 | tf_op jit(solution)/shard_map/ppermute | solution.py:47
  45.3 4.8 %collective-permute-start.17 = (bf16[2,32,576]{2,1,0:T(8,128)(2,1)S(1)}, bf16[2,32,576]{2,1,0:T(8,128)(2,1)S(1)}, u32[]{:S(2)}, u32[]{:S(2)}) collective-permute-start(bf16[2,32,576]{2,1,0:T(8,128)(2,1)S(1)} %slice_bitcast_fusion), channel_id=1, source_target_pairs={{0,2},{1,3},{2,0},{3,1},{4,6},{5,7},{6,4},{7,5},{8,10},{9,11},{10,... | collective-permute-start | bytes 221192 | tf_op jit(solution)/shard_map/ppermute | solution.py:47
  50.0 12.4 %copy-start.3 = (f32[256,16]{0,1:T(8,128)S(1)}, f32[256,16]{0,1:T(8,128)}, u32[]{:S(2)}) copy-start(f32[256,16]{0,1:T(8,128)} %param.28) | copy-start | bytes 49156
  50.0 12.4 %copy-start.6 = (f32[256]{0:T(256)S(1)}, f32[256]{0:T(256)}, u32[]{:S(2)}) copy-start(f32[256]{0:T(256)} %param.27) | copy-start | bytes 3076
  50.0 12.4 %copy-start.7 = (f32[16]{0:T(128)S(1)}, f32[16]{0:T(128)}, u32[]{:S(2)}) copy-start(f32[16]{0:T(128)} %param.29) | copy-start | bytes 196

commit v5 on v4

--- a/solution.py
+++ b/solution.py
@@ -14,7 +14,8 @@
 ACROSS = (((1,), (1,)), ((), ()))
 
 ALL = ("y", "z", "x", "c")
-PLANE = ("y", "z", "x")
+ODD_FIRST = [*range(1, 32, 2), *range(0, 32, 2)]
+PLANES = [list(range(30 + core, -1, -2)) for core in range(2)]
 
 
 def attend(queries, key_cache, value_cache, new_key, new_value, lengths):
@@ -134,7 +135,7 @@
         share = jnp.concatenate(share, axis=1).astype(jnp.bfloat16)
         to_c, to_y = at // 2, at % 2
         for zx in range(8):
-            out_ref[to_y * 16 + zx * 2 + to_c] = share
+            out_ref[(1 - to_c) * 16 + to_y * 8 + zx] = share
         if at + 1 < len(groups):
             weighed = following
 
@@ -203,23 +204,24 @@
     )(value, *others)
 
 
-def project_near_kernel(taken, weight_own, weight_other, kept, out_ref, far_ref, rows):
-    y = lax.axis_index("y")
+def project_kernel(taken, near_own, near_other, far_own, kept, *rest):
+    far_other, (out_ref, rows) = rest[:-2], rest[-2:]
+    y, core = lax.axis_index("y"), lax.axis_index("c")
     blocks, share = taken.shape[0] // 2, taken.shape[1]
     for b in range(blocks):
-        rows[0, b * share : (b + 1) * share, :] = taken[y * blocks + b].astype(jnp.float32)
-        rows[1, b * share : (b + 1) * share, :] = taken[(1 - y) * blocks + b].astype(jnp.float32)
-    far_ref[...] = rows[1].astype(jnp.bfloat16)
-    near = rows[0].astype(jnp.bfloat16)
-    for at, weight in enumerate((weight_own, weight_other)):
-        out_ref[at] = kept[at] + lax.dot_general(near, weight[...], ACROSS, preferred_element_type=jnp.float32)
-
-
-def project_far_kernel(far, weight_own, weight_other, near, out_ref):
-    rows = far[...]
-    own = near[0] + lax.dot_general(rows, weight_own[...], ACROSS, preferred_element_type=jnp.float32)
-    other = near[1] + lax.dot_general(rows, weight_other[...], ACROSS, preferred_element_type=jnp.float32)
-    core = lax.axis_index("c")
+        at = (1 - b % 2) * blocks + b // 2
+        rows[0, b * share : (b + 1) * share, :] = taken[at + y * 8].astype(jnp.float32)
+        rows[1, b * share : (b + 1) * share, :] = taken[at + (1 - y) * 8].astype(jnp.float32)
+    near, far = rows[0].astype(jnp.bfloat16), rows[1].astype(jnp.bfloat16)
+
+    def across(left, right):
+        return lax.dot_general(left, right, ACROSS, preferred_element_type=jnp.float32)
+
+    own = kept[0] + across(near, near_own[...]) + across(far, far_own[...])
+    other = kept[1] + across(near, near_other[...])
+    depth = far_other[0].shape[1]
+    for at, piece in enumerate(far_other):
+        other += across(far[:, at * depth : (at + 1) * depth], piece[...])
     first, second = jnp.where(core == 0, own, other), jnp.where(core == 0, other, own)
     stream = jnp.concatenate([first, second], axis=1).astype(jnp.bfloat16)
     half = stream.shape[0] // 2
@@ -227,35 +229,19 @@
     out_ref[1] = stream[half:]
 
 
-def project_near(taken, weight_own, weight_other, kept):
+def project(taken, near_own, near_other, far_own, far_other, kept):
     depth = taken.shape[2]
-    rows = kept.shape[1]
-    return pl.pallas_call(
-        project_near_kernel,
-        out_shape=(
-            jax.ShapeDtypeStruct(kept.shape, jnp.float32),
-            jax.ShapeDtypeStruct((rows, depth), taken.dtype),
-        ),
-        in_specs=vmem(4),
-        out_specs=tuple(vmem(2)),
+    rows, width = kept.shape[1:]
+    return pl.pallas_call(
+        project_kernel,
+        out_shape=jax.ShapeDtypeStruct((2, rows // 2, 2 * width), jnp.bfloat16),
+        in_specs=vmem(5 + len(far_other)),
+        out_specs=pl.BlockSpec(memory_space=pltpu.VMEM),
         scratch_shapes=[pltpu.VMEM((2, rows, depth), jnp.float32)],
         compiler_params=pltpu.CompilerParams(vmem_limit_bytes=16 * 1024 * 1024),
         cost_estimate=cost(2e-6),
-        name="project_near",
-    )(taken, weight_own, weight_other, kept)
-
-
-def project_far(far, weight_own, weight_other, near):
-    rows, width = near.shape[1:]
-    return pl.pallas_call(
-        project_far_kernel,
-        out_shape=jax.ShapeDtypeStruct((2, rows // 2, 2 * width), jnp.bfloat16),
-        in_specs=vmem(4),
-        out_specs=pl.BlockSpec(memory_space=pltpu.VMEM),
-        compiler_params=pltpu.CompilerParams(vmem_limit_bytes=16 * 1024 * 1024),
-        cost_estimate=cost(2e-6),
-        name="project_far",
-    )(far, weight_own, weight_other, near)
+        name="project",
+    )(taken, near_own, near_other, far_own, kept, *far_other)
 
 
 def pre_activations(rows, weights):
@@ -336,7 +322,7 @@
     for half in range(2):
         for b in range(16):
             at = half * 64 + b * 4
-            ordered[b, 4 * half : 4 * half + 4, :] = partial[at : at + 4, :]
+            ordered[15 - b, 4 * half : 4 * half + 4, :] = partial[at : at + 4, :]
     out_ref[...] = ordered[...].astype(jnp.bfloat16)
 
 
@@ -376,8 +362,8 @@
 
 def finish_kernel(parts, probe_bias, head_weight, head_bias, scores_ref, logits_ref):
     sums = parts[...].astype(jnp.float32)
-    first = jnp.sum(sums[:8], axis=0)
-    second = jnp.sum(sums[8:], axis=0)
+    first = jnp.sum(sums[8:], axis=0)
+    second = jnp.sum(sums[:8], axis=0)
     scores = first + jnp.concatenate([second[4:], second[:4]], axis=0) + probe_bias[...]
     scores_ref[...] = scores
     gated = scores / (1.0 + jnp.exp(-scores))
@@ -435,12 +421,13 @@
     kept_other = xor(kept, 1)
 
     sent = attend_shares(queries, key_cache, value_cache, new_key, new_value, lengths)
-    kept_rows, token = keep(kept, kept_other, (probe_other, bias_other, code_other))
-    taken = lax.all_to_all(sent, ALL, 0, 0, tiled=True)
-    proj_y = after(proj_y, taken, token)
-    proj_yc = xor(proj_y, 1)
-    near, far = project_near(taken, proj, proj_c, kept_rows)
-    stream = project_far(far, proj_y, proj_yc, near)
+    kept_rows, token = keep(kept, kept_other, ())
+    taken = lax.all_to_all(sent, ALL, 0, 0, tiled=True, axis_index_groups=[ODD_FIRST])
+    proj_y = after(proj_y, token)
+    depth = proj_y.shape[1] // 4
+    proj_yc = [xor(proj_y[:, at : at + depth], 1) for at in range(0, proj_y.shape[1], depth)]
+    taken = after(taken, *proj_yc, probe_other, bias_other, code_other)
+    stream = project(taken, proj, proj_c, proj_y, proj_yc, kept_rows)
     along_z = [stream, xor(stream, 4), xor(stream, 8), xor(stream, 12)]
 
     def spread(mine):
@@ -458,7 +445,7 @@
         (enc_bias[None], threshold_code[None], probe_weight),
         (bias_other[None], code_other[None], probe_other),
     )
-    parts = lax.all_to_all(partial, PLANE, 0, 0, tiled=True)
+    parts = lax.all_to_all(partial, ALL, 0, 0, tiled=True, axis_index_groups=PLANES)
     return finish(parts, probe_bias, head_weight, head_bias)
 
 

time: 63.5 us -> 61.7 us (0.972)
  starting transfers between devices: 24.4 us -> 21.7 us
  waiting for transfers between devices: 15.4 us -> 17.9 us
  blocking collectives: 11.6 us -> 10.1 us
    ppermute x19 -> x22, starting transfers between devices: 19.5 us -> 16.7 us  [xor(): return lax.ppermute(value, ALL, [(i, i ^ bits) for i in range(32)])]
    ppermute x19 -> x22, waiting for transfers between devices: 11.4 us -> 13.3 us  [xor(): return lax.ppermute(value, ALL, [(i, i ^ bits) for i in range(32)])]
    all_to_all x1, blocking collectives: 11.6 us -> 10.1 us  [chip_body(): lax.all_to_all(partial, ALL, 0, 0, tiled=True, axis_index_groups=PLANES)]
  transfers between devices with their start and end apart: 20 -> 23, of which waited for: 8 -> 10; matrix products, arithmetic and copies ran while one was open for 0% -> 0% of each run, Pallas kernels for 15% -> 15%
where the time goes in v5:
time: 61.7 us; the launch traced here: 61.4 us
  starting transfers between devices  21.7 us (35%)
  waiting for transfers between devices  17.9 us (29%)
  Pallas kernels  10.6 us (17%)
  blocking collectives  10.1 us (16%)
  between operations  0.86 us (1%)
    ppermute x22, starting transfers between devices, xor(): return lax.ppermute(value, ALL, [(i, i ^ bits) for i in range(32)])  16.7 us
    ppermute x22, waiting for transfers between devices, xor(): return lax.ppermute(value, ALL, [(i, i ^ bits) for i in range(32)])  13.3 us
    all_to_all x1, blocking collectives, chip_body(): lax.all_to_all(partial, ALL, 0, 0, tiled=True, axis_index_groups=PLANES)  10.1 us
    pallas_call x1, Pallas kernels, attend_shares(): pl.pallas_call(attend_kernel, out_shape=jax.ShapeDtypeStruct((32, 4, widt...  5.51 us
    all_to_all x1, starting transfers between devices, chip_body(): lax.all_to_all(sent, ALL, 0, 0, tiled=True, axis_index_groups=[ODD_FIRST])  5.01 us
    all_to_all x1, waiting for transfers between devices, chip_body(): lax.all_to_all(sent, ALL, 0, 0, tiled=True, axis_index_groups=[ODD_FIRST])  4.57 us
    pallas_call x1, Pallas kernels, encode_first(): pl.pallas_call(encode_first_kernel, out_shape=(jax.ShapeDtypeStruct((2, r...  2.43 us
  transfers between devices with their start and end apart: 23, of which 10 were waited for; matrix products, arithmetic and copies ran while one was open for 0% of the time, Pallas kernels for 15%

profile of v5, /device:TPU:0, one launch (start us, length us, event | category | flops | bytes accessed | tf_op | source)
XLA Modules:
  0.0 61.4 jit_solution(7687619702637452132)
XLA Ops:
  0.6 3.0 %collective-permute-start = (bf16[288,1024]{1,0:T(8,128)(2,1)}, bf16[288,1024]{1,0:T(8,128)(2,1)S(1)}, u32[]{:S(2)}, u32[]{:S(2)}) collective-permute-start(bf16[288,1024]{1,0:T(8,128)(2,1)} %bitcast.21), channel_id=1, source_target_pairs={{0,16},{1,17},{2,18},{3,19},{4,20},{5,21},{6,22},{7,23},{8,24},{9,... | collective-permute-start | bytes 1769480 | tf_op jit(solution)/shard_map/ppermute | solution.py:48
  3.7 0.0 collective-permute-start.21
  3.7 0.5 collective-permute-start.1
  4.2 0.0 collective-permute-start.9
  4.2 5.5 %attend.1 = bf16[32,4,1024]{2,1,0:T(4,128)(2,1)} custom-call(s32[16]{0:T(128)} %lengths.1, bf16[16,1024]{1,0:T(8,128)(2,1)} %queries.1, bf16[16,512]{1,0:T(8,128)(2,1)} %new_key.1, bf16[16,512]{1,0:T(8,128)(2,1)} %new_value.1, bf16[16,256,512]{2,1,0:T(8,128)(2,1)} %keys_at.1, bf16[16,256,512]{2,1,0:T(8,128)(2,1)} %values_at.1), custom_call_target="tpu_custom_call" | custom-call | bytes 44280000 | tf_op jit(solution)/shard_map/attend/pallas_call | solution.py:146
  9.7 0.0 copy-start.2
  9.7 0.0 copy-start.4
  9.7 0.0 copy-start.5
  9.7 0.0 copy-start
  9.7 5.0 %all-to-all-start = ((bf16[32,4,1024]{2,1,0:T(4,128)(2,1)}), bf16[32,4,1024]{2,1,0:T(4,128)(2,1)S(1)}, u32[]{:S(2)}, u32[]{:S(2)}) async-start(bf16[32,4,1024]{2,1,0:T(4,128)(2,1)} %attend.1), calls=%async_computation | async-start | bytes 524288 | tf_op jit(solution)/shard_map/all_to_all | solution.py:425
  14.8 0.0 collective-permute-done.1.kept_other
  14.8 0.0 copy-done.1
  14.8 0.3 keep.1
  15.1 2.1 %collective-permute-done.refs_0_ = bf16[288,1024]{1,0:T(8,128)(2,1)S(1)} collective-permute-done((bf16[288,1024]{1,0:T(8,128)(2,1)}, bf16[288,1024]{1,0:T(8,128)(2,1)S(1)}, u32[]{:S(2)}, u32[]{:S(2)}) %collective-permute-start) | collective-permute-done | bytes 589856 | tf_op jit(solution)/shard_map/ppermute | solution.py:48
  17.2 0.1 collective-permute-start.2
  17.3 0.0 copy-done.2
  17.3 0.5 collective-permute-start.6
  17.8 0.0 copy-done.4
  17.8 0.1 collective-permute-start.7
  17.9 1.1 %collective-permute-done.7.refs_6_ = f32[256]{0:T(256)S(1)} collective-permute-done((f32[256]{0:T(256)S(1)}, f32[256]{0:T(256)S(1)}, u32[]{:S(2)}, u32[]{:S(2)}) %collective-permute-start.7) | collective-permute-done | bytes 1056 | tf_op jit(solution)/shard_map/ppermute | solution.py:48
  19.0 0.2 collective-permute-start.8
  19.2 0.9 %collective-permute-done.8.refs_7_ = s32[256]{0:T(256)S(1)} collective-permute-done((s32[256]{0:T(256)S(1)}, s32[256]{0:T(256)S(1)}, u32[]{:S(2)}, u32[]{:S(2)}) %collective-permute-start.8) | collective-permute-done | bytes 1056 | tf_op jit(solution)/shard_map/ppermute | solution.py:48
  20.1 0.2 collective-permute-start.3
  20.3 0.0 collective-permute-done.6.refs_5_.probe_other
  20.3 0.3 collective-permute-start.4
  20.6 0.0 collective-permute-done.2.refs_1_.rest_0_
  20.6 0.2 collective-permute-start.5
  20.8 4.6 %all-to-all-done.refs_0_ = bf16[32,4,1024]{2,1,0:T(4,128)(2,1)S(1)} async-done(((bf16[32,4,1024]{2,1,0:T(4,128)(2,1)}), bf16[32,4,1024]{2,1,0:T(4,128)(2,1)S(1)}, u32[]{:S(2)}, u32[]{:S(2)}) %all-to-all-start) | async-done | bytes 262176 | tf_op jit(solution)/shard_map/all_to_all | solution.py:425
  25.4 0.0 collective-permute-done.3.refs_2_.rest_1_
  25.4 0.0 collective-permute-done.4.refs_3_.rest_2_
  25.4 0.0 collective-permute-done.5.refs_4_.rest_3_
  25.4 0.0 collective-permute-done.9.near_other
  25.5 0.9 %project.1 = bf16[2,32,576]{2,1,0:T(8,128)(2,1)S(1)} custom-call(bf16[32,4,1024]{2,1,0:T(4,128)(2,1)S(1)} %after.4.taken, bf16[288,1024]{1,0:T(8,128)(2,1)S(1)} %bitcast.23, bf16[288,1024]{1,0:T(8,128)(2,1)S(1)} %collective-permute-done.9.near_other, bf16[288,1024]{1,0:T(8,128)(2,1)S(1)} %after.3.far_own, f32[2,64,288]{2,1,0:T(8,128)S(1)} %get-tuple-element.7.kept, ...), custom_call_target="tpu_custom_call" | custom-call | bytes 7380000 | tf_op jit(solution)/shard_map/project/pallas_call | solution.py:235
  26.4 1.1 %collective-permute-start.10 = (bf16[2,32,576]{2,1,0:T(8,128)(2,1)S(1)}, bf16[2,32,576]{2,1,0:T(8,128)(2,1)S(1)}, u32[]{:S(2)}, u32[]{:S(2)}) collective-permute-start(bf16[2,32,576]{2,1,0:T(8,128)(2,1)S(1)} %project.1), channel_id=1, source_target_pairs={{0,4},{1,5},{2,6},{3,7},{4,0},{5,1},{6,2},{7,3},{8,12},{9,13},{10,... | collective-permute-start | bytes 221192 | tf_op jit(solution)/shard_map/ppermute | solution.py:48
  27.5 1.1 %collective-permute-start.15 = (bf16[2,32,576]{2,1,0:T(8,128)(2,1)S(1)}, bf16[2,32,576]{2,1,0:T(8,128)(2,1)S(1)}, u32[]{:S(2)}, u32[]{:S(2)}) collective-permute-start(bf16[2,32,576]{2,1,0:T(8,128)(2,1)S(1)} %project.1), channel_id=1, source_target_pairs={{0,8},{1,9},{2,10},{3,11},{4,12},{5,13},{6,14},{7,15},{8,0},{9,1},... | collective-permute-start | bytes 221192 | tf_op jit(solution)/shard_map/ppermute | solution.py:48
  28.7 2.2 %collective-permute-start.16 = (bf16[2,32,576]{2,1,0:T(8,128)(2,1)S(1)}, bf16[2,32,576]{2,1,0:T(8,128)(2,1)S(1)}, u32[]{:S(2)}, u32[]{:S(2)}) collective-permute-start(bf16[2,32,576]{2,1,0:T(8,128)(2,1)S(1)} %project.1), channel_id=1, source_target_pairs={{0,12},{1,13},{2,14},{3,15},{4,8},{5,9},{6,10},{7,11},{8,4},{9,5},... | collective-permute-start | bytes 221192 | tf_op jit(solution)/shard_map/ppermute | solution.py:48
  30.9 1.2 %collective-permute-done.10 = bf16[2,32,576]{2,1,0:T(8,128)(2,1)S(1)} collective-permute-done((bf16[2,32,576]{2,1,0:T(8,128)(2,1)S(1)}, bf16[2,32,576]{2,1,0:T(8,128)(2,1)S(1)}, u32[]{:S(2)}, u32[]{:S(2)}) %collective-permute-start.10) | collective-permute-done | bytes 73760 | tf_op jit(solution)/shard_map/ppermute | solution.py:48
  32.1 0.5 collective-permute-start.11
  32.6 0.7 %collective-permute-start.13 = (bf16[2,2,32,576]{3,2,1,0:T(8,128)(2,1)S(1)}, bf16[2,2,32,576]{3,2,1,0:T(8,128)(2,1)S(1)}, u32[]{:S(2)}, u32[]{:S(2)}) collective-permute-start(bf16[2,2,32,576]{3,2,1,0:T(8,128)(2,1)S(1)} %pad_maximum_fusion.own), channel_id=1, source_target_pairs={{0,16},{1,17},{2,18},{3,19},{4,20},{5,21},{6,22},{7,23},{8,24},{9,... | collective-permute-start | bytes 442376 | tf_op jit(solution)/shard_map/ppermute | solution.py:48
  33.3 3.2 %collective-permute-done.15 = bf16[2,32,576]{2,1,0:T(8,128)(2,1)S(1)} collective-permute-done((bf16[2,32,576]{2,1,0:T(8,128)(2,1)S(1)}, bf16[2,32,576]{2,1,0:T(8,128)(2,1)S(1)}, u32[]{:S(2)}, u32[]{:S(2)}) %collective-permute-start.15) | collective-permute-done | bytes 73760 | tf_op jit(solution)/shard_map/ppermute | solution.py:48
  36.6 0.0 collective-permute-done.16
  36.6 1.2 %collective-permute-done.11.refs_1_.own = bf16[2,2,32,576]{3,2,1,0:T(8,128)(2,1)S(1)} collective-permute-done((bf16[2,2,32,576]{3,2,1,0:T(8,128)(2,1)S(1)}, bf16[2,2,32,576]{3,2,1,0:T(8,128)(2,1)S(1)}, u32[]{:S(2)}, u32[]{:S(2)}) %collective-permute-start.11) | collective-permute-done | bytes 147488 | tf_op jit(solution)/shard_map/ppermute | solution.py:48
  37.8 0.7 %collective-permute-start.19 = (bf16[2,2,32,576]{3,2,1,0:T(8,128)(2,1)S(1)}, bf16[2,2,32,576]{3,2,1,0:T(8,128)(2,1)S(1)}, u32[]{:S(2)}, u32[]{:S(2)}) collective-permute-start(bf16[2,2,32,576]{3,2,1,0:T(8,128)(2,1)S(1)} %after.5.own_far), channel_id=1, source_target_pairs={{0,16},{1,17},{2,18},{3,19},{4,20},{5,21},{6,22},{7,23},{8,24},{9,... | collective-permute-start | bytes 442376 | tf_op jit(solution)/shard_map/ppermute | solution.py:48
  38.6 0.6 %collective-permute-start.17 = (bf16[2,2,32,576]{3,2,1,0:T(8,128)(2,1)S(1)}, bf16[2,2,32,576]{3,2,1,0:T(8,128)(2,1)S(1)}, u32[]{:S(2)}, u32[]{:S(2)}) collective-permute-start(bf16[2,2,32,576]{3,2,1,0:T(8,128)(2,1)S(1)} %after.5.own_far), channel_id=1, source_target_pairs={{0,2},{1,3},{2,0},{3,1},{4,6},{5,7},{6,4},{7,5},{8,10},{9,11},{10,... | collective-permute-start | bytes 442376 | tf_op jit(solution)/shard_map/ppermute | solution.py:48
  39.2 1.0 %collective-permute-start.12 = (bf16[2,32,576]{2,1,0:T(8,128)(2,1)S(1)}, bf16[2,32,576]{2,1,0:T(8,128)(2,1)S(1)}, u32[]{:S(2)}, u32[]{:S(2)}) collective-permute-start(bf16[2,32,576]{2,1,0:T(8,128)(2,1)S(1)} %slice_bitcast_fusion.3), channel_id=1, source_target_pairs={{0,16},{1,17},{2,18},{3,19},{4,20},{5,21},{6,22},{7,23},{8,24},{9,... | collective-permute-start | bytes 221192 | tf_op jit(solution)/shard_map/ppermute | solution.py:48
  40.2 0.0 collective-permute-done.13.other
  40.3 1.8 %collective-permute-start.14 = (bf16[2,32,576]{2,1,0:T(8,128)(2,1)S(1)}, bf16[2,32,576]{2,1,0:T(8,128)(2,1)S(1)}, u32[]{:S(2)}, u32[]{:S(2)}) collective-permute-start(bf16[2,32,576]{2,1,0:T(8,128)(2,1)S(1)} %slice_bitcast_fusion.2), channel_id=1, source_target_pairs={{0,2},{1,3},{2,0},{3,1},{4,6},{5,7},{6,4},{7,5},{8,10},{9,11},{10,... | collective-permute-start | bytes 221192 | tf_op jit(solution)/shard_map/ppermute | solution.py:48
  42.1 1.8 %collective-permute-done.17.own_far = bf16[2,2,32,576]{3,2,1,0:T(8,128)(2,1)S(1)} collective-permute-done((bf16[2,2,32,576]{3,2,1,0:T(8,128)(2,1)S(1)}, bf16[2,2,32,576]{3,2,1,0:T(8,128)(2,1)S(1)}, u32[]{:S(2)}, u32[]{:S(2)}) %collective-permute-start.17) | collective-permute-done | bytes 147488 | tf_op jit(solution)/shard_map/ppermute | solution.py:48
  43.9 1.4 %collective-permute-start.18 = (bf16[2,32,576]{2,1,0:T(8,128)(2,1)S(1)}, bf16[2,32,576]{2,1,0:T(8,128)(2,1)S(1)}, u32[]{:S(2)}, u32[]{:S(2)}) collective-permute-start(bf16[2,32,576]{2,1,0:T(8,128)(2,1)S(1)} %slice_bitcast_fusion.1), channel_id=1, source_target_pairs={{0,16},{1,17},{2,18},{3,19},{4,20},{5,21},{6,22},{7,23},{8,24},{9,... | collective-permute-start | bytes 221192 | tf_op jit(solution)/shard_map/ppermute | solution.py:48
  45.3 0.0 collective-permute-done.19.other_far
  45.3 0.3 collective-permute-start.20
  45.7 0.0 collective-permute-done.21.enc_other
  45.7 2.4 %encode_first.1 = (f32[2,128,256]{2,1,0:T(8,128)S(1)}, bf16[2,4,576,256]{3,2,1,0:T(8,128)(2,1)S(1)}) custom-call(bf16[2,2,32,576]{3,2,1,0:T(8,128)(2,1)S(1)} %pad_maximum_fusion.own, bf16[2,2,32,576]{3,2,1,0:T(8,128)(2,1)S(1)} %collective-permute-done.13.other, bf16[2,2,32,576]{3,2,1,0:T(8,128)(2,1)S(1)} %after.5.own_far, ...), custom_call_target="tpu_custom_call" | custom-call | bytes 7380000 | tf_op jit(solution)/shard_map/encode_first/pallas_call | solution.py:334
  48.1 0.0 copy-start.3
  48.1 0.0 copy-start.6
  48.1 0.0 copy-start.7
  48.1 0.0 collective-permute-done.12.upper
  48.2 0.0 collective-permute-done.14.lower
  48.2 0.2 collective-permute-done.18.upper_far
  48.4 1.4 %collective-permute-done.20.lower_far = bf16[2,32,576]{2,1,0:T(8,128)(2,1)S(1)} collective-permute-done((bf16[2,32,576]{2,1,0:T(8,128)(2,1)S(1)}, bf16[2,32,576]{2,1,0:T(8,128)(2,1)S(1)}, u32[]{:S(2)}, u32[]{:S(2)}) %collective-permute-start.20) | collective-permute-done | bytes 73760 | tf_op jit(solution)/shard_map/ppermute | solution.py:48
  49.8 0.7 %encode_second.1 = bf16[16,8,256]{2,1,0:T(8,128)(2,1)S(1)} custom-call(bf16[2,2,32,576]{3,2,1,0:T(8,128)(2,1)S(1)} %collective-permute-done.11.refs_1_.own, bf16[2,32,576]{2,1,0:T(8,128)(2,1)S(1)} %collective-permute-done.12.upper, bf16[2,32,576]{2,1,0:T(8,128)(2,1)S(1)} %collective-permute-done.14.lower, ...), custom_call_target="tpu_custom_call" | custom-call | bytes 7380000 | tf_op jit(solution)/shard_map/encode_second/pallas_call | solution.py:351
  50.5 10.1 %all_to_all.10.parts = bf16[16,8,256]{2,1,0:T(8,128)(2,1)S(1)} all-to-all(bf16[16,8,256]{2,1,0:T(8,128)(2,1)S(1)} %encode_second.1), channel_id=1, replica_groups={{30,28,26,24,22,20,18,16,14,12,10,8,6,4,2,0},{31,29,27,25,23,21,19,17,1..., dimensions={0} | all-to-all | bytes 131072 | tf_op jit(solution)/shard_map/all_to_all | solution.py:448
  60.6 0.0 copy-done.6
  60.7 0.8 %finish.1 = (f32[8,256]{1,0:T(8,128)}, f32[8,16]{1,0:T(8,128)}) custom-call(bf16[16,8,256]{2,1,0:T(8,128)(2,1)S(1)} %all_to_all.10.parts, f32[1,256]{1,0:T(1,128)S(1)} %bitcast.32, f32[16,256]{1,0:T(8,128)S(1)} %bitcast.27, f32[1,16]{1,0:T(1,128)S(1)} %bitcast.33), custom_call_target="tpu_custom_call" | custom-call | tf_op jit(solution)/shard_map/finish/pallas_call | solution.py:384
  (15 shorter events, 0.1 us)
Async XLA Ops:
  0.6 16.6 %collective-permute-start = (bf16[288,1024]{1,0:T(8,128)(2,1)}, bf16[288,1024]{1,0:T(8,128)(2,1)S(1)}, u32[]{:S(2)}, u32[]{:S(2)}) collective-permute-start(bf16[288,1024]{1,0:T(8,128)(2,1)} %bitcast.21), channel_id=1, source_target_pairs={{0,16},{1,17},{2,18},{3,19},{4,20},{5,21},{6,22},{7,23},{8,24},{9,... | collective-permute-start | bytes 1769480 | tf_op jit(solution)/shard_map/ppermute | solution.py:48
  3.7 42.0 %collective-permute-start.21 = (bf16[4608,256]{1,0:T(8,128)(2,1)}, bf16[4608,256]{1,0:T(8,128)(2,1)}, u32[]{:S(2)}, u32[]{:S(2)}) collective-permute-start(bf16[4608,256]{1,0:T(8,128)(2,1)} %enc_own.1), channel_id=1, source_target_pairs={{0,1},{1,0},{2,3},{3,2},{4,5},{5,4},{6,7},{7,6},{8,9},{9,8},{10,11... | collective-permute-start | bytes 7077896 | tf_op jit(solution)/shard_map/ppermute | solution.py:48
  3.7 11.1 %copy-start.1 = (bf16[256,288]{0,1:T(8,128)(2,1)S(1)}, bf16[256,288]{0,1:T(8,128)(2,1)}, u32[]{:S(2)}) copy-start(bf16[256,288]{0,1:T(8,128)(2,1)} %param.22) | copy-start | bytes 442372
  3.7 11.1 %collective-permute-start.1 = (bf16[288,256]{1,0:T(8,128)(2,1)}, bf16[288,256]{1,0:T(8,128)(2,1)S(1)}, u32[]{:S(2)}, u32[]{:S(2)}) collective-permute-start(bf16[288,256]{1,0:T(8,128)(2,1)} %bitcast.25), channel_id=1, source_target_pairs={{0,1},{1,0},{2,3},{3,2},{4,5},{5,4},{6,7},{7,6},{8,9},{9,8},{10,11... | collective-permute-start | bytes 442376 | tf_op jit(solution)/shard_map/ppermute | solution.py:48
  4.2 21.3 %collective-permute-start.9 = (bf16[288,1024]{1,0:T(8,128)(2,1)}, bf16[288,1024]{1,0:T(8,128)(2,1)S(1)}, u32[]{:S(2)}, u32[]{:S(2)}) collective-permute-start(bf16[288,1024]{1,0:T(8,128)(2,1)} %bitcast.22), channel_id=1, source_target_pairs={{0,1},{1,0},{2,3},{3,2},{4,5},{5,4},{6,7},{7,6},{8,9},{9,8},{10,11... | collective-permute-start | bytes 1769480 | tf_op jit(solution)/shard_map/ppermute | solution.py:48
  9.7 7.6 %copy-start.2 = (bf16[256,256]{1,0:T(8,128)(2,1)S(1)}, bf16[256,256]{1,0:T(8,128)(2,1)}, u32[]{:S(2)}) copy-start(bf16[256,256]{1,0:T(8,128)(2,1)} %probe_own.1) | copy-start | bytes 393220
  9.7 8.1 %copy-start.4 = (f32[256]{0:T(256)S(1)}, f32[256]{0:T(256)}, u32[]{:S(2)}) copy-start(f32[256]{0:T(256)} %param.24) | copy-start | bytes 3076
  9.7 9.3 %copy-start.5 = (s32[256]{0:T(256)S(1)}, s32[256]{0:T(256)}, u32[]{:S(2)}) copy-start(s32[256]{0:T(256)} %param.25) | copy-start | bytes 3076
  9.7 15.7 %copy-start = (bf16[1024,288]{0,1:T(8,128)(2,1)S(1)}, bf16[1024,288]{0,1:T(8,128)(2,1)}, u32[]{:S(2)}) copy-start(bf16[1024,288]{0,1:T(8,128)(2,1)} %param.21) | copy-start | bytes 1769476
  9.7 15.7 %all-to-all-start = ((bf16[32,4,1024]{2,1,0:T(4,128)(2,1)}), bf16[32,4,1024]{2,1,0:T(4,128)(2,1)S(1)}, u32[]{:S(2)}, u32[]{:S(2)}) async-start(bf16[32,4,1024]{2,1,0:T(4,128)(2,1)} %attend.1), calls=%async_computation | async-start | bytes 524288 | tf_op jit(solution)/shard_map/all_to_all | solution.py:425
  17.2 3.4 %collective-permute-start.2 = (bf16[288,256]{1,0:T(8,128)(2,1)S(1)}, bf16[288,256]{1,0:T(8,128)(2,1)S(1)}, u32[]{:S(2)}, u32[]{:S(2)}) collective-permute-start(bf16[288,256]{1,0:T(8,128)(2,1)S(1)} %get-tuple-element.13), channel_id=1, source_target_pairs={{0,1},{1,0},{2,3},{3,2},{4,5},{5,4},{6,7},{7,6},{8,9},{9,8},{10,11... | collective-permute-start | bytes 442376 | tf_op jit(solution)/shard_map/ppermute | solution.py:48
  17.3 3.0 %collective-permute-start.6 = (bf16[256,256]{1,0:T(8,128)(2,1)S(1)}, bf16[256,256]{1,0:T(8,128)(2,1)S(1)}, u32[]{:S(2)}, u32[]{:S(2)}) collective-permute-start(bf16[256,256]{1,0:T(8,128)(2,1)S(1)} %copy-done.2), channel_id=1, source_target_pairs={{0,1},{1,0},{2,3},{3,2},{4,5},{5,4},{6,7},{7,6},{8,9},{9,8},{10,11... | collective-permute-start | bytes 393224 | tf_op jit(solution)/shard_map/ppermute | solution.py:48
  17.8 1.1 %collective-permute-start.7 = (f32[256]{0:T(256)S(1)}, f32[256]{0:T(256)S(1)}, u32[]{:S(2)}, u32[]{:S(2)}) collective-permute-start(f32[256]{0:T(256)S(1)} %copy-done.4), channel_id=1, source_target_pairs={{0,1},{1,0},{2,3},{3,2},{4,5},{5,4},{6,7},{7,6},{8,9},{9,8},{10,11... | collective-permute-start | bytes 3080 | tf_op jit(solution)/shard_map/ppermute | solution.py:48
  19.0 1.1 %collective-permute-start.8 = (s32[256]{0:T(256)S(1)}, s32[256]{0:T(256)S(1)}, u32[]{:S(2)}, u32[]{:S(2)}) collective-permute-start(s32[256]{0:T(256)S(1)} %copy-done.5), channel_id=1, source_target_pairs={{0,1},{1,0},{2,3},{3,2},{4,5},{5,4},{6,7},{7,6},{8,9},{9,8},{10,11... | collective-permute-start | bytes 3080 | tf_op jit(solution)/shard_map/ppermute | solution.py:48
  20.1 5.3 %collective-permute-start.3 = (bf16[288,256]{1,0:T(8,128)(2,1)S(1)}, bf16[288,256]{1,0:T(8,128)(2,1)S(1)}, u32[]{:S(2)}, u32[]{:S(2)}) collective-permute-start(bf16[288,256]{1,0:T(8,128)(2,1)S(1)} %get-tuple-element.12), channel_id=1, source_target_pairs={{0,1},{1,0},{2,3},{3,2},{4,5},{5,4},{6,7},{7,6},{8,9},{9,8},{10,11... | collective-permute-start | bytes 442376 | tf_op jit(solution)/shard_map/ppermute | solution.py:48
  20.3 5.1 %collective-permute-start.4 = (bf16[288,256]{1,0:T(8,128)(2,1)S(1)}, bf16[288,256]{1,0:T(8,128)(2,1)S(1)}, u32[]{:S(2)}, u32[]{:S(2)}) collective-permute-start(bf16[288,256]{1,0:T(8,128)(2,1)S(1)} %get-tuple-element.11), channel_id=1, source_target_pairs={{0,1},{1,0},{2,3},{3,2},{4,5},{5,4},{6,7},{7,6},{8,9},{9,8},{10,11... | collective-permute-start | bytes 442376 | tf_op jit(solution)/shard_map/ppermute | solution.py:48
  20.6 4.8 %collective-permute-start.5 = (bf16[288,256]{1,0:T(8,128)(2,1)S(1)}, bf16[288,256]{1,0:T(8,128)(2,1)S(1)}, u32[]{:S(2)}, u32[]{:S(2)}) collective-permute-start(bf16[288,256]{1,0:T(8,128)(2,1)S(1)} %get-tuple-element.10), channel_id=1, source_target_pairs={{0,1},{1,0},{2,3},{3,2},{4,5},{5,4},{6,7},{7,6},{8,9},{9,8},{10,11... | collective-permute-start | bytes 442376 | tf_op jit(solution)/shard_map/ppermute | solution.py:48
  26.4 5.7 %collective-permute-start.10 = (bf16[2,32,576]{2,1,0:T(8,128)(2,1)S(1)}, bf16[2,32,576]{2,1,0:T(8,128)(2,1)S(1)}, u32[]{:S(2)}, u32[]{:S(2)}) collective-permute-start(bf16[2,32,576]{2,1,0:T(8,128)(2,1)S(1)} %project.1), channel_id=1, source_target_pairs={{0,4},{1,5},{2,6},{3,7},{4,0},{5,1},{6,2},{7,3},{8,12},{9,13},{10,... | collective-permute-start | bytes 221192 | tf_op jit(solution)/shard_map/ppermute | solution.py:48
  27.5 9.1 %collective-permute-start.15 = (bf16[2,32,576]{2,1,0:T(8,128)(2,1)S(1)}, bf16[2,32,576]{2,1,0:T(8,128)(2,1)S(1)}, u32[]{:S(2)}, u32[]{:S(2)}) collective-permute-start(bf16[2,32,576]{2,1,0:T(8,128)(2,1)S(1)} %project.1), channel_id=1, source_target_pairs={{0,8},{1,9},{2,10},{3,11},{4,12},{5,13},{6,14},{7,15},{8,0},{9,1},... | collective-permute-start | bytes 221192 | tf_op jit(solution)/shard_map/ppermute | solution.py:48
  28.7 7.9 %collective-permute-start.16 = (bf16[2,32,576]{2,1,0:T(8,128)(2,1)S(1)}, bf16[2,32,576]{2,1,0:T(8,128)(2,1)S(1)}, u32[]{:S(2)}, u32[]{:S(2)}) collective-permute-start(bf16[2,32,576]{2,1,0:T(8,128)(2,1)S(1)} %project.1), channel_id=1, source_target_pairs={{0,12},{1,13},{2,14},{3,15},{4,8},{5,9},{6,10},{7,11},{8,4},{9,5},... | collective-permute-start | bytes 221192 | tf_op jit(solution)/shard_map/ppermute | solution.py:48
  32.1 5.7 %collective-permute-start.11 = (bf16[2,2,32,576]{3,2,1,0:T(8,128)(2,1)S(1)}, bf16[2,2,32,576]{3,2,1,0:T(8,128)(2,1)S(1)}, u32[]{:S(2)}, u32[]{:S(2)}) collective-permute-start(bf16[2,2,32,576]{3,2,1,0:T(8,128)(2,1)S(1)} %pad_maximum_fusion.own), channel_id=1, source_target_pairs={{0,2},{1,3},{2,0},{3,1},{4,6},{5,7},{6,4},{7,5},{8,10},{9,11},{10,... | collective-permute-start | bytes 442376 | tf_op jit(solution)/shard_map/ppermute | solution.py:48
  32.6 7.6 %collective-permute-start.13 = (bf16[2,2,32,576]{3,2,1,0:T(8,128)(2,1)S(1)}, bf16[2,2,32,576]{3,2,1,0:T(8,128)(2,1)S(1)}, u32[]{:S(2)}, u32[]{:S(2)}) collective-permute-start(bf16[2,2,32,576]{3,2,1,0:T(8,128)(2,1)S(1)} %pad_maximum_fusion.own), channel_id=1, source_target_pairs={{0,16},{1,17},{2,18},{3,19},{4,20},{5,21},{6,22},{7,23},{8,24},{9,... | collective-permute-start | bytes 442376 | tf_op jit(solution)/shard_map/ppermute | solution.py:48
  37.8 7.5 %collective-permute-start.19 = (bf16[2,2,32,576]{3,2,1,0:T(8,128)(2,1)S(1)}, bf16[2,2,32,576]{3,2,1,0:T(8,128)(2,1)S(1)}, u32[]{:S(2)}, u32[]{:S(2)}) collective-permute-start(bf16[2,2,32,576]{3,2,1,0:T(8,128)(2,1)S(1)} %after.5.own_far), channel_id=1, source_target_pairs={{0,16},{1,17},{2,18},{3,19},{4,20},{5,21},{6,22},{7,23},{8,24},{9,... | collective-permute-start | bytes 442376 | tf_op jit(solution)/shard_map/ppermute | solution.py:48
  38.6 5.3 %collective-permute-start.17 = (bf16[2,2,32,576]{3,2,1,0:T(8,128)(2,1)S(1)}, bf16[2,2,32,576]{3,2,1,0:T(8,128)(2,1)S(1)}, u32[]{:S(2)}, u32[]{:S(2)}) collective-permute-start(bf16[2,2,32,576]{3,2,1,0:T(8,128)(2,1)S(1)} %after.5.own_far), channel_id=1, source_target_pairs={{0,2},{1,3},{2,0},{3,1},{4,6},{5,7},{6,4},{7,5},{8,10},{9,11},{10,... | collective-permute-start | bytes 442376 | tf_op jit(solution)/shard_map/ppermute | solution.py:48
  39.2 8.9 %collective-permute-start.12 = (bf16[2,32,576]{2,1,0:T(8,128)(2,1)S(1)}, bf16[2,32,576]{2,1,0:T(8,128)(2,1)S(1)}, u32[]{:S(2)}, u32[]{:S(2)}) collective-permute-start(bf16[2,32,576]{2,1,0:T(8,128)(2,1)S(1)} %slice_bitcast_fusion.3), channel_id=1, source_target_pairs={{0,16},{1,17},{2,18},{3,19},{4,20},{5,21},{6,22},{7,23},{8,24},{9,... | collective-permute-start | bytes 221192 | tf_op jit(solution)/shard_map/ppermute | solution.py:48
  40.3 7.9 %collective-permute-start.14 = (bf16[2,32,576]{2,1,0:T(8,128)(2,1)S(1)}, bf16[2,32,576]{2,1,0:T(8,128)(2,1)S(1)}, u32[]{:S(2)}, u32[]{:S(2)}) collective-permute-start(bf16[2,32,576]{2,1,0:T(8,128)(2,1)S(1)} %slice_bitcast_fusion.2), channel_id=1, source_target_pairs={{0,2},{1,3},{2,0},{3,1},{4,6},{5,7},{6,4},{7,5},{8,10},{9,11},{10,... | collective-permute-start | bytes 221192 | tf_op jit(solution)/shard_map/ppermute | solution.py:48
  43.9 4.5 %collective-permute-start.18 = (bf16[2,32,576]{2,1,0:T(8,128)(2,1)S(1)}, bf16[2,32,576]{2,1,0:T(8,128)(2,1)S(1)}, u32[]{:S(2)}, u32[]{:S(2)}) collective-permute-start(bf16[2,32,576]{2,1,0:T(8,128)(2,1)S(1)} %slice_bitcast_fusion.1), channel_id=1, source_target_pairs={{0,16},{1,17},{2,18},{3,19},{4,20},{5,21},{6,22},{7,23},{8,24},{9,... | collective-permute-start | bytes 221192 | tf_op jit(solution)/shard_map/ppermute | solution.py:48
  45.3 4.5 %collective-permute-start.20 = (bf16[2,32,576]{2,1,0:T(8,128)(2,1)S(1)}, bf16[2,32,576]{2,1,0:T(8,128)(2,1)S(1)}, u32[]{:S(2)}, u32[]{:S(2)}) collective-permute-start(bf16[2,32,576]{2,1,0:T(8,128)(2,1)S(1)} %slice_bitcast_fusion), channel_id=1, source_target_pairs={{0,2},{1,3},{2,0},{3,1},{4,6},{5,7},{6,4},{7,5},{8,10},{9,11},{10,... | collective-permute-start | bytes 221192 | tf_op jit(solution)/shard_map/ppermute | solution.py:48
  48.1 12.5 %copy-start.3 = (f32[256,16]{0,1:T(8,128)S(1)}, f32[256,16]{0,1:T(8,128)}, u32[]{:S(2)}) copy-start(f32[256,16]{0,1:T(8,128)} %param.28) | copy-start | bytes 49156
  48.1 12.5 %copy-start.6 = (f32[256]{0:T(256)S(1)}, f32[256]{0:T(256)}, u32[]{:S(2)}) copy-start(f32[256]{0:T(256)} %param.27) | copy-start | bytes 3076
  48.1 12.5 %copy-start.7 = (f32[16]{0:T(128)S(1)}, f32[16]{0:T(128)}, u32[]{:S(2)}) copy-start(f32[16]{0:T(128)} %param.29) | copy-start | bytes 196

commit v6 on v5

--- a/solution.py
+++ b/solution.py
@@ -14,7 +14,7 @@
 ACROSS = (((1,), (1,)), ((), ()))
 
 ALL = ("y", "z", "x", "c")
-ODD_FIRST = [*range(1, 32, 2), *range(0, 32, 2)]
+ORDER = [*range(1, 32, 2), *range(0, 32, 2)]
 PLANES = [list(range(30 + core, -1, -2)) for core in range(2)]
 
 
@@ -422,7 +422,7 @@
 
     sent = attend_shares(queries, key_cache, value_cache, new_key, new_value, lengths)
     kept_rows, token = keep(kept, kept_other, ())
-    taken = lax.all_to_all(sent, ALL, 0, 0, tiled=True, axis_index_groups=[ODD_FIRST])
+    taken = lax.all_to_all(sent, ALL, 0, 0, tiled=True, axis_index_groups=[ORDER])
     proj_y = after(proj_y, token)
     depth = proj_y.shape[1] // 4
     proj_yc = [xor(proj_y[:, at : at + depth], 1) for at in range(0, proj_y.shape[1], depth)]

time: 61.7 us -> 61.7 us (level)
  no operation moved by 1% of the time
where the time goes in v6:
time: 61.7 us; the launch traced here: 61.4 us
  starting transfers between devices  21.7 us (35%)
  waiting for transfers between devices  17.9 us (29%)
  Pallas kernels  10.6 us (17%)
  blocking collectives  10.1 us (16%)
  between operations  0.86 us (1%)
    ppermute x22, starting transfers between devices, xor(): return lax.ppermute(value, ALL, [(i, i ^ bits) for i in range(32)])  16.7 us
    ppermute x22, waiting for transfers between devices, xor(): return lax.ppermute(value, ALL, [(i, i ^ bits) for i in range(32)])  13.3 us
    all_to_all x1, blocking collectives, chip_body(): lax.all_to_all(partial, ALL, 0, 0, tiled=True, axis_index_groups=PLANES)  10.1 us
    pallas_call x1, Pallas kernels, attend_shares(): pl.pallas_call(attend_kernel, out_shape=jax.ShapeDtypeStruct((32, 4, widt...  5.51 us
    all_to_all x1, starting transfers between devices, chip_body(): lax.all_to_all(sent, ALL, 0, 0, tiled=True, axis_index_groups=[ORDER])  5.01 us
    all_to_all x1, waiting for transfers between devices, chip_body(): lax.all_to_all(sent, ALL, 0, 0, tiled=True, axis_index_groups=[ORDER])  4.57 us
    pallas_call x1, Pallas kernels, encode_first(): pl.pallas_call(encode_first_kernel, out_shape=(jax.ShapeDtypeStruct((2, r...  2.43 us
  transfers between devices with their start and end apart: 23, of which 10 were waited for; matrix products, arithmetic and copies ran while one was open for 0% of the time, Pallas kernels for 15%

profile of v6, /device:TPU:0, one launch (start us, length us, event | category | flops | bytes accessed | tf_op | source)
XLA Modules:
  0.0 61.4 jit_solution(7687619702637452132)
XLA Ops:
  0.6 3.0 %collective-permute-start = (bf16[288,1024]{1,0:T(8,128)(2,1)}, bf16[288,1024]{1,0:T(8,128)(2,1)S(1)}, u32[]{:S(2)}, u32[]{:S(2)}) collective-permute-start(bf16[288,1024]{1,0:T(8,128)(2,1)} %bitcast.21), channel_id=1, source_target_pairs={{0,16},{1,17},{2,18},{3,19},{4,20},{5,21},{6,22},{7,23},{8,24},{9,... | collective-permute-start | bytes 1769480 | tf_op jit(solution)/shard_map/ppermute | solution.py:48
  3.7 0.0 collective-permute-start.21
  3.7 0.5 collective-permute-start.1
  4.2 0.0 collective-permute-start.9
  4.2 5.5 %attend.1 = bf16[32,4,1024]{2,1,0:T(4,128)(2,1)} custom-call(s32[16]{0:T(128)} %lengths.1, bf16[16,1024]{1,0:T(8,128)(2,1)} %queries.1, bf16[16,512]{1,0:T(8,128)(2,1)} %new_key.1, bf16[16,512]{1,0:T(8,128)(2,1)} %new_value.1, bf16[16,256,512]{2,1,0:T(8,128)(2,1)} %keys_at.1, bf16[16,256,512]{2,1,0:T(8,128)(2,1)} %values_at.1), custom_call_target="tpu_custom_call" | custom-call | bytes 44280000 | tf_op jit(solution)/shard_map/attend/pallas_call | solution.py:146
  9.7 0.0 copy-start.2
  9.7 0.0 copy-start.4
  9.7 0.0 copy-start.5
  9.7 0.0 copy-start
  9.7 5.0 %all-to-all-start = ((bf16[32,4,1024]{2,1,0:T(4,128)(2,1)}), bf16[32,4,1024]{2,1,0:T(4,128)(2,1)S(1)}, u32[]{:S(2)}, u32[]{:S(2)}) async-start(bf16[32,4,1024]{2,1,0:T(4,128)(2,1)} %attend.1), calls=%async_computation | async-start | bytes 524288 | tf_op jit(solution)/shard_map/all_to_all | solution.py:425
  14.8 0.0 collective-permute-done.1.kept_other
  14.8 0.0 copy-done.1
  14.8 0.3 keep.1
  15.1 2.1 %collective-permute-done.refs_0_ = bf16[288,1024]{1,0:T(8,128)(2,1)S(1)} collective-permute-done((bf16[288,1024]{1,0:T(8,128)(2,1)}, bf16[288,1024]{1,0:T(8,128)(2,1)S(1)}, u32[]{:S(2)}, u32[]{:S(2)}) %collective-permute-start) | collective-permute-done | bytes 589856 | tf_op jit(solution)/shard_map/ppermute | solution.py:48
  17.2 0.1 collective-permute-start.2
  17.3 0.0 copy-done.2
  17.3 0.5 collective-permute-start.6
  17.8 0.0 copy-done.4
  17.8 0.1 collective-permute-start.7
  17.9 1.1 %collective-permute-done.7.refs_6_ = f32[256]{0:T(256)S(1)} collective-permute-done((f32[256]{0:T(256)S(1)}, f32[256]{0:T(256)S(1)}, u32[]{:S(2)}, u32[]{:S(2)}) %collective-permute-start.7) | collective-permute-done | bytes 1056 | tf_op jit(solution)/shard_map/ppermute | solution.py:48
  19.0 0.2 collective-permute-start.8
  19.2 0.9 %collective-permute-done.8.refs_7_ = s32[256]{0:T(256)S(1)} collective-permute-done((s32[256]{0:T(256)S(1)}, s32[256]{0:T(256)S(1)}, u32[]{:S(2)}, u32[]{:S(2)}) %collective-permute-start.8) | collective-permute-done | bytes 1056 | tf_op jit(solution)/shard_map/ppermute | solution.py:48
  20.1 0.2 collective-permute-start.3
  20.3 0.0 collective-permute-done.6.refs_5_.probe_other
  20.3 0.3 collective-permute-start.4
  20.6 0.0 collective-permute-done.2.refs_1_.rest_0_
  20.6 0.2 collective-permute-start.5
  20.8 4.6 %all-to-all-done.refs_0_ = bf16[32,4,1024]{2,1,0:T(4,128)(2,1)S(1)} async-done(((bf16[32,4,1024]{2,1,0:T(4,128)(2,1)}), bf16[32,4,1024]{2,1,0:T(4,128)(2,1)S(1)}, u32[]{:S(2)}, u32[]{:S(2)}) %all-to-all-start) | async-done | bytes 262176 | tf_op jit(solution)/shard_map/all_to_all | solution.py:425
  25.4 0.0 collective-permute-done.3.refs_2_.rest_1_
  25.4 0.0 collective-permute-done.4.refs_3_.rest_2_
  25.4 0.0 collective-permute-done.5.refs_4_.rest_3_
  25.4 0.0 collective-permute-done.9.near_other
  25.5 0.9 %project.1 = bf16[2,32,576]{2,1,0:T(8,128)(2,1)S(1)} custom-call(bf16[32,4,1024]{2,1,0:T(4,128)(2,1)S(1)} %after.4.taken, bf16[288,1024]{1,0:T(8,128)(2,1)S(1)} %bitcast.23, bf16[288,1024]{1,0:T(8,128)(2,1)S(1)} %collective-permute-done.9.near_other, bf16[288,1024]{1,0:T(8,128)(2,1)S(1)} %after.3.far_own, f32[2,64,288]{2,1,0:T(8,128)S(1)} %get-tuple-element.7.kept, ...), custom_call_target="tpu_custom_call" | custom-call | bytes 7380000 | tf_op jit(solution)/shard_map/project/pallas_call | solution.py:235
  26.4 1.1 %collective-permute-start.10 = (bf16[2,32,576]{2,1,0:T(8,128)(2,1)S(1)}, bf16[2,32,576]{2,1,0:T(8,128)(2,1)S(1)}, u32[]{:S(2)}, u32[]{:S(2)}) collective-permute-start(bf16[2,32,576]{2,1,0:T(8,128)(2,1)S(1)} %project.1), channel_id=1, source_target_pairs={{0,4},{1,5},{2,6},{3,7},{4,0},{5,1},{6,2},{7,3},{8,12},{9,13},{10,... | collective-permute-start | bytes 221192 | tf_op jit(solution)/shard_map/ppermute | solution.py:48
  27.5 1.1 %collective-permute-start.15 = (bf16[2,32,576]{2,1,0:T(8,128)(2,1)S(1)}, bf16[2,32,576]{2,1,0:T(8,128)(2,1)S(1)}, u32[]{:S(2)}, u32[]{:S(2)}) collective-permute-start(bf16[2,32,576]{2,1,0:T(8,128)(2,1)S(1)} %project.1), channel_id=1, source_target_pairs={{0,8},{1,9},{2,10},{3,11},{4,12},{5,13},{6,14},{7,15},{8,0},{9,1},... | collective-permute-start | bytes 221192 | tf_op jit(solution)/shard_map/ppermute | solution.py:48
  28.7 2.2 %collective-permute-start.16 = (bf16[2,32,576]{2,1,0:T(8,128)(2,1)S(1)}, bf16[2,32,576]{2,1,0:T(8,128)(2,1)S(1)}, u32[]{:S(2)}, u32[]{:S(2)}) collective-permute-start(bf16[2,32,576]{2,1,0:T(8,128)(2,1)S(1)} %project.1), channel_id=1, source_target_pairs={{0,12},{1,13},{2,14},{3,15},{4,8},{5,9},{6,10},{7,11},{8,4},{9,5},... | collective-permute-start | bytes 221192 | tf_op jit(solution)/shard_map/ppermute | solution.py:48
  30.9 1.2 %collective-permute-done.10 = bf16[2,32,576]{2,1,0:T(8,128)(2,1)S(1)} collective-permute-done((bf16[2,32,576]{2,1,0:T(8,128)(2,1)S(1)}, bf16[2,32,576]{2,1,0:T(8,128)(2,1)S(1)}, u32[]{:S(2)}, u32[]{:S(2)}) %collective-permute-start.10) | collective-permute-done | bytes 73760 | tf_op jit(solution)/shard_map/ppermute | solution.py:48
  32.1 0.5 collective-permute-start.11
  32.6 0.7 %collective-permute-start.13 = (bf16[2,2,32,576]{3,2,1,0:T(8,128)(2,1)S(1)}, bf16[2,2,32,576]{3,2,1,0:T(8,128)(2,1)S(1)}, u32[]{:S(2)}, u32[]{:S(2)}) collective-permute-start(bf16[2,2,32,576]{3,2,1,0:T(8,128)(2,1)S(1)} %pad_maximum_fusion.own), channel_id=1, source_target_pairs={{0,16},{1,17},{2,18},{3,19},{4,20},{5,21},{6,22},{7,23},{8,24},{9,... | collective-permute-start | bytes 442376 | tf_op jit(solution)/shard_map/ppermute | solution.py:48
  33.3 3.2 %collective-permute-done.15 = bf16[2,32,576]{2,1,0:T(8,128)(2,1)S(1)} collective-permute-done((bf16[2,32,576]{2,1,0:T(8,128)(2,1)S(1)}, bf16[2,32,576]{2,1,0:T(8,128)(2,1)S(1)}, u32[]{:S(2)}, u32[]{:S(2)}) %collective-permute-start.15) | collective-permute-done | bytes 73760 | tf_op jit(solution)/shard_map/ppermute | solution.py:48
  36.6 0.0 collective-permute-done.16
  36.6 1.2 %collective-permute-done.11.refs_1_.own = bf16[2,2,32,576]{3,2,1,0:T(8,128)(2,1)S(1)} collective-permute-done((bf16[2,2,32,576]{3,2,1,0:T(8,128)(2,1)S(1)}, bf16[2,2,32,576]{3,2,1,0:T(8,128)(2,1)S(1)}, u32[]{:S(2)}, u32[]{:S(2)}) %collective-permute-start.11) | collective-permute-done | bytes 147488 | tf_op jit(solution)/shard_map/ppermute | solution.py:48
  37.8 0.7 %collective-permute-start.19 = (bf16[2,2,32,576]{3,2,1,0:T(8,128)(2,1)S(1)}, bf16[2,2,32,576]{3,2,1,0:T(8,128)(2,1)S(1)}, u32[]{:S(2)}, u32[]{:S(2)}) collective-permute-start(bf16[2,2,32,576]{3,2,1,0:T(8,128)(2,1)S(1)} %after.5.own_far), channel_id=1, source_target_pairs={{0,16},{1,17},{2,18},{3,19},{4,20},{5,21},{6,22},{7,23},{8,24},{9,... | collective-permute-start | bytes 442376 | tf_op jit(solution)/shard_map/ppermute | solution.py:48
  38.6 0.6 %collective-permute-start.17 = (bf16[2,2,32,576]{3,2,1,0:T(8,128)(2,1)S(1)}, bf16[2,2,32,576]{3,2,1,0:T(8,128)(2,1)S(1)}, u32[]{:S(2)}, u32[]{:S(2)}) collective-permute-start(bf16[2,2,32,576]{3,2,1,0:T(8,128)(2,1)S(1)} %after.5.own_far), channel_id=1, source_target_pairs={{0,2},{1,3},{2,0},{3,1},{4,6},{5,7},{6,4},{7,5},{8,10},{9,11},{10,... | collective-permute-start | bytes 442376 | tf_op jit(solution)/shard_map/ppermute | solution.py:48
  39.2 1.0 %collective-permute-start.12 = (bf16[2,32,576]{2,1,0:T(8,128)(2,1)S(1)}, bf16[2,32,576]{2,1,0:T(8,128)(2,1)S(1)}, u32[]{:S(2)}, u32[]{:S(2)}) collective-permute-start(bf16[2,32,576]{2,1,0:T(8,128)(2,1)S(1)} %slice_bitcast_fusion.3), channel_id=1, source_target_pairs={{0,16},{1,17},{2,18},{3,19},{4,20},{5,21},{6,22},{7,23},{8,24},{9,... | collective-permute-start | bytes 221192 | tf_op jit(solution)/shard_map/ppermute | solution.py:48
  40.2 0.0 collective-permute-done.13.other
  40.3 1.8 %collective-permute-start.14 = (bf16[2,32,576]{2,1,0:T(8,128)(2,1)S(1)}, bf16[2,32,576]{2,1,0:T(8,128)(2,1)S(1)}, u32[]{:S(2)}, u32[]{:S(2)}) collective-permute-start(bf16[2,32,576]{2,1,0:T(8,128)(2,1)S(1)} %slice_bitcast_fusion.2), channel_id=1, source_target_pairs={{0,2},{1,3},{2,0},{3,1},{4,6},{5,7},{6,4},{7,5},{8,10},{9,11},{10,... | collective-permute-start | bytes 221192 | tf_op jit(solution)/shard_map/ppermute | solution.py:48
  42.1 1.8 %collective-permute-done.17.own_far = bf16[2,2,32,576]{3,2,1,0:T(8,128)(2,1)S(1)} collective-permute-done((bf16[2,2,32,576]{3,2,1,0:T(8,128)(2,1)S(1)}, bf16[2,2,32,576]{3,2,1,0:T(8,128)(2,1)S(1)}, u32[]{:S(2)}, u32[]{:S(2)}) %collective-permute-start.17) | collective-permute-done | bytes 147488 | tf_op jit(solution)/shard_map/ppermute | solution.py:48
  43.9 1.4 %collective-permute-start.18 = (bf16[2,32,576]{2,1,0:T(8,128)(2,1)S(1)}, bf16[2,32,576]{2,1,0:T(8,128)(2,1)S(1)}, u32[]{:S(2)}, u32[]{:S(2)}) collective-permute-start(bf16[2,32,576]{2,1,0:T(8,128)(2,1)S(1)} %slice_bitcast_fusion.1), channel_id=1, source_target_pairs={{0,16},{1,17},{2,18},{3,19},{4,20},{5,21},{6,22},{7,23},{8,24},{9,... | collective-permute-start | bytes 221192 | tf_op jit(solution)/shard_map/ppermute | solution.py:48
  45.3 0.0 collective-permute-done.19.other_far
  45.3 0.3 collective-permute-start.20
  45.7 0.0 collective-permute-done.21.enc_other
  45.7 2.4 %encode_first.1 = (f32[2,128,256]{2,1,0:T(8,128)S(1)}, bf16[2,4,576,256]{3,2,1,0:T(8,128)(2,1)S(1)}) custom-call(bf16[2,2,32,576]{3,2,1,0:T(8,128)(2,1)S(1)} %pad_maximum_fusion.own, bf16[2,2,32,576]{3,2,1,0:T(8,128)(2,1)S(1)} %collective-permute-done.13.other, bf16[2,2,32,576]{3,2,1,0:T(8,128)(2,1)S(1)} %after.5.own_far, ...), custom_call_target="tpu_custom_call" | custom-call | bytes 7380000 | tf_op jit(solution)/shard_map/encode_first/pallas_call | solution.py:334
  48.1 0.0 copy-start.3
  48.1 0.0 copy-start.6
  48.1 0.0 copy-start.7
  48.1 0.0 collective-permute-done.12.upper
  48.2 0.0 collective-permute-done.14.lower
  48.2 0.2 collective-permute-done.18.upper_far
  48.4 1.4 %collective-permute-done.20.lower_far = bf16[2,32,576]{2,1,0:T(8,128)(2,1)S(1)} collective-permute-done((bf16[2,32,576]{2,1,0:T(8,128)(2,1)S(1)}, bf16[2,32,576]{2,1,0:T(8,128)(2,1)S(1)}, u32[]{:S(2)}, u32[]{:S(2)}) %collective-permute-start.20) | collective-permute-done | bytes 73760 | tf_op jit(solution)/shard_map/ppermute | solution.py:48
  49.8 0.7 %encode_second.1 = bf16[16,8,256]{2,1,0:T(8,128)(2,1)S(1)} custom-call(bf16[2,2,32,576]{3,2,1,0:T(8,128)(2,1)S(1)} %collective-permute-done.11.refs_1_.own, bf16[2,32,576]{2,1,0:T(8,128)(2,1)S(1)} %collective-permute-done.12.upper, bf16[2,32,576]{2,1,0:T(8,128)(2,1)S(1)} %collective-permute-done.14.lower, ...), custom_call_target="tpu_custom_call" | custom-call | bytes 7380000 | tf_op jit(solution)/shard_map/encode_second/pallas_call | solution.py:351
  50.5 10.1 %all_to_all.10.parts = bf16[16,8,256]{2,1,0:T(8,128)(2,1)S(1)} all-to-all(bf16[16,8,256]{2,1,0:T(8,128)(2,1)S(1)} %encode_second.1), channel_id=1, replica_groups={{30,28,26,24,22,20,18,16,14,12,10,8,6,4,2,0},{31,29,27,25,23,21,19,17,1..., dimensions={0} | all-to-all | bytes 131072 | tf_op jit(solution)/shard_map/all_to_all | solution.py:448
  60.6 0.0 copy-done.6
  60.7 0.8 %finish.1 = (f32[8,256]{1,0:T(8,128)}, f32[8,16]{1,0:T(8,128)}) custom-call(bf16[16,8,256]{2,1,0:T(8,128)(2,1)S(1)} %all_to_all.10.parts, f32[1,256]{1,0:T(1,128)S(1)} %bitcast.32, f32[16,256]{1,0:T(8,128)S(1)} %bitcast.27, f32[1,16]{1,0:T(1,128)S(1)} %bitcast.33), custom_call_target="tpu_custom_call" | custom-call | tf_op jit(solution)/shard_map/finish/pallas_call | solution.py:384
  (15 shorter events, 0.1 us)
Async XLA Ops:
  0.6 16.6 %collective-permute-start = (bf16[288,1024]{1,0:T(8,128)(2,1)}, bf16[288,1024]{1,0:T(8,128)(2,1)S(1)}, u32[]{:S(2)}, u32[]{:S(2)}) collective-permute-start(bf16[288,1024]{1,0:T(8,128)(2,1)} %bitcast.21), channel_id=1, source_target_pairs={{0,16},{1,17},{2,18},{3,19},{4,20},{5,21},{6,22},{7,23},{8,24},{9,... | collective-permute-start | bytes 1769480 | tf_op jit(solution)/shard_map/ppermute | solution.py:48
  3.7 42.0 %collective-permute-start.21 = (bf16[4608,256]{1,0:T(8,128)(2,1)}, bf16[4608,256]{1,0:T(8,128)(2,1)}, u32[]{:S(2)}, u32[]{:S(2)}) collective-permute-start(bf16[4608,256]{1,0:T(8,128)(2,1)} %enc_own.1), channel_id=1, source_target_pairs={{0,1},{1,0},{2,3},{3,2},{4,5},{5,4},{6,7},{7,6},{8,9},{9,8},{10,11... | collective-permute-start | bytes 7077896 | tf_op jit(solution)/shard_map/ppermute | solution.py:48
  3.7 11.1 %copy-start.1 = (bf16[256,288]{0,1:T(8,128)(2,1)S(1)}, bf16[256,288]{0,1:T(8,128)(2,1)}, u32[]{:S(2)}) copy-start(bf16[256,288]{0,1:T(8,128)(2,1)} %param.22) | copy-start | bytes 442372
  3.7 11.1 %collective-permute-start.1 = (bf16[288,256]{1,0:T(8,128)(2,1)}, bf16[288,256]{1,0:T(8,128)(2,1)S(1)}, u32[]{:S(2)}, u32[]{:S(2)}) collective-permute-start(bf16[288,256]{1,0:T(8,128)(2,1)} %bitcast.25), channel_id=1, source_target_pairs={{0,1},{1,0},{2,3},{3,2},{4,5},{5,4},{6,7},{7,6},{8,9},{9,8},{10,11... | collective-permute-start | bytes 442376 | tf_op jit(solution)/shard_map/ppermute | solution.py:48
  4.2 21.3 %collective-permute-start.9 = (bf16[288,1024]{1,0:T(8,128)(2,1)}, bf16[288,1024]{1,0:T(8,128)(2,1)S(1)}, u32[]{:S(2)}, u32[]{:S(2)}) collective-permute-start(bf16[288,1024]{1,0:T(8,128)(2,1)} %bitcast.22), channel_id=1, source_target_pairs={{0,1},{1,0},{2,3},{3,2},{4,5},{5,4},{6,7},{7,6},{8,9},{9,8},{10,11... | collective-permute-start | bytes 1769480 | tf_op jit(solution)/shard_map/ppermute | solution.py:48
  9.7 7.6 %copy-start.2 = (bf16[256,256]{1,0:T(8,128)(2,1)S(1)}, bf16[256,256]{1,0:T(8,128)(2,1)}, u32[]{:S(2)}) copy-start(bf16[256,256]{1,0:T(8,128)(2,1)} %probe_own.1) | copy-start | bytes 393220
  9.7 8.1 %copy-start.4 = (f32[256]{0:T(256)S(1)}, f32[256]{0:T(256)}, u32[]{:S(2)}) copy-start(f32[256]{0:T(256)} %param.24) | copy-start | bytes 3076
  9.7 9.3 %copy-start.5 = (s32[256]{0:T(256)S(1)}, s32[256]{0:T(256)}, u32[]{:S(2)}) copy-start(s32[256]{0:T(256)} %param.25) | copy-start | bytes 3076
  9.7 15.7 %copy-start = (bf16[1024,288]{0,1:T(8,128)(2,1)S(1)}, bf16[1024,288]{0,1:T(8,128)(2,1)}, u32[]{:S(2)}) copy-start(bf16[1024,288]{0,1:T(8,128)(2,1)} %param.21) | copy-start | bytes 1769476
  9.7 15.7 %all-to-all-start = ((bf16[32,4,1024]{2,1,0:T(4,128)(2,1)}), bf16[32,4,1024]{2,1,0:T(4,128)(2,1)S(1)}, u32[]{:S(2)}, u32[]{:S(2)}) async-start(bf16[32,4,1024]{2,1,0:T(4,128)(2,1)} %attend.1), calls=%async_computation | async-start | bytes 524288 | tf_op jit(solution)/shard_map/all_to_all | solution.py:425
  17.2 3.4 %collective-permute-start.2 = (bf16[288,256]{1,0:T(8,128)(2,1)S(1)}, bf16[288,256]{1,0:T(8,128)(2,1)S(1)}, u32[]{:S(2)}, u32[]{:S(2)}) collective-permute-start(bf16[288,256]{1,0:T(8,128)(2,1)S(1)} %get-tuple-element.13), channel_id=1, source_target_pairs={{0,1},{1,0},{2,3},{3,2},{4,5},{5,4},{6,7},{7,6},{8,9},{9,8},{10,11... | collective-permute-start | bytes 442376 | tf_op jit(solution)/shard_map/ppermute | solution.py:48
  17.3 3.0 %collective-permute-start.6 = (bf16[256,256]{1,0:T(8,128)(2,1)S(1)}, bf16[256,256]{1,0:T(8,128)(2,1)S(1)}, u32[]{:S(2)}, u32[]{:S(2)}) collective-permute-start(bf16[256,256]{1,0:T(8,128)(2,1)S(1)} %copy-done.2), channel_id=1, source_target_pairs={{0,1},{1,0},{2,3},{3,2},{4,5},{5,4},{6,7},{7,6},{8,9},{9,8},{10,11... | collective-permute-start | bytes 393224 | tf_op jit(solution)/shard_map/ppermute | solution.py:48
  17.8 1.1 %collective-permute-start.7 = (f32[256]{0:T(256)S(1)}, f32[256]{0:T(256)S(1)}, u32[]{:S(2)}, u32[]{:S(2)}) collective-permute-start(f32[256]{0:T(256)S(1)} %copy-done.4), channel_id=1, source_target_pairs={{0,1},{1,0},{2,3},{3,2},{4,5},{5,4},{6,7},{7,6},{8,9},{9,8},{10,11... | collective-permute-start | bytes 3080 | tf_op jit(solution)/shard_map/ppermute | solution.py:48
  19.0 1.1 %collective-permute-start.8 = (s32[256]{0:T(256)S(1)}, s32[256]{0:T(256)S(1)}, u32[]{:S(2)}, u32[]{:S(2)}) collective-permute-start(s32[256]{0:T(256)S(1)} %copy-done.5), channel_id=1, source_target_pairs={{0,1},{1,0},{2,3},{3,2},{4,5},{5,4},{6,7},{7,6},{8,9},{9,8},{10,11... | collective-permute-start | bytes 3080 | tf_op jit(solution)/shard_map/ppermute | solution.py:48
  20.1 5.3 %collective-permute-start.3 = (bf16[288,256]{1,0:T(8,128)(2,1)S(1)}, bf16[288,256]{1,0:T(8,128)(2,1)S(1)}, u32[]{:S(2)}, u32[]{:S(2)}) collective-permute-start(bf16[288,256]{1,0:T(8,128)(2,1)S(1)} %get-tuple-element.12), channel_id=1, source_target_pairs={{0,1},{1,0},{2,3},{3,2},{4,5},{5,4},{6,7},{7,6},{8,9},{9,8},{10,11... | collective-permute-start | bytes 442376 | tf_op jit(solution)/shard_map/ppermute | solution.py:48
  20.3 5.1 %collective-permute-start.4 = (bf16[288,256]{1,0:T(8,128)(2,1)S(1)}, bf16[288,256]{1,0:T(8,128)(2,1)S(1)}, u32[]{:S(2)}, u32[]{:S(2)}) collective-permute-start(bf16[288,256]{1,0:T(8,128)(2,1)S(1)} %get-tuple-element.11), channel_id=1, source_target_pairs={{0,1},{1,0},{2,3},{3,2},{4,5},{5,4},{6,7},{7,6},{8,9},{9,8},{10,11... | collective-permute-start | bytes 442376 | tf_op jit(solution)/shard_map/ppermute | solution.py:48
  20.6 4.8 %collective-permute-start.5 = (bf16[288,256]{1,0:T(8,128)(2,1)S(1)}, bf16[288,256]{1,0:T(8,128)(2,1)S(1)}, u32[]{:S(2)}, u32[]{:S(2)}) collective-permute-start(bf16[288,256]{1,0:T(8,128)(2,1)S(1)} %get-tuple-element.10), channel_id=1, source_target_pairs={{0,1},{1,0},{2,3},{3,2},{4,5},{5,4},{6,7},{7,6},{8,9},{9,8},{10,11... | collective-permute-start | bytes 442376 | tf_op jit(solution)/shard_map/ppermute | solution.py:48
  26.4 5.7 %collective-permute-start.10 = (bf16[2,32,576]{2,1,0:T(8,128)(2,1)S(1)}, bf16[2,32,576]{2,1,0:T(8,128)(2,1)S(1)}, u32[]{:S(2)}, u32[]{:S(2)}) collective-permute-start(bf16[2,32,576]{2,1,0:T(8,128)(2,1)S(1)} %project.1), channel_id=1, source_target_pairs={{0,4},{1,5},{2,6},{3,7},{4,0},{5,1},{6,2},{7,3},{8,12},{9,13},{10,... | collective-permute-start | bytes 221192 | tf_op jit(solution)/shard_map/ppermute | solution.py:48
  27.5 9.1 %collective-permute-start.15 = (bf16[2,32,576]{2,1,0:T(8,128)(2,1)S(1)}, bf16[2,32,576]{2,1,0:T(8,128)(2,1)S(1)}, u32[]{:S(2)}, u32[]{:S(2)}) collective-permute-start(bf16[2,32,576]{2,1,0:T(8,128)(2,1)S(1)} %project.1), channel_id=1, source_target_pairs={{0,8},{1,9},{2,10},{3,11},{4,12},{5,13},{6,14},{7,15},{8,0},{9,1},... | collective-permute-start | bytes 221192 | tf_op jit(solution)/shard_map/ppermute | solution.py:48
  28.7 7.9 %collective-permute-start.16 = (bf16[2,32,576]{2,1,0:T(8,128)(2,1)S(1)}, bf16[2,32,576]{2,1,0:T(8,128)(2,1)S(1)}, u32[]{:S(2)}, u32[]{:S(2)}) collective-permute-start(bf16[2,32,576]{2,1,0:T(8,128)(2,1)S(1)} %project.1), channel_id=1, source_target_pairs={{0,12},{1,13},{2,14},{3,15},{4,8},{5,9},{6,10},{7,11},{8,4},{9,5},... | collective-permute-start | bytes 221192 | tf_op jit(solution)/shard_map/ppermute | solution.py:48
  32.1 5.7 %collective-permute-start.11 = (bf16[2,2,32,576]{3,2,1,0:T(8,128)(2,1)S(1)}, bf16[2,2,32,576]{3,2,1,0:T(8,128)(2,1)S(1)}, u32[]{:S(2)}, u32[]{:S(2)}) collective-permute-start(bf16[2,2,32,576]{3,2,1,0:T(8,128)(2,1)S(1)} %pad_maximum_fusion.own), channel_id=1, source_target_pairs={{0,2},{1,3},{2,0},{3,1},{4,6},{5,7},{6,4},{7,5},{8,10},{9,11},{10,... | collective-permute-start | bytes 442376 | tf_op jit(solution)/shard_map/ppermute | solution.py:48
  32.6 7.6 %collective-permute-start.13 = (bf16[2,2,32,576]{3,2,1,0:T(8,128)(2,1)S(1)}, bf16[2,2,32,576]{3,2,1,0:T(8,128)(2,1)S(1)}, u32[]{:S(2)}, u32[]{:S(2)}) collective-permute-start(bf16[2,2,32,576]{3,2,1,0:T(8,128)(2,1)S(1)} %pad_maximum_fusion.own), channel_id=1, source_target_pairs={{0,16},{1,17},{2,18},{3,19},{4,20},{5,21},{6,22},{7,23},{8,24},{9,... | collective-permute-start | bytes 442376 | tf_op jit(solution)/shard_map/ppermute | solution.py:48
  37.8 7.5 %collective-permute-start.19 = (bf16[2,2,32,576]{3,2,1,0:T(8,128)(2,1)S(1)}, bf16[2,2,32,576]{3,2,1,0:T(8,128)(2,1)S(1)}, u32[]{:S(2)}, u32[]{:S(2)}) collective-permute-start(bf16[2,2,32,576]{3,2,1,0:T(8,128)(2,1)S(1)} %after.5.own_far), channel_id=1, source_target_pairs={{0,16},{1,17},{2,18},{3,19},{4,20},{5,21},{6,22},{7,23},{8,24},{9,... | collective-permute-start | bytes 442376 | tf_op jit(solution)/shard_map/ppermute | solution.py:48
  38.6 5.3 %collective-permute-start.17 = (bf16[2,2,32,576]{3,2,1,0:T(8,128)(2,1)S(1)}, bf16[2,2,32,576]{3,2,1,0:T(8,128)(2,1)S(1)}, u32[]{:S(2)}, u32[]{:S(2)}) collective-permute-start(bf16[2,2,32,576]{3,2,1,0:T(8,128)(2,1)S(1)} %after.5.own_far), channel_id=1, source_target_pairs={{0,2},{1,3},{2,0},{3,1},{4,6},{5,7},{6,4},{7,5},{8,10},{9,11},{10,... | collective-permute-start | bytes 442376 | tf_op jit(solution)/shard_map/ppermute | solution.py:48
  39.2 8.9 %collective-permute-start.12 = (bf16[2,32,576]{2,1,0:T(8,128)(2,1)S(1)}, bf16[2,32,576]{2,1,0:T(8,128)(2,1)S(1)}, u32[]{:S(2)}, u32[]{:S(2)}) collective-permute-start(bf16[2,32,576]{2,1,0:T(8,128)(2,1)S(1)} %slice_bitcast_fusion.3), channel_id=1, source_target_pairs={{0,16},{1,17},{2,18},{3,19},{4,20},{5,21},{6,22},{7,23},{8,24},{9,... | collective-permute-start | bytes 221192 | tf_op jit(solution)/shard_map/ppermute | solution.py:48
  40.3 7.9 %collective-permute-start.14 = (bf16[2,32,576]{2,1,0:T(8,128)(2,1)S(1)}, bf16[2,32,576]{2,1,0:T(8,128)(2,1)S(1)}, u32[]{:S(2)}, u32[]{:S(2)}) collective-permute-start(bf16[2,32,576]{2,1,0:T(8,128)(2,1)S(1)} %slice_bitcast_fusion.2), channel_id=1, source_target_pairs={{0,2},{1,3},{2,0},{3,1},{4,6},{5,7},{6,4},{7,5},{8,10},{9,11},{10,... | collective-permute-start | bytes 221192 | tf_op jit(solution)/shard_map/ppermute | solution.py:48
  43.9 4.5 %collective-permute-start.18 = (bf16[2,32,576]{2,1,0:T(8,128)(2,1)S(1)}, bf16[2,32,576]{2,1,0:T(8,128)(2,1)S(1)}, u32[]{:S(2)}, u32[]{:S(2)}) collective-permute-start(bf16[2,32,576]{2,1,0:T(8,128)(2,1)S(1)} %slice_bitcast_fusion.1), channel_id=1, source_target_pairs={{0,16},{1,17},{2,18},{3,19},{4,20},{5,21},{6,22},{7,23},{8,24},{9,... | collective-permute-start | bytes 221192 | tf_op jit(solution)/shard_map/ppermute | solution.py:48
  45.3 4.5 %collective-permute-start.20 = (bf16[2,32,576]{2,1,0:T(8,128)(2,1)S(1)}, bf16[2,32,576]{2,1,0:T(8,128)(2,1)S(1)}, u32[]{:S(2)}, u32[]{:S(2)}) collective-permute-start(bf16[2,32,576]{2,1,0:T(8,128)(2,1)S(1)} %slice_bitcast_fusion), channel_id=1, source_target_pairs={{0,2},{1,3},{2,0},{3,1},{4,6},{5,7},{6,4},{7,5},{8,10},{9,11},{10,... | collective-permute-start | bytes 221192 | tf_op jit(solution)/shard_map/ppermute | solution.py:48
  48.1 12.5 %copy-start.3 = (f32[256,16]{0,1:T(8,128)S(1)}, f32[256,16]{0,1:T(8,128)}, u32[]{:S(2)}) copy-start(f32[256,16]{0,1:T(8,128)} %param.28) | copy-start | bytes 49156
  48.1 12.5 %copy-start.6 = (f32[256]{0:T(256)S(1)}, f32[256]{0:T(256)}, u32[]{:S(2)}) copy-start(f32[256]{0:T(256)} %param.27) | copy-start | bytes 3076
  48.1 12.5 %copy-start.7 = (f32[16]{0:T(128)S(1)}, f32[16]{0:T(128)}, u32[]{:S(2)}) copy-start(f32[16]{0:T(128)} %param.29) | copy-start | bytes 196

commit v7 on v6

--- a/solution.py
+++ b/solution.py
@@ -217,11 +217,12 @@
     def across(left, right):
         return lax.dot_general(left, right, ACROSS, preferred_element_type=jnp.float32)
 
-    own = kept[0] + across(near, near_own[...]) + across(far, far_own[...])
-    other = kept[1] + across(near, near_other[...])
-    depth = far_other[0].shape[1]
+    width, depth = near_own.shape[0], far_other[0].shape[1]
+    both = across(near, jnp.concatenate([near_own[...], near_other[...]], axis=0))
     for at, piece in enumerate(far_other):
-        other += across(far[:, at * depth : (at + 1) * depth], piece[...])
+        part = slice(at * depth, (at + 1) * depth)
+        both += across(far[:, part], jnp.concatenate([far_own[:, part], piece[...]], axis=0))
+    own, other = kept[0] + both[:, :width], kept[1] + both[:, width:]
     first, second = jnp.where(core == 0, own, other), jnp.where(core == 0, other, own)
     stream = jnp.concatenate([first, second], axis=1).astype(jnp.bfloat16)
     half = stream.shape[0] // 2

time: 61.7 us -> 61.7 us (level)
  no operation moved by 1% of the time
where the time goes in v7:
time: 61.7 us; the launch traced here: 61.4 us
  starting transfers between devices  21.7 us (35%)
  waiting for transfers between devices  17.9 us (29%)
  Pallas kernels  10.6 us (17%)
  blocking collectives  10.1 us (16%)
  between operations  0.86 us (1%)
    ppermute x22, starting transfers between devices, xor(): return lax.ppermute(value, ALL, [(i, i ^ bits) for i in range(32)])  16.7 us
    ppermute x22, waiting for transfers between devices, xor(): return lax.ppermute(value, ALL, [(i, i ^ bits) for i in range(32)])  13.3 us
    all_to_all x1, blocking collectives, chip_body(): lax.all_to_all(partial, ALL, 0, 0, tiled=True, axis_index_groups=PLANES)  10.1 us
    pallas_call x1, Pallas kernels, attend_shares(): pl.pallas_call(attend_kernel, out_shape=jax.ShapeDtypeStruct((32, 4, widt...  5.51 us
    all_to_all x1, starting transfers between devices, chip_body(): lax.all_to_all(sent, ALL, 0, 0, tiled=True, axis_index_groups=[ORDER])  5.01 us
    all_to_all x1, waiting for transfers between devices, chip_body(): lax.all_to_all(sent, ALL, 0, 0, tiled=True, axis_index_groups=[ORDER])  4.57 us
    pallas_call x1, Pallas kernels, encode_first(): pl.pallas_call(encode_first_kernel, out_shape=(jax.ShapeDtypeStruct((2, r...  2.43 us
  transfers between devices with their start and end apart: 23, of which 10 were waited for; matrix products, arithmetic and copies ran while one was open for 0% of the time, Pallas kernels for 15%

profile of v7, /device:TPU:0, one launch (start us, length us, event | category | flops | bytes accessed | tf_op | source)
XLA Modules:
  0.0 61.4 jit_solution(48016181167399295)
XLA Ops:
  0.6 3.0 %collective-permute-start = (bf16[288,1024]{1,0:T(8,128)(2,1)}, bf16[288,1024]{1,0:T(8,128)(2,1)S(1)}, u32[]{:S(2)}, u32[]{:S(2)}) collective-permute-start(bf16[288,1024]{1,0:T(8,128)(2,1)} %bitcast.21), channel_id=1, source_target_pairs={{0,16},{1,17},{2,18},{3,19},{4,20},{5,21},{6,22},{7,23},{8,24},{9,... | collective-permute-start | bytes 1769480 | tf_op jit(solution)/shard_map/ppermute | solution.py:48
  3.7 0.0 collective-permute-start.21
  3.7 0.5 collective-permute-start.1
  4.2 0.0 collective-permute-start.9
  4.2 5.5 %attend.1 = bf16[32,4,1024]{2,1,0:T(4,128)(2,1)} custom-call(s32[16]{0:T(128)} %lengths.1, bf16[16,1024]{1,0:T(8,128)(2,1)} %queries.1, bf16[16,512]{1,0:T(8,128)(2,1)} %new_key.1, bf16[16,512]{1,0:T(8,128)(2,1)} %new_value.1, bf16[16,256,512]{2,1,0:T(8,128)(2,1)} %keys_at.1, bf16[16,256,512]{2,1,0:T(8,128)(2,1)} %values_at.1), custom_call_target="tpu_custom_call" | custom-call | bytes 44280000 | tf_op jit(solution)/shard_map/attend/pallas_call | solution.py:146
  9.7 0.0 copy-start.2
  9.7 0.0 copy-start.4
  9.7 0.0 copy-start.5
  9.7 0.0 copy-start
  9.7 5.0 %all-to-all-start = ((bf16[32,4,1024]{2,1,0:T(4,128)(2,1)}), bf16[32,4,1024]{2,1,0:T(4,128)(2,1)S(1)}, u32[]{:S(2)}, u32[]{:S(2)}) async-start(bf16[32,4,1024]{2,1,0:T(4,128)(2,1)} %attend.1), calls=%async_computation | async-start | bytes 524288 | tf_op jit(solution)/shard_map/all_to_all | solution.py:426
  14.8 0.0 collective-permute-done.1.kept_other
  14.8 0.0 copy-done.1
  14.8 0.3 keep.1
  15.1 2.1 %collective-permute-done.refs_0_ = bf16[288,1024]{1,0:T(8,128)(2,1)S(1)} collective-permute-done((bf16[288,1024]{1,0:T(8,128)(2,1)}, bf16[288,1024]{1,0:T(8,128)(2,1)S(1)}, u32[]{:S(2)}, u32[]{:S(2)}) %collective-permute-start) | collective-permute-done | bytes 589856 | tf_op jit(solution)/shard_map/ppermute | solution.py:48
  17.2 0.1 collective-permute-start.2
  17.3 0.0 copy-done.2
  17.3 0.5 collective-permute-start.6
  17.8 0.0 copy-done.4
  17.8 0.1 collective-permute-start.7
  17.9 1.1 %collective-permute-done.7.refs_6_ = f32[256]{0:T(256)S(1)} collective-permute-done((f32[256]{0:T(256)S(1)}, f32[256]{0:T(256)S(1)}, u32[]{:S(2)}, u32[]{:S(2)}) %collective-permute-start.7) | collective-permute-done | bytes 1056 | tf_op jit(solution)/shard_map/ppermute | solution.py:48
  19.0 0.2 collective-permute-start.8
  19.2 0.9 %collective-permute-done.8.refs_7_ = s32[256]{0:T(256)S(1)} collective-permute-done((s32[256]{0:T(256)S(1)}, s32[256]{0:T(256)S(1)}, u32[]{:S(2)}, u32[]{:S(2)}) %collective-permute-start.8) | collective-permute-done | bytes 1056 | tf_op jit(solution)/shard_map/ppermute | solution.py:48
  20.1 0.2 collective-permute-start.3
  20.3 0.0 collective-permute-done.6.refs_5_.probe_other
  20.3 0.3 collective-permute-start.4
  20.6 0.0 collective-permute-done.2.refs_1_.rest_0_
  20.6 0.2 collective-permute-start.5
  20.8 4.6 %all-to-all-done.refs_0_ = bf16[32,4,1024]{2,1,0:T(4,128)(2,1)S(1)} async-done(((bf16[32,4,1024]{2,1,0:T(4,128)(2,1)}), bf16[32,4,1024]{2,1,0:T(4,128)(2,1)S(1)}, u32[]{:S(2)}, u32[]{:S(2)}) %all-to-all-start) | async-done | bytes 262176 | tf_op jit(solution)/shard_map/all_to_all | solution.py:426
  25.4 0.0 collective-permute-done.3.refs_2_.rest_1_
  25.4 0.0 collective-permute-done.4.refs_3_.rest_2_
  25.4 0.0 collective-permute-done.5.refs_4_.rest_3_
  25.4 0.0 collective-permute-done.9.near_other
  25.5 0.9 %project.1 = bf16[2,32,576]{2,1,0:T(8,128)(2,1)S(1)} custom-call(bf16[32,4,1024]{2,1,0:T(4,128)(2,1)S(1)} %after.4.taken, bf16[288,1024]{1,0:T(8,128)(2,1)S(1)} %bitcast.23, bf16[288,1024]{1,0:T(8,128)(2,1)S(1)} %collective-permute-done.9.near_other, bf16[288,1024]{1,0:T(8,128)(2,1)S(1)} %after.3.far_own, f32[2,64,288]{2,1,0:T(8,128)S(1)} %get-tuple-element.7.kept, ...), custom_call_target="tpu_custom_call" | custom-call | bytes 7380000 | tf_op jit(solution)/shard_map/project/pallas_call | solution.py:236
  26.4 1.1 %collective-permute-start.10 = (bf16[2,32,576]{2,1,0:T(8,128)(2,1)S(1)}, bf16[2,32,576]{2,1,0:T(8,128)(2,1)S(1)}, u32[]{:S(2)}, u32[]{:S(2)}) collective-permute-start(bf16[2,32,576]{2,1,0:T(8,128)(2,1)S(1)} %project.1), channel_id=1, source_target_pairs={{0,4},{1,5},{2,6},{3,7},{4,0},{5,1},{6,2},{7,3},{8,12},{9,13},{10,... | collective-permute-start | bytes 221192 | tf_op jit(solution)/shard_map/ppermute | solution.py:48
  27.5 1.1 %collective-permute-start.15 = (bf16[2,32,576]{2,1,0:T(8,128)(2,1)S(1)}, bf16[2,32,576]{2,1,0:T(8,128)(2,1)S(1)}, u32[]{:S(2)}, u32[]{:S(2)}) collective-permute-start(bf16[2,32,576]{2,1,0:T(8,128)(2,1)S(1)} %project.1), channel_id=1, source_target_pairs={{0,8},{1,9},{2,10},{3,11},{4,12},{5,13},{6,14},{7,15},{8,0},{9,1},... | collective-permute-start | bytes 221192 | tf_op jit(solution)/shard_map/ppermute | solution.py:48
  28.6 2.2 %collective-permute-start.16 = (bf16[2,32,576]{2,1,0:T(8,128)(2,1)S(1)}, bf16[2,32,576]{2,1,0:T(8,128)(2,1)S(1)}, u32[]{:S(2)}, u32[]{:S(2)}) collective-permute-start(bf16[2,32,576]{2,1,0:T(8,128)(2,1)S(1)} %project.1), channel_id=1, source_target_pairs={{0,12},{1,13},{2,14},{3,15},{4,8},{5,9},{6,10},{7,11},{8,4},{9,5},... | collective-permute-start | bytes 221192 | tf_op jit(solution)/shard_map/ppermute | solution.py:48
  30.9 1.2 %collective-permute-done.10 = bf16[2,32,576]{2,1,0:T(8,128)(2,1)S(1)} collective-permute-done((bf16[2,32,576]{2,1,0:T(8,128)(2,1)S(1)}, bf16[2,32,576]{2,1,0:T(8,128)(2,1)S(1)}, u32[]{:S(2)}, u32[]{:S(2)}) %collective-permute-start.10) | collective-permute-done | bytes 73760 | tf_op jit(solution)/shard_map/ppermute | solution.py:48
  32.1 0.5 collective-permute-start.11
  32.6 0.7 %collective-permute-start.13 = (bf16[2,2,32,576]{3,2,1,0:T(8,128)(2,1)S(1)}, bf16[2,2,32,576]{3,2,1,0:T(8,128)(2,1)S(1)}, u32[]{:S(2)}, u32[]{:S(2)}) collective-permute-start(bf16[2,2,32,576]{3,2,1,0:T(8,128)(2,1)S(1)} %pad_maximum_fusion.own), channel_id=1, source_target_pairs={{0,16},{1,17},{2,18},{3,19},{4,20},{5,21},{6,22},{7,23},{8,24},{9,... | collective-permute-start | bytes 442376 | tf_op jit(solution)/shard_map/ppermute | solution.py:48
  33.3 3.2 %collective-permute-done.15 = bf16[2,32,576]{2,1,0:T(8,128)(2,1)S(1)} collective-permute-done((bf16[2,32,576]{2,1,0:T(8,128)(2,1)S(1)}, bf16[2,32,576]{2,1,0:T(8,128)(2,1)S(1)}, u32[]{:S(2)}, u32[]{:S(2)}) %collective-permute-start.15) | collective-permute-done | bytes 73760 | tf_op jit(solution)/shard_map/ppermute | solution.py:48
  36.6 0.0 collective-permute-done.16
  36.6 1.2 %collective-permute-done.11.refs_1_.own = bf16[2,2,32,576]{3,2,1,0:T(8,128)(2,1)S(1)} collective-permute-done((bf16[2,2,32,576]{3,2,1,0:T(8,128)(2,1)S(1)}, bf16[2,2,32,576]{3,2,1,0:T(8,128)(2,1)S(1)}, u32[]{:S(2)}, u32[]{:S(2)}) %collective-permute-start.11) | collective-permute-done | bytes 147488 | tf_op jit(solution)/shard_map/ppermute | solution.py:48
  37.8 0.7 %collective-permute-start.19 = (bf16[2,2,32,576]{3,2,1,0:T(8,128)(2,1)S(1)}, bf16[2,2,32,576]{3,2,1,0:T(8,128)(2,1)S(1)}, u32[]{:S(2)}, u32[]{:S(2)}) collective-permute-start(bf16[2,2,32,576]{3,2,1,0:T(8,128)(2,1)S(1)} %after.5.own_far), channel_id=1, source_target_pairs={{0,16},{1,17},{2,18},{3,19},{4,20},{5,21},{6,22},{7,23},{8,24},{9,... | collective-permute-start | bytes 442376 | tf_op jit(solution)/shard_map/ppermute | solution.py:48
  38.6 0.6 %collective-permute-start.17 = (bf16[2,2,32,576]{3,2,1,0:T(8,128)(2,1)S(1)}, bf16[2,2,32,576]{3,2,1,0:T(8,128)(2,1)S(1)}, u32[]{:S(2)}, u32[]{:S(2)}) collective-permute-start(bf16[2,2,32,576]{3,2,1,0:T(8,128)(2,1)S(1)} %after.5.own_far), channel_id=1, source_target_pairs={{0,2},{1,3},{2,0},{3,1},{4,6},{5,7},{6,4},{7,5},{8,10},{9,11},{10,... | collective-permute-start | bytes 442376 | tf_op jit(solution)/shard_map/ppermute | solution.py:48
  39.2 1.0 %collective-permute-start.12 = (bf16[2,32,576]{2,1,0:T(8,128)(2,1)S(1)}, bf16[2,32,576]{2,1,0:T(8,128)(2,1)S(1)}, u32[]{:S(2)}, u32[]{:S(2)}) collective-permute-start(bf16[2,32,576]{2,1,0:T(8,128)(2,1)S(1)} %slice_bitcast_fusion.3), channel_id=1, source_target_pairs={{0,16},{1,17},{2,18},{3,19},{4,20},{5,21},{6,22},{7,23},{8,24},{9,... | collective-permute-start | bytes 221192 | tf_op jit(solution)/shard_map/ppermute | solution.py:48
  40.2 0.0 collective-permute-done.13.other
  40.2 1.8 %collective-permute-start.14 = (bf16[2,32,576]{2,1,0:T(8,128)(2,1)S(1)}, bf16[2,32,576]{2,1,0:T(8,128)(2,1)S(1)}, u32[]{:S(2)}, u32[]{:S(2)}) collective-permute-start(bf16[2,32,576]{2,1,0:T(8,128)(2,1)S(1)} %slice_bitcast_fusion.2), channel_id=1, source_target_pairs={{0,2},{1,3},{2,0},{3,1},{4,6},{5,7},{6,4},{7,5},{8,10},{9,11},{10,... | collective-permute-start | bytes 221192 | tf_op jit(solution)/shard_map/ppermute | solution.py:48
  42.0 1.8 %collective-permute-done.17.own_far = bf16[2,2,32,576]{3,2,1,0:T(8,128)(2,1)S(1)} collective-permute-done((bf16[2,2,32,576]{3,2,1,0:T(8,128)(2,1)S(1)}, bf16[2,2,32,576]{3,2,1,0:T(8,128)(2,1)S(1)}, u32[]{:S(2)}, u32[]{:S(2)}) %collective-permute-start.17) | collective-permute-done | bytes 147488 | tf_op jit(solution)/shard_map/ppermute | solution.py:48
  43.9 1.4 %collective-permute-start.18 = (bf16[2,32,576]{2,1,0:T(8,128)(2,1)S(1)}, bf16[2,32,576]{2,1,0:T(8,128)(2,1)S(1)}, u32[]{:S(2)}, u32[]{:S(2)}) collective-permute-start(bf16[2,32,576]{2,1,0:T(8,128)(2,1)S(1)} %slice_bitcast_fusion.1), channel_id=1, source_target_pairs={{0,16},{1,17},{2,18},{3,19},{4,20},{5,21},{6,22},{7,23},{8,24},{9,... | collective-permute-start | bytes 221192 | tf_op jit(solution)/shard_map/ppermute | solution.py:48
  45.3 0.0 collective-permute-done.19.other_far
  45.3 0.3 collective-permute-start.20
  45.7 0.0 collective-permute-done.21.enc_other
  45.7 2.4 %encode_first.1 = (f32[2,128,256]{2,1,0:T(8,128)S(1)}, bf16[2,4,576,256]{3,2,1,0:T(8,128)(2,1)S(1)}) custom-call(bf16[2,2,32,576]{3,2,1,0:T(8,128)(2,1)S(1)} %pad_maximum_fusion.own, bf16[2,2,32,576]{3,2,1,0:T(8,128)(2,1)S(1)} %collective-permute-done.13.other, bf16[2,2,32,576]{3,2,1,0:T(8,128)(2,1)S(1)} %after.5.own_far, ...), custom_call_target="tpu_custom_call" | custom-call | bytes 7380000 | tf_op jit(solution)/shard_map/encode_first/pallas_call | solution.py:335
  48.1 0.0 copy-start.3
  48.1 0.0 copy-start.6
  48.1 0.0 copy-start.7
  48.1 0.0 collective-permute-done.12.upper
  48.1 0.0 collective-permute-done.14.lower
  48.2 0.2 collective-permute-done.18.upper_far
  48.4 1.4 %collective-permute-done.20.lower_far = bf16[2,32,576]{2,1,0:T(8,128)(2,1)S(1)} collective-permute-done((bf16[2,32,576]{2,1,0:T(8,128)(2,1)S(1)}, bf16[2,32,576]{2,1,0:T(8,128)(2,1)S(1)}, u32[]{:S(2)}, u32[]{:S(2)}) %collective-permute-start.20) | collective-permute-done | bytes 73760 | tf_op jit(solution)/shard_map/ppermute | solution.py:48
  49.8 0.7 %encode_second.1 = bf16[16,8,256]{2,1,0:T(8,128)(2,1)S(1)} custom-call(bf16[2,2,32,576]{3,2,1,0:T(8,128)(2,1)S(1)} %collective-permute-done.11.refs_1_.own, bf16[2,32,576]{2,1,0:T(8,128)(2,1)S(1)} %collective-permute-done.12.upper, bf16[2,32,576]{2,1,0:T(8,128)(2,1)S(1)} %collective-permute-done.14.lower, ...), custom_call_target="tpu_custom_call" | custom-call | bytes 7380000 | tf_op jit(solution)/shard_map/encode_second/pallas_call | solution.py:352
  50.5 10.1 %all_to_all.10.parts = bf16[16,8,256]{2,1,0:T(8,128)(2,1)S(1)} all-to-all(bf16[16,8,256]{2,1,0:T(8,128)(2,1)S(1)} %encode_second.1), channel_id=1, replica_groups={{30,28,26,24,22,20,18,16,14,12,10,8,6,4,2,0},{31,29,27,25,23,21,19,17,1..., dimensions={0} | all-to-all | bytes 131072 | tf_op jit(solution)/shard_map/all_to_all | solution.py:449
  60.6 0.0 copy-done.6
  60.6 0.8 %finish.1 = (f32[8,256]{1,0:T(8,128)}, f32[8,16]{1,0:T(8,128)}) custom-call(bf16[16,8,256]{2,1,0:T(8,128)(2,1)S(1)} %all_to_all.10.parts, f32[1,256]{1,0:T(1,128)S(1)} %bitcast.32, f32[16,256]{1,0:T(8,128)S(1)} %bitcast.27, f32[1,16]{1,0:T(1,128)S(1)} %bitcast.33), custom_call_target="tpu_custom_call" | custom-call | tf_op jit(solution)/shard_map/finish/pallas_call | solution.py:385
  (15 shorter events, 0.1 us)
Async XLA Ops:
  0.6 16.6 %collective-permute-start = (bf16[288,1024]{1,0:T(8,128)(2,1)}, bf16[288,1024]{1,0:T(8,128)(2,1)S(1)}, u32[]{:S(2)}, u32[]{:S(2)}) collective-permute-start(bf16[288,1024]{1,0:T(8,128)(2,1)} %bitcast.21), channel_id=1, source_target_pairs={{0,16},{1,17},{2,18},{3,19},{4,20},{5,21},{6,22},{7,23},{8,24},{9,... | collective-permute-start | bytes 1769480 | tf_op jit(solution)/shard_map/ppermute | solution.py:48
  3.7 42.0 %collective-permute-start.21 = (bf16[4608,256]{1,0:T(8,128)(2,1)}, bf16[4608,256]{1,0:T(8,128)(2,1)}, u32[]{:S(2)}, u32[]{:S(2)}) collective-permute-start(bf16[4608,256]{1,0:T(8,128)(2,1)} %enc_own.1), channel_id=1, source_target_pairs={{0,1},{1,0},{2,3},{3,2},{4,5},{5,4},{6,7},{7,6},{8,9},{9,8},{10,11... | collective-permute-start | bytes 7077896 | tf_op jit(solution)/shard_map/ppermute | solution.py:48
  3.7 11.1 %copy-start.1 = (bf16[256,288]{0,1:T(8,128)(2,1)S(1)}, bf16[256,288]{0,1:T(8,128)(2,1)}, u32[]{:S(2)}) copy-start(bf16[256,288]{0,1:T(8,128)(2,1)} %param.22) | copy-start | bytes 442372
  3.7 11.1 %collective-permute-start.1 = (bf16[288,256]{1,0:T(8,128)(2,1)}, bf16[288,256]{1,0:T(8,128)(2,1)S(1)}, u32[]{:S(2)}, u32[]{:S(2)}) collective-permute-start(bf16[288,256]{1,0:T(8,128)(2,1)} %bitcast.25), channel_id=1, source_target_pairs={{0,1},{1,0},{2,3},{3,2},{4,5},{5,4},{6,7},{7,6},{8,9},{9,8},{10,11... | collective-permute-start | bytes 442376 | tf_op jit(solution)/shard_map/ppermute | solution.py:48
  4.2 21.3 %collective-permute-start.9 = (bf16[288,1024]{1,0:T(8,128)(2,1)}, bf16[288,1024]{1,0:T(8,128)(2,1)S(1)}, u32[]{:S(2)}, u32[]{:S(2)}) collective-permute-start(bf16[288,1024]{1,0:T(8,128)(2,1)} %bitcast.22), channel_id=1, source_target_pairs={{0,1},{1,0},{2,3},{3,2},{4,5},{5,4},{6,7},{7,6},{8,9},{9,8},{10,11... | collective-permute-start | bytes 1769480 | tf_op jit(solution)/shard_map/ppermute | solution.py:48
  9.7 7.6 %copy-start.2 = (bf16[256,256]{1,0:T(8,128)(2,1)S(1)}, bf16[256,256]{1,0:T(8,128)(2,1)}, u32[]{:S(2)}) copy-start(bf16[256,256]{1,0:T(8,128)(2,1)} %probe_own.1) | copy-start | bytes 393220
  9.7 8.1 %copy-start.4 = (f32[256]{0:T(256)S(1)}, f32[256]{0:T(256)}, u32[]{:S(2)}) copy-start(f32[256]{0:T(256)} %param.24) | copy-start | bytes 3076
  9.7 9.3 %copy-start.5 = (s32[256]{0:T(256)S(1)}, s32[256]{0:T(256)}, u32[]{:S(2)}) copy-start(s32[256]{0:T(256)} %param.25) | copy-start | bytes 3076
  9.7 15.7 %copy-start = (bf16[1024,288]{0,1:T(8,128)(2,1)S(1)}, bf16[1024,288]{0,1:T(8,128)(2,1)}, u32[]{:S(2)}) copy-start(bf16[1024,288]{0,1:T(8,128)(2,1)} %param.21) | copy-start | bytes 1769476
  9.7 15.7 %all-to-all-start = ((bf16[32,4,1024]{2,1,0:T(4,128)(2,1)}), bf16[32,4,1024]{2,1,0:T(4,128)(2,1)S(1)}, u32[]{:S(2)}, u32[]{:S(2)}) async-start(bf16[32,4,1024]{2,1,0:T(4,128)(2,1)} %attend.1), calls=%async_computation | async-start | bytes 524288 | tf_op jit(solution)/shard_map/all_to_all | solution.py:426
  17.2 3.4 %collective-permute-start.2 = (bf16[288,256]{1,0:T(8,128)(2,1)S(1)}, bf16[288,256]{1,0:T(8,128)(2,1)S(1)}, u32[]{:S(2)}, u32[]{:S(2)}) collective-permute-start(bf16[288,256]{1,0:T(8,128)(2,1)S(1)} %get-tuple-element.13), channel_id=1, source_target_pairs={{0,1},{1,0},{2,3},{3,2},{4,5},{5,4},{6,7},{7,6},{8,9},{9,8},{10,11... | collective-permute-start | bytes 442376 | tf_op jit(solution)/shard_map/ppermute | solution.py:48
  17.3 3.0 %collective-permute-start.6 = (bf16[256,256]{1,0:T(8,128)(2,1)S(1)}, bf16[256,256]{1,0:T(8,128)(2,1)S(1)}, u32[]{:S(2)}, u32[]{:S(2)}) collective-permute-start(bf16[256,256]{1,0:T(8,128)(2,1)S(1)} %copy-done.2), channel_id=1, source_target_pairs={{0,1},{1,0},{2,3},{3,2},{4,5},{5,4},{6,7},{7,6},{8,9},{9,8},{10,11... | collective-permute-start | bytes 393224 | tf_op jit(solution)/shard_map/ppermute | solution.py:48
  17.8 1.1 %collective-permute-start.7 = (f32[256]{0:T(256)S(1)}, f32[256]{0:T(256)S(1)}, u32[]{:S(2)}, u32[]{:S(2)}) collective-permute-start(f32[256]{0:T(256)S(1)} %copy-done.4), channel_id=1, source_target_pairs={{0,1},{1,0},{2,3},{3,2},{4,5},{5,4},{6,7},{7,6},{8,9},{9,8},{10,11... | collective-permute-start | bytes 3080 | tf_op jit(solution)/shard_map/ppermute | solution.py:48
  19.0 1.1 %collective-permute-start.8 = (s32[256]{0:T(256)S(1)}, s32[256]{0:T(256)S(1)}, u32[]{:S(2)}, u32[]{:S(2)}) collective-permute-start(s32[256]{0:T(256)S(1)} %copy-done.5), channel_id=1, source_target_pairs={{0,1},{1,0},{2,3},{3,2},{4,5},{5,4},{6,7},{7,6},{8,9},{9,8},{10,11... | collective-permute-start | bytes 3080 | tf_op jit(solution)/shard_map/ppermute | solution.py:48
  20.1 5.3 %collective-permute-start.3 = (bf16[288,256]{1,0:T(8,128)(2,1)S(1)}, bf16[288,256]{1,0:T(8,128)(2,1)S(1)}, u32[]{:S(2)}, u32[]{:S(2)}) collective-permute-start(bf16[288,256]{1,0:T(8,128)(2,1)S(1)} %get-tuple-element.12), channel_id=1, source_target_pairs={{0,1},{1,0},{2,3},{3,2},{4,5},{5,4},{6,7},{7,6},{8,9},{9,8},{10,11... | collective-permute-start | bytes 442376 | tf_op jit(solution)/shard_map/ppermute | solution.py:48
  20.3 5.1 %collective-permute-start.4 = (bf16[288,256]{1,0:T(8,128)(2,1)S(1)}, bf16[288,256]{1,0:T(8,128)(2,1)S(1)}, u32[]{:S(2)}, u32[]{:S(2)}) collective-permute-start(bf16[288,256]{1,0:T(8,128)(2,1)S(1)} %get-tuple-element.11), channel_id=1, source_target_pairs={{0,1},{1,0},{2,3},{3,2},{4,5},{5,4},{6,7},{7,6},{8,9},{9,8},{10,11... | collective-permute-start | bytes 442376 | tf_op jit(solution)/shard_map/ppermute | solution.py:48
  20.6 4.8 %collective-permute-start.5 = (bf16[288,256]{1,0:T(8,128)(2,1)S(1)}, bf16[288,256]{1,0:T(8,128)(2,1)S(1)}, u32[]{:S(2)}, u32[]{:S(2)}) collective-permute-start(bf16[288,256]{1,0:T(8,128)(2,1)S(1)} %get-tuple-element.10), channel_id=1, source_target_pairs={{0,1},{1,0},{2,3},{3,2},{4,5},{5,4},{6,7},{7,6},{8,9},{9,8},{10,11... | collective-permute-start | bytes 442376 | tf_op jit(solution)/shard_map/ppermute | solution.py:48
  26.4 5.7 %collective-permute-start.10 = (bf16[2,32,576]{2,1,0:T(8,128)(2,1)S(1)}, bf16[2,32,576]{2,1,0:T(8,128)(2,1)S(1)}, u32[]{:S(2)}, u32[]{:S(2)}) collective-permute-start(bf16[2,32,576]{2,1,0:T(8,128)(2,1)S(1)} %project.1), channel_id=1, source_target_pairs={{0,4},{1,5},{2,6},{3,7},{4,0},{5,1},{6,2},{7,3},{8,12},{9,13},{10,... | collective-permute-start | bytes 221192 | tf_op jit(solution)/shard_map/ppermute | solution.py:48
  27.5 9.1 %collective-permute-start.15 = (bf16[2,32,576]{2,1,0:T(8,128)(2,1)S(1)}, bf16[2,32,576]{2,1,0:T(8,128)(2,1)S(1)}, u32[]{:S(2)}, u32[]{:S(2)}) collective-permute-start(bf16[2,32,576]{2,1,0:T(8,128)(2,1)S(1)} %project.1), channel_id=1, source_target_pairs={{0,8},{1,9},{2,10},{3,11},{4,12},{5,13},{6,14},{7,15},{8,0},{9,1},... | collective-permute-start | bytes 221192 | tf_op jit(solution)/shard_map/ppermute | solution.py:48
  28.6 7.9 %collective-permute-start.16 = (bf16[2,32,576]{2,1,0:T(8,128)(2,1)S(1)}, bf16[2,32,576]{2,1,0:T(8,128)(2,1)S(1)}, u32[]{:S(2)}, u32[]{:S(2)}) collective-permute-start(bf16[2,32,576]{2,1,0:T(8,128)(2,1)S(1)} %project.1), channel_id=1, source_target_pairs={{0,12},{1,13},{2,14},{3,15},{4,8},{5,9},{6,10},{7,11},{8,4},{9,5},... | collective-permute-start | bytes 221192 | tf_op jit(solution)/shard_map/ppermute | solution.py:48
  32.1 5.7 %collective-permute-start.11 = (bf16[2,2,32,576]{3,2,1,0:T(8,128)(2,1)S(1)}, bf16[2,2,32,576]{3,2,1,0:T(8,128)(2,1)S(1)}, u32[]{:S(2)}, u32[]{:S(2)}) collective-permute-start(bf16[2,2,32,576]{3,2,1,0:T(8,128)(2,1)S(1)} %pad_maximum_fusion.own), channel_id=1, source_target_pairs={{0,2},{1,3},{2,0},{3,1},{4,6},{5,7},{6,4},{7,5},{8,10},{9,11},{10,... | collective-permute-start | bytes 442376 | tf_op jit(solution)/shard_map/ppermute | solution.py:48
  32.6 7.6 %collective-permute-start.13 = (bf16[2,2,32,576]{3,2,1,0:T(8,128)(2,1)S(1)}, bf16[2,2,32,576]{3,2,1,0:T(8,128)(2,1)S(1)}, u32[]{:S(2)}, u32[]{:S(2)}) collective-permute-start(bf16[2,2,32,576]{3,2,1,0:T(8,128)(2,1)S(1)} %pad_maximum_fusion.own), channel_id=1, source_target_pairs={{0,16},{1,17},{2,18},{3,19},{4,20},{5,21},{6,22},{7,23},{8,24},{9,... | collective-permute-start | bytes 442376 | tf_op jit(solution)/shard_map/ppermute | solution.py:48
  37.8 7.5 %collective-permute-start.19 = (bf16[2,2,32,576]{3,2,1,0:T(8,128)(2,1)S(1)}, bf16[2,2,32,576]{3,2,1,0:T(8,128)(2,1)S(1)}, u32[]{:S(2)}, u32[]{:S(2)}) collective-permute-start(bf16[2,2,32,576]{3,2,1,0:T(8,128)(2,1)S(1)} %after.5.own_far), channel_id=1, source_target_pairs={{0,16},{1,17},{2,18},{3,19},{4,20},{5,21},{6,22},{7,23},{8,24},{9,... | collective-permute-start | bytes 442376 | tf_op jit(solution)/shard_map/ppermute | solution.py:48
  38.6 5.3 %collective-permute-start.17 = (bf16[2,2,32,576]{3,2,1,0:T(8,128)(2,1)S(1)}, bf16[2,2,32,576]{3,2,1,0:T(8,128)(2,1)S(1)}, u32[]{:S(2)}, u32[]{:S(2)}) collective-permute-start(bf16[2,2,32,576]{3,2,1,0:T(8,128)(2,1)S(1)} %after.5.own_far), channel_id=1, source_target_pairs={{0,2},{1,3},{2,0},{3,1},{4,6},{5,7},{6,4},{7,5},{8,10},{9,11},{10,... | collective-permute-start | bytes 442376 | tf_op jit(solution)/shard_map/ppermute | solution.py:48
  39.2 8.9 %collective-permute-start.12 = (bf16[2,32,576]{2,1,0:T(8,128)(2,1)S(1)}, bf16[2,32,576]{2,1,0:T(8,128)(2,1)S(1)}, u32[]{:S(2)}, u32[]{:S(2)}) collective-permute-start(bf16[2,32,576]{2,1,0:T(8,128)(2,1)S(1)} %slice_bitcast_fusion.3), channel_id=1, source_target_pairs={{0,16},{1,17},{2,18},{3,19},{4,20},{5,21},{6,22},{7,23},{8,24},{9,... | collective-permute-start | bytes 221192 | tf_op jit(solution)/shard_map/ppermute | solution.py:48
  40.2 7.9 %collective-permute-start.14 = (bf16[2,32,576]{2,1,0:T(8,128)(2,1)S(1)}, bf16[2,32,576]{2,1,0:T(8,128)(2,1)S(1)}, u32[]{:S(2)}, u32[]{:S(2)}) collective-permute-start(bf16[2,32,576]{2,1,0:T(8,128)(2,1)S(1)} %slice_bitcast_fusion.2), channel_id=1, source_target_pairs={{0,2},{1,3},{2,0},{3,1},{4,6},{5,7},{6,4},{7,5},{8,10},{9,11},{10,... | collective-permute-start | bytes 221192 | tf_op jit(solution)/shard_map/ppermute | solution.py:48
  43.9 4.5 %collective-permute-start.18 = (bf16[2,32,576]{2,1,0:T(8,128)(2,1)S(1)}, bf16[2,32,576]{2,1,0:T(8,128)(2,1)S(1)}, u32[]{:S(2)}, u32[]{:S(2)}) collective-permute-start(bf16[2,32,576]{2,1,0:T(8,128)(2,1)S(1)} %slice_bitcast_fusion.1), channel_id=1, source_target_pairs={{0,16},{1,17},{2,18},{3,19},{4,20},{5,21},{6,22},{7,23},{8,24},{9,... | collective-permute-start | bytes 221192 | tf_op jit(solution)/shard_map/ppermute | solution.py:48
  45.3 4.5 %collective-permute-start.20 = (bf16[2,32,576]{2,1,0:T(8,128)(2,1)S(1)}, bf16[2,32,576]{2,1,0:T(8,128)(2,1)S(1)}, u32[]{:S(2)}, u32[]{:S(2)}) collective-permute-start(bf16[2,32,576]{2,1,0:T(8,128)(2,1)S(1)} %slice_bitcast_fusion), channel_id=1, source_target_pairs={{0,2},{1,3},{2,0},{3,1},{4,6},{5,7},{6,4},{7,5},{8,10},{9,11},{10,... | collective-permute-start | bytes 221192 | tf_op jit(solution)/shard_map/ppermute | solution.py:48
  48.1 12.5 %copy-start.3 = (f32[256,16]{0,1:T(8,128)S(1)}, f32[256,16]{0,1:T(8,128)}, u32[]{:S(2)}) copy-start(f32[256,16]{0,1:T(8,128)} %param.28) | copy-start | bytes 49156
  48.1 12.5 %copy-start.6 = (f32[256]{0:T(256)S(1)}, f32[256]{0:T(256)}, u32[]{:S(2)}) copy-start(f32[256]{0:T(256)} %param.27) | copy-start | bytes 3076
  48.1 12.5 %copy-start.7 = (f32[16]{0:T(128)S(1)}, f32[16]{0:T(128)}, u32[]{:S(2)}) copy-start(f32[16]{0:T(128)} %param.29) | copy-start | bytes 196
